TPU v7x, 512 devices: a whole 4x8x8 slice. The times are simulated.
512 devices in a mesh: stream: 64 (over y, z_hi, core), span: 8 (over x, z_lo).
Axes of the slice: x: 4, y: 8, z: 8 (z_hi: 4, z_lo: 2; z = z_hi * 2 + z_lo), core: 2. Of those that a mesh axis runs over, the one named last changes fastest.
Arguments:
- rhs_field: float32 [64, 8, 8, 2, 320], P('stream', 'span'), may hold values from -6 to 6
- guess: float32 [64, 8, 8, 2, 320], P('stream', 'span'), may hold values from -6 to 6
- inverse_diag: float32 [64, 8, 2, 320, 320], P('stream', 'span'), may hold values from -0.3125 to 0.3125
- lower_block: float32 [64, 8, 2, 80, 80], P('stream', 'span'), may hold values from -1.25 to 1.25
- upper_block: float32 [64, 8, 2, 80, 80], P('stream', 'span'), may hold values from -1.25 to 1.25
- west_block: float32 [64, 8, 2, 80, 80], P('stream', 'span'), may hold values from -0.625 to 0.625
- east_block: float32 [64, 8, 2, 80, 80], P('stream', 'span'), may hold values from -0.625 to 0.625
- inflow_map: int32 [64, 8, 2], P('stream', 'span'), may hold values from 0 to 1, each once within a row
Outputs:
- updated: float32 [64, 8, 8, 2, 320], P('stream', 'span')
Inputs may be any that keep to these rules, and one draw needn't show every extreme that they name: `inflow_map`: each row of a layer names each of the 2 elements of the layer upstream once.
All inputs are finite; a program needn't handle non-finite values.
Results may differ from a plain program's by a relative error of at most 0.0003.
Values sent between devices are 32-bit elements; how exact they have to be, the bound alone decides.
No kernel may reach another device: no remote copies, remote signals or barrier semaphores. Data moves between devices by JAX's collectives and lax.ppermute only.
A program may use at most 64 MiB of HBM per device.

v0:
```python
import jax
import jax.numpy as jnp
from jax import lax
from jax.sharding import PartitionSpec as P

NVAR = 5
NB = 4
FACE = 80


PRECISE = lax.Precision.HIGHEST


def with_halo(cells, sides, width):
    for axis, dim in sides:
        count = lax.axis_size(axis)
        head = lax.slice_in_dim(cells, 0, width, axis=dim)
        tail = lax.slice_in_dim(cells, cells.shape[dim] - width, cells.shape[dim], axis=dim)
        cells = jnp.concatenate(
            [
                lax.ppermute(tail, axis, [(i, (i + 1) % count) for i in range(count)]),
                cells,
                lax.ppermute(head, axis, [((i + 1) % count, i) for i in range(count)]),
            ],
            axis=dim,
        )
    return cells


def shifted(block, axis, distance):
    devices = range(lax.axis_size(axis))
    route = [(i - distance, i) for i in devices if i - distance in devices]
    return lax.ppermute(block, axis, route)


def prefix(part, axis, combine, identity, reverse):
    count = lax.axis_size(axis)
    place = lax.axis_index(axis)
    ahead = count - 1 - place if reverse else place
    gathered = jax.tree.map(lambda a: lax.all_gather(a, axis), part)
    state = jax.tree.map(lambda a, e: jnp.zeros_like(a) + jnp.asarray(e, a.dtype), part, identity)

    def one(hop, state):
        source = count - 1 - hop if reverse else hop
        return combine(
            state, jax.tree.map(lambda a: lax.dynamic_index_in_dim(a, source, 0, False), gathered)
        )

    return lax.fori_loop(0, ahead, one, state)


def stream_face(values_in, j):
    shape_lead = values_in.shape[:-1]
    nodal = values_in.reshape(shape_lead + (NVAR, NB, NB * NB))
    return nodal[..., :, j, :].reshape(shape_lead + (FACE,))


def span_face(values_in, j):
    shape_lead = values_in.shape[:-1]
    nodal = values_in.reshape(shape_lead + (NVAR, NB, NB, NB))
    return nodal[..., :, :, j, :].reshape(shape_lead + (FACE,))


def add_stream(values_in, added, j):
    shape_lead = values_in.shape[:-1]
    nodal = values_in.reshape(shape_lead + (NVAR, NB, NB * NB))
    nodal = nodal.at[..., :, j, :].add(added.reshape(shape_lead + (NVAR, NB * NB)))
    return nodal.reshape(values_in.shape)


def add_span(values_in, added, j):
    shape_lead = values_in.shape[:-1]
    nodal = values_in.reshape(shape_lead + (NVAR, NB, NB, NB))
    nodal = nodal.at[..., :, :, j, :].add(added.reshape(shape_lead + (NVAR, NB, NB)))
    return nodal.reshape(values_in.shape)


def stream_cols(matrices, j):
    shape_lead = matrices.shape[:-1]
    nodal = matrices.reshape(shape_lead + (NVAR, NB, NB * NB))
    return nodal[..., :, j, :].reshape(shape_lead + (FACE,))


def stream_rows(matrices, j):
    shape_lead = matrices.shape[:-2]
    columns = matrices.shape[-1]
    nodal = matrices.reshape(shape_lead + (NVAR, NB, NB * NB, columns))
    return nodal[..., :, j, :, :].reshape(shape_lead + (FACE, columns))


def blocks_times(blocks, vectors):
    return jnp.einsum("...ngf,...rnf->...rng", blocks, vectors, precision=PRECISE)


def pull_rows(onehot, vectors):
    return jnp.einsum("...mp,...rpf->...rmf", onehot, vectors, precision=PRECISE)


def push_rows(onehot, vectors):
    return jnp.einsum("...mn,...rmf->...rnf", onehot, vectors, precision=PRECISE)


def compose(earlier, latter):
    return (
        jnp.dot(earlier[0], latter[0], precision=PRECISE),
        jnp.dot(earlier[1], latter[0], precision=PRECISE) + latter[1],
    )


def per_device(
    rhs_field, guess, inverse_diag, lower_block, upper_block, west_block, east_block, inflow_map
):
    right_side = rhs_field[:, 0]
    lagged_field = guess[:, 0]
    inverse_blocks = inverse_diag[:, 0]
    lower_faces = lower_block[:, 0]
    upper_faces = upper_block[:, 0]
    layer_count = right_side.shape[0]
    count_rhs = right_side.shape[1]
    count_elems = right_side.shape[2]
    state_width = count_elems * FACE
    onehot = (inflow_map[:, 0, :, None] == jnp.arange(count_elems, dtype=jnp.int32)).astype(
        jnp.float32
    )
    padded = with_halo(guess, (("span", 1),), 1)
    from_west = span_face(padded[:, 0], NB - 1)
    from_east = span_face(padded[:, 2], 0)
    west_term = blocks_times(west_block[:, 0], from_west)
    east_term = blocks_times(east_block[:, 0], from_east)
    lagged_all = push_rows(onehot, blocks_times(upper_faces, stream_face(lagged_field, 0)))
    from_down = shifted(lagged_all[0], "stream", -1)
    lagged = jnp.concatenate([lagged_all[1:], from_down[None]], axis=0)
    source = add_span(add_span(right_side, -west_term, 0), -east_term, NB - 1)
    source = add_stream(source, -lagged, NB - 1)
    identity_map = jnp.eye(state_width, dtype=jnp.float32)
    zero_shift = jnp.zeros((count_rhs, state_width), jnp.float32)
    inner_fwd = stream_rows(stream_cols(inverse_blocks, 0), NB - 1)
    fwd_product = jnp.einsum("kneg,kngf->knef", inner_fwd, lower_faces, precision=PRECISE)
    fwd_layers = -jnp.einsum("kmp,kmef->kpfme", onehot, fwd_product, precision=PRECISE).reshape(
        layer_count, state_width, state_width
    )
    source_trace = jnp.einsum(
        "knfd,krnd->krnf", stream_rows(inverse_blocks, NB - 1), source, precision=PRECISE
    )
    source_trace = source_trace.reshape(layer_count, count_rhs, state_width)
    forward_map = identity_map
    forward_shift = zero_shift
    layer_at = 0
    forward_map = jnp.dot(forward_map, fwd_layers[layer_at], precision=PRECISE)
    forward_shift = (
        jnp.dot(forward_shift, fwd_layers[layer_at], precision=PRECISE) + source_trace[layer_at]
    )
    _, incoming = prefix(
        (forward_map, forward_shift), "stream", compose, (identity_map, zero_shift), False
    )
    outflow = incoming.reshape(count_rhs, count_elems, FACE)
    layer_at = 0
    inflow = blocks_times(lower_faces[layer_at], pull_rows(onehot[layer_at], outflow))
    solved = jnp.einsum(
        "ned,rnd->rne",
        inverse_blocks[layer_at],
        add_stream(source[layer_at], -inflow, 0),
        precision=PRECISE,
    )
    sweep_one = [solved]
    inner_back = stream_rows(stream_cols(inverse_blocks, NB - 1), 0)
    back_product = jnp.einsum("kmge,kmef->kmgf", upper_faces, inner_back, precision=PRECISE)
    back_layers = -jnp.einsum("kmp,kmgf->kmfpg", onehot, back_product, precision=PRECISE).reshape(
        layer_count, state_width, state_width
    )
    backward_map = identity_map
    backward_shift = zero_shift
    for layer_at in reversed(range(layer_count)):
        inflow_trace = stream_face(sweep_one[layer_at], 0) + jnp.einsum(
            "nef,rnf->rne", inner_back[layer_at], lagged[layer_at], precision=PRECISE
        )
        constant = push_rows(
            onehot[layer_at], blocks_times(upper_faces[layer_at], inflow_trace)
        ).reshape(count_rhs, state_width)
        backward_map = jnp.dot(backward_map, back_layers[layer_at], precision=PRECISE)
        backward_shift = (
            jnp.dot(backward_shift, back_layers[layer_at], precision=PRECISE) + constant
        )
    _, arriving = prefix(
        (backward_map, backward_shift), "stream", compose, (identity_map, zero_shift), True
    )
    coupled = arriving.reshape(count_rhs, count_elems, FACE)
    out_cols = stream_cols(inverse_blocks, NB - 1)
    results = [None] * layer_count
    for layer_at in reversed(range(layer_count)):
        solved = sweep_one[layer_at] + jnp.einsum(
            "nef,rnf->rne", out_cols[layer_at], lagged[layer_at] - coupled, precision=PRECISE
        )
        results[layer_at] = solved
        coupled = push_rows(
            onehot[layer_at], blocks_times(upper_faces[layer_at], stream_face(solved, 0))
        )
    return jnp.stack(results)[:, None]


def solution(mesh):
    in_specs = (
        P("stream", "span", None, None, None),
        P("stream", "span", None, None, None),
        P("stream", "span", None, None, None),
        P("stream", "span", None, None, None),
        P("stream", "span", None, None, None),
        P("stream", "span", None, None, None),
        P("stream", "span", None, None, None),
        P("stream", "span", None),
    )
    out_specs = P("stream", "span", None, None, None)
    return jax.shard_map(
        per_device, mesh=mesh, in_specs=in_specs, out_specs=out_specs, check_vma=False
    )
```

profile of v0, /device:TPU:1, one launch (start us, length us, event | category | flops | bytes accessed | tf_op | source)
XLA Modules:
  0.0 374.9 jit_solution(16859587687788026413)
XLA Ops:
  6.6 1.6 copy.100
  11.1 1.7 reshape_reshape_squeeze.6
  13.8 1.2 fusion.20
  17.8 4.8 %collective-permute-start = (f32[1,1,8,2,320]{2,4,3,1,0:T(8,128)S(1)}, f32[1,1,8,2,320]{2,4,3,1,0:T(8,128)S(1)}, u32[]{:S(2)}, u32[]{:S(2)}) collective-permute-start(f32[1,1,8,2,320]{2,4,3,1,0:T(8,128)S(1)} %copy.85), channel_id=1, source_target_pairs={{0,1},{1,2},{2,3},{3,4},{4,5},{5,6},{6,7},{7,0},{8,9},{9,10},{10,1... | collective-permute-start | bytes 61448 | tf_op jit(solution)/shard_map/ppermute | solution.py:21
  23.5 5.9 %collective-permute-start.2 = (f32[8,2,80]{2,0,1:T(8,128)S(1)}, f32[8,2,80]{2,0,1:T(8,128)S(1)}, u32[]{:S(2)}, u32[]{:S(2)}) collective-permute-start(f32[8,2,80]{2,0,1:T(8,128)S(1)} %bitcast.217), channel_id=1, source_target_pairs={{8,0},{16,8},{24,16},{32,24},{40,32},{48,40},{56,48},{64,56},{72,6... | collective-permute-start | bytes 15368 | tf_op jit(solution)/shard_map/ppermute | solution.py:33
  29.4 5.8 %collective-permute-start.1 = (f32[1,1,8,2,320]{2,4,3,1,0:T(8,128)S(1)}, f32[1,1,8,2,320]{2,4,3,1,0:T(8,128)S(1)}, u32[]{:S(2)}, u32[]{:S(2)}) collective-permute-start(f32[1,1,8,2,320]{2,4,3,1,0:T(8,128)S(1)} %copy.85), channel_id=1, source_target_pairs={{1,0},{2,1},{3,2},{4,3},{5,4},{6,5},{7,6},{0,7},{9,8},{10,9},{11,1... | collective-permute-start | bytes 61448 | tf_op jit(solution)/shard_map/ppermute | solution.py:23
  36.2 1.2 fusion.13
  37.5 6.8 %collective-permute-done.1 = f32[1,1,8,2,320]{2,4,3,1,0:T(8,128)S(1)} collective-permute-done((f32[1,1,8,2,320]{2,4,3,1,0:T(8,128)S(1)}, f32[1,1,8,2,320]{2,4,3,1,0:T(8,128)S(1)}, u32[]{:S(2)}, u32[]{:S(2)}) %collective-permute-start.1) | collective-permute-done | bytes 20512 | tf_op jit(solution)/shard_map/ppermute | solution.py:23
  44.3 1.2 fusion.12
  46.7 90.9 %all-gather.1 = f32[512,160]{1,0:T(8,128)S(1)} all-gather(f32[8,160]{1,0:T(8,128)S(1)} %convolution_add_fusion.1), channel_id=3, replica_groups=mesh['stream'=64,'span'=8] {'stream'}, dimensions={0}, use_global_device_ids=true | all-gather | bytes 332800 | tf_op jit(solution)/shard_map/all_gather | solution.py:40
  143.7 154.0 %all-gather.3 = f32[512,160]{1,0:T(8,128)S(1)} all-gather(f32[8,160]{1,0:T(8,128)S(1)} %convolution_add_fusion), channel_id=5, replica_groups=mesh['stream'=64,'span'=8] {'stream'}, dimensions={0}, use_global_device_ids=true | all-gather | bytes 332800 | tf_op jit(solution)/shard_map/all_gather | solution.py:40
  297.8 69.3 %while.31 = (s32[]{:T(128)}, f32[8,160]{1,0:T(8,128)S(1)}, s32[]{:T(128)}, f32[64,160,160]{2,1,0:T(8,128)}, f32[64,8,160]{2,1,0:T(8,128)S(1)}, /*index=5*/s32[]{:T(128)}, s32[]{:T(128)}, s32[]{:T(128)}, s32[]{:T(128)}) while((s32[]{:T(128)}, f32[8,160]{1,0:T(8,128)S(1)}, s32[]{:T(128)}, f32[64,160,160]{2,1,0:T(8,128)}, ...), condition=%wide.region_3.4_spmd, body=%wide.region_2.0_spmd.sunk | while | flops 2458886 | bytes 190603 | solution.py:49
  298.9 1.1 fusion.78
  300.0 1.1 fusion.78
  301.1 1.1 fusion.78
  302.2 1.1 fusion.78
  303.3 1.1 fusion.78
  304.5 1.1 fusion.78
  305.6 1.1 fusion.78
  306.7 1.1 fusion.78
  307.8 1.1 fusion.78
  308.9 1.1 fusion.78
  310.1 1.1 fusion.78
  311.2 1.1 fusion.78
  312.3 1.1 fusion.78
  313.4 1.1 fusion.78
  315.6 1.1 fusion.78
  316.8 1.1 fusion.78
  317.9 1.1 fusion.78
  320.1 1.1 fusion.78
  321.2 1.1 fusion.78
  322.4 1.1 fusion.78
  (189 shorter events, 64.5 us)
Async XLA Ops:
  6.5 7.0 %copy-start = (f32[1,1,2,80,80]{4,3,2,1,0:T(8,128)S(1)}, f32[1,1,2,80,80]{4,3,2,1,0:T(8,128)}, u32[]{:S(2)}) copy-start(f32[1,1,2,80,80]{4,3,2,1,0:T(8,128)} %param.24) | copy-start | bytes 153604
  6.5 29.5 %copy-start.1 = (f32[1,1,2,320,320]{4,3,2,1,0:T(8,128)S(1)}, f32[1,1,2,320,320]{4,3,2,1,0:T(8,128)}, u32[]{:S(2)}) copy-start(f32[1,1,2,320,320]{4,3,2,1,0:T(8,128)} %param.22) | copy-start | bytes 2457604
  6.5 16.6 %copy-start.5 = (s32[1,1,2]{2,1,0:T(1,128)S(1)}, s32[1,1,2]{2,1,0:T(1,128)}, u32[]{:S(2)}) copy-start(s32[1,1,2]{2,1,0:T(1,128)} %param.27) | copy-start | bytes 28
  6.5 11.0 %copy-start.4 = (f32[1,1,8,2,320]{4,3,2,1,0:T(2,128)S(1)}, f32[1,1,8,2,320]{4,3,2,1,0:T(2,128)}, u32[]{:S(2)}) copy-start(f32[1,1,8,2,320]{4,3,2,1,0:T(2,128)} %param.21) | copy-start | bytes 61444
  6.5 132.2 %all-gather.7.cloned.1.call-start = ((), (), s32[]{:S(2)}) async-start(), calls=%async_computation | async-start | bytes 10649600 | tf_op jit(solution)/shard_map/all_gather | solution.py:40
  10.3 6.2 %copy-start.2 = (f32[1,2,5,1,16,80]{5,4,2,1,3,0:T(8,128)}, f32[1,2,5,1,16,80]{5,4,2,1,3,0:T(8,128)S(1)}, u32[]{:S(2)}) copy-start(f32[1,2,5,1,16,80]{5,4,2,1,3,0:T(8,128)S(1)} %copy.112) | copy-start | bytes 153604
  13.2 126.9 %copy-start.3 = (f32[1,1,2,80,80]{4,3,2,1,0:T(8,128)S(1)}, f32[1,1,2,80,80]{4,3,2,1,0:T(8,128)}, u32[]{:S(2)}) copy-start(f32[1,1,2,80,80]{4,3,2,1,0:T(8,128)} %param.23) | copy-start | bytes 153604
  16.5 281.3 %all-gather.9.cloned.1.call-start = ((), (), s32[]{:S(2)}) async-start(), calls=%async_computation.1 | async-start | bytes 10649600 | tf_op jit(solution)/shard_map/all_gather | solution.py:40
  17.8 18.4 %collective-permute-start = (f32[1,1,8,2,320]{2,4,3,1,0:T(8,128)S(1)}, f32[1,1,8,2,320]{2,4,3,1,0:T(8,128)S(1)}, u32[]{:S(2)}, u32[]{:S(2)}) collective-permute-start(f32[1,1,8,2,320]{2,4,3,1,0:T(8,128)S(1)} %copy.85), channel_id=1, source_target_pairs={{0,1},{1,2},{2,3},{3,4},{4,5},{5,6},{6,7},{7,0},{8,9},{9,10},{10,1... | collective-permute-start | bytes 61448 | tf_op jit(solution)/shard_map/ppermute | solution.py:21
  23.5 12.6 %collective-permute-start.2 = (f32[8,2,80]{2,0,1:T(8,128)S(1)}, f32[8,2,80]{2,0,1:T(8,128)S(1)}, u32[]{:S(2)}, u32[]{:S(2)}) collective-permute-start(f32[8,2,80]{2,0,1:T(8,128)S(1)} %bitcast.217), channel_id=1, source_target_pairs={{8,0},{16,8},{24,16},{32,24},{40,32},{48,40},{56,48},{64,56},{72,6... | collective-permute-start | bytes 15368 | tf_op jit(solution)/shard_map/ppermute | solution.py:33
  29.4 14.9 %collective-permute-start.1 = (f32[1,1,8,2,320]{2,4,3,1,0:T(8,128)S(1)}, f32[1,1,8,2,320]{2,4,3,1,0:T(8,128)S(1)}, u32[]{:S(2)}, u32[]{:S(2)}) collective-permute-start(f32[1,1,8,2,320]{2,4,3,1,0:T(8,128)S(1)} %copy.85), channel_id=1, source_target_pairs={{1,0},{2,1},{3,2},{4,3},{5,4},{6,5},{7,6},{0,7},{9,8},{10,9},{11,1... | collective-permute-start | bytes 61448 | tf_op jit(solution)/shard_map/ppermute | solution.py:23
Sparse Core Ops, SparseCore 0:
  16.6 122.0 all-gather.6
  142.0 111.8 all-gather.8
where the time goes:
time: 377 us; the launch traced here: 375 us
  blocking collectives  245 us (65%)
  matrix products  79.5 us (21%)
  starting transfers between devices  16.5 us (4%)
  between operations  13.7 us (4%)
  local copies, waits for them, and re-layouts  10.7 us (3%)
  waiting for transfers between devices  7.94 us (2%)
    all_gather x2, blocking collectives, prefix(): gathered = jax.tree.map(lambda a: lax.all_gather(a, axis), part)  245 us
    dot_general x63, matrix products, compose(): jnp.dot(earlier[1], latter[0], precision=PRECISE) + latter[1]  69.5 us
  transfers between devices with their start and end apart: 5, of which 2 were waited for; matrix products, arithmetic and copies ran while one was open for 3% of the time, Pallas kernels for 0%

commit v1 on v0

v1 whole, which is shorter than its diff:
```python
import functools

import jax
import jax.numpy as jnp
import numpy as np
from jax import lax
from jax.experimental import pallas as pl
from jax.experimental.pallas import tpu as pltpu
from jax.sharding import PartitionSpec as P

NVAR = 5
NB = 4
FACE = 80
DOF = 320
LANES = 128
VEC = FACE
REST = FACE + 8
HALF = LANES - REST
BF16 = jnp.bfloat16
F32 = jnp.float32
NN = (((1,), (0,)), ((), ()))
NT = (((1,), (1,)), ((), ()))


def split(x):
    hi = x.astype(BF16)
    return hi, (x - hi.astype(F32)).astype(BF16)


def dot(a, b, dims=NN):
    ah, al = split(a)
    bh, bl = split(b)
    one = functools.partial(lax.dot_general, dimension_numbers=dims, preferred_element_type=F32)
    return one(ah, bh) + (one(ah, bl) + one(al, bh))


def pick(x, onehot, dims=NN):
    hi = x.astype(BF16)
    rest = x - hi.astype(F32)
    mid = rest.astype(BF16)
    low = (rest - mid.astype(F32)).astype(BF16)
    one = functools.partial(lax.dot_general, dimension_numbers=dims, preferred_element_type=F32)
    return one(hi, onehot) + one(mid, onehot) + one(low, onehot)


def pick2(x, onehot, dims=NN):
    hi, low = split(x)
    one = functools.partial(lax.dot_general, dimension_numbers=dims, preferred_element_type=F32)
    return one(hi, onehot) + one(low, onehot)


def stream_pick(j):
    s = np.zeros((NVAR, NB, NB * NB, FACE), np.float32)
    for v in range(NVAR):
        for q in range(NB * NB):
            s[v, j, q, v * NB * NB + q] = 1
    return s.reshape(DOF, FACE)


def span_pick(j):
    s = np.zeros((NVAR, NB, NB, NB, FACE), np.float32)
    for v in range(NVAR):
        for a in range(NB):
            for c in range(NB):
                s[v, a, j, c, (v * NB + a) * NB + c] = 1
    return s.reshape(DOF, FACE)


def stream_rows(x, j):
    step = NB * NB
    return jnp.concatenate(
        [x[(v * NB + j) * step : (v * NB + j + 1) * step] for v in range(NVAR)], axis=0
    )


def place_rows(x, j):
    step = NB * NB
    zeros = jnp.zeros((step, x.shape[1]), x.dtype)
    parts = []
    for v in range(NVAR):
        for a in range(NB):
            parts.append(x[v * step : (v + 1) * step] if a == j else zeros)
    return jnp.concatenate(parts, axis=0)


def widen(x):
    return jnp.concatenate([x, jnp.zeros((x.shape[0], LANES - x.shape[1]), x.dtype)], axis=1)


def lane_of(shape):
    return lax.broadcasted_iota(jnp.int32, shape, 1)


def pack(ab, be, d):
    lane = lane_of(ab.shape)
    left = jnp.where(lane < REST, ab, pltpu.roll(d, REST, 1))
    right = jnp.where(lane < REST, be, pltpu.roll(d, REST - HALF, 1))
    return left, right


def unpack_d(left, right):
    lane = lane_of(left.shape)
    return jnp.where(
        lane < HALF, pltpu.roll(left, LANES - REST, 1), pltpu.roll(right, LANES - REST + HALF, 1)
    )


def tall(x):
    return jnp.concatenate([x, jnp.zeros((LANES - FACE, x.shape[1]), x.dtype)], axis=0)


def compose(first, second):
    left1, right1 = first
    left2, right2 = second
    d1, d2 = unpack_d(left1, right1), unpack_d(left2, right2)
    lane = lane_of(left1.shape)
    vec = (lane >= VEC) & (lane < REST)
    through = dot(jnp.concatenate([left2, d2], axis=0), tall(left1))
    ab = through[:FACE] + jnp.where(vec, left2, 0.0)
    back = through[FACE:] + jnp.where(vec, right2, 0.0)
    both = dot(right1, tall(jnp.concatenate([right2, back], axis=1)))
    be = jnp.where(lane < VEC, both[:, :LANES], right1 + both[:, LANES:])
    return pack(ab, be, d1 + both[:, LANES:])


def blocks_kernel(inv, low, up, guess, swap, pin, pout, zin, zout, maps, lag):
    pick_in, pick_out = pin[...], pout[...]
    made = []
    for n in range(2):
        m = inv[n]
        u = up[n]
        z_in = dot(m, place_rows(low[n], 0))
        z_out = pick(m, pick_out)
        zin[n] = z_in
        zout[n] = z_out
        face = pick(guess[:, n, :], pick_in)
        down = dot(u, stream_rows(z_in, 0))
        back = dot(u, stream_rows(z_out, 0))
        made.append((-stream_rows(z_in, 3), -back, -down, dot(face, u, NT)))
    swapped = swap[...] > 0.5
    for p in range(2):
        for i in range(3):
            maps[p, i] = jnp.where(swapped, made[1 - p][i], made[p][i])
        lag[p] = jnp.where(swapped[:8], made[1 - p][3], made[p][3])


def vectors_kernel(
    inv, up, rhs, west_blk, east_blk, from_west, from_east, lag, zout, maps, swap,
    pick_w, pick_e, pin, pout, solved, out,
):
    swapped = swap[...] > 0.5
    made = []
    for n in range(2):
        m = inv[n]
        west = dot(pick(from_west[:, n, :], pick_e[...]), west_blk[n], NT)
        east = dot(pick(from_east[:, n, :], pick_w[...]), east_blk[n], NT)
        h = rhs[:, n, :] - pick(west, pick_w[...], NT) - pick(east, pick_e[...], NT)
        y = dot(h, m, NT)
        solved[n] = y
        y_in = pick(y, pin[...])
        y_out = pick(y, pout[...]) - dot(lag[n], stream_rows(zout[n], 3), NT)
        rows = jnp.zeros((VEC, FACE), F32)
        tail = jnp.zeros((LANES - REST, FACE), F32)
        b = jnp.concatenate([rows, y_out, tail], axis=0).T
        e = dot(up[n], jnp.concatenate([rows, y_in, tail], axis=0), NT)
        made.append((b, e))
    for p in range(2):
        b = jnp.where(swapped, made[1 - p][0], made[p][0])
        e = jnp.where(swapped, made[1 - p][1], made[p][1])
        left, right = pack(widen(maps[p, 0]) + b, widen(maps[p, 1]) + e, widen(maps[p, 2]))
        out[(2 * p) * FACE : (2 * p + 1) * FACE] = left
        out[(2 * p + 1) * FACE : (2 * p + 2) * FACE] = right
    out[4 * FACE :] = jnp.broadcast_to(swap[...][:1], (8, LANES))


def tiles(ref, p):
    return (
        ref[2 * p * FACE : (2 * p + 1) * FACE],
        ref[(2 * p + 1) * FACE : (2 * p + 2) * FACE],
    )


def pair_kernel(level, last, above, own, got, out):
    def put(first, second):
        s1 = first[4 * FACE : 4 * FACE + 1, :]
        s2 = second[4 * FACE : 4 * FACE + 1, :]
        w1 = s1 > 0.5
        near = [tiles(first, p) for p in range(2)]
        far = [tiles(second, p) for p in range(2)]
        both = jnp.abs(s1 - s2)
        for p in range(2):
            left2 = jnp.where(w1, far[1 - p][0], far[p][0])
            right2 = jnp.where(w1, far[1 - p][1], far[p][1])
            left, right = compose(near[p], (left2, right2))
            if last:
                lane = lane_of(left.shape)
                d = unpack_d(left, right)
                tile = jnp.where(lane < VEC, d, left)
                tile = jnp.where(lane < REST, tile, pltpu.roll(right, 8, 1))
                out[p * FACE : (p + 1) * FACE] = jnp.where(
                    lane < REST + 8, tile, jnp.broadcast_to(both, tile.shape)
                )
            else:
                out[2 * p * FACE : (2 * p + 1) * FACE] = left
                out[(2 * p + 1) * FACE : (2 * p + 2) * FACE] = right
        if not last:
            out[4 * FACE :] = jnp.broadcast_to(both, (8, LANES))

    @pl.when(above[level] == 1)
    def _():
        put(got, own)

    @pl.when(above[level] == 0)
    def _():
        put(own, got)


def down_kernel(levels, above, own_top, got_top, *rest):
    owns, gots = rest[:levels], rest[levels : 2 * levels]
    zin, zout, solved, swap, out, t_ref, c_ref = rest[2 * levels :]
    lane = lane_of((FACE, LANES))
    vec = (lane >= VEC) & (lane < REST)

    def only(x):
        return jnp.where(vec, x, 0.0)

    def top(ref, p):
        return ref[p * FACE : (p + 1) * FACE]

    def choose(flag, pair, p):
        return jnp.where(flag, pair[1 - p], pair[p])

    @pl.when(above[levels] == 1)
    def _():
        w = jnp.broadcast_to(got_top[0:1, LANES - 1 :], (1, LANES)) > 0.5
        for p in range(2):
            t_ref[p] = only(choose(w, [top(got_top, 0), top(got_top, 1)], p))
            c_ref[p] = jnp.zeros((FACE, LANES), F32)

    @pl.when(above[levels] == 0)
    def _():
        w = jnp.broadcast_to(own_top[0:1, LANES - 1 :], (1, LANES)) > 0.5
        for p in range(2):
            t_ref[p] = jnp.zeros((FACE, LANES), F32)
            far = choose(w, [top(got_top, 0), top(got_top, 1)], p)
            b = only(top(own_top, p))
            c_ref[p] = only(dot(far, tall(b)) + pltpu.roll(far, LANES - 8, 1))

    for level in reversed(range(levels)):
        own, got = owns[level], gots[level]

        @pl.when(above[level] == 1)
        def _():
            w = got[4 * FACE : 4 * FACE + 1, :] > 0.5
            t = []
            c = [c_ref[0], c_ref[1]]
            for p in range(2):
                left, _ = tiles(got, p)
                t.append(only(dot(left, tall(t_ref[p])) + left))
            for p in range(2):
                t_ref[p] = choose(w, t, p)
                c_ref[p] = choose(w, c, p)

        @pl.when(above[level] == 0)
        def _():
            w = own[4 * FACE : 4 * FACE + 1, :] > 0.5
            far = [tiles(got, p) for p in range(2)]
            for p in range(2):
                left, _ = tiles(own, p)
                mid = only(dot(left, tall(t_ref[p])) + left)
                left2 = choose(w, [far[0][0], far[1][0]], p)
                right2 = choose(w, [far[0][1], far[1][1]], p)
                c_ref[p] = only(
                    dot(unpack_d(left2, right2), tall(mid))
                    + dot(right2, tall(c_ref[p]))
                    + right2
                )

    swapped = swap[...] > 0.5
    for n in range(2):
        t = choose(swapped, [t_ref[0], t_ref[1]], n)
        c = choose(swapped, [c_ref[0], c_ref[1]], n)
        t = t.T[VEC:REST]
        c = c.T[VEC:REST]
        out[:, n, :] = solved[n] - dot(t, zin[n], NT) - dot(c, zout[n], NT)


def call(kernel, out_shape, flops=0, scratch=(), smem=False, operands=()):
    specs = [pl.BlockSpec(memory_space=pltpu.VMEM) for _ in operands]
    if smem:
        specs[0] = pl.BlockSpec(memory_space=pltpu.SMEM)
    return pl.pallas_call(
        kernel,
        out_shape=out_shape,
        in_specs=specs,
        scratch_shapes=list(scratch),
        compiler_params=pltpu.CompilerParams(vmem_limit_bytes=32 * 1024 * 1024),
    )(*operands)


def f32(*shape):
    return jax.ShapeDtypeStruct(shape, F32)


ACROSS = (1, 2, 6, 8, 16)
TOP = (6, 7, 4, 5, 2, 3, 0, 1)


def per_device(
    rhs_field, guess, inverse_diag, lower_block, upper_block, west_block, east_block, inflow_map
):
    rhs, own_guess = rhs_field[0, 0], guess[0, 0]
    inv, low, up = inverse_diag[0, 0], lower_block[0, 0], upper_block[0, 0]
    west_blk, east_blk = west_block[0, 0], east_block[0, 0]
    wide = lax.axis_size("span")
    layers = lax.axis_size("stream")
    ring = [(i, (i + 1) % wide) for i in range(wide)]
    from_west = lax.ppermute(own_guess, "span", ring)
    from_east = lax.ppermute(own_guess, "span", [(b, a) for a, b in ring])
    swap = jnp.broadcast_to(inflow_map[0, 0, 0].astype(F32), (FACE, LANES))
    place = lax.axis_index("stream")
    above = (place >> jnp.arange(6, dtype=jnp.int32)) & 1
    pin, pout = jnp.asarray(stream_pick(0), BF16), jnp.asarray(stream_pick(3), BF16)
    pick_w, pick_e = jnp.asarray(span_pick(0), BF16), jnp.asarray(span_pick(3), BF16)
    swap_map = swap[:, :FACE]
    zin, zout, maps, lag_out = call(
        blocks_kernel,
        (f32(2, DOF, FACE), f32(2, DOF, FACE), f32(2, 3, FACE, FACE), f32(2, 8, FACE)),
        operands=(inv, low, up, own_guess, swap_map, pin, pout),
    )
    lag = lax.ppermute(lag_out, "stream", [(i + 1, i) for i in range(layers - 1)])
    solved, own = call(
        vectors_kernel,
        (f32(2, 8, DOF), f32(4 * FACE + 8, LANES)),
        operands=(
            inv, up, rhs, west_blk, east_blk, from_west, from_east, lag, zout, maps, swap,
            pick_w, pick_e, pin, pout,
        ),
    )
    owns, gots = [], []
    for level, across in enumerate(ACROSS):
        got = lax.ppermute(own, "stream", [(i, i ^ across) for i in range(layers)])
        owns.append(own)
        gots.append(got)
        last = level == len(ACROSS) - 1
        own = call(
            functools.partial(pair_kernel, level, last),
            f32(2 * FACE, LANES) if last else f32(4 * FACE + 8, LANES),
            smem=True,
            operands=(above, own, got),
        )
    got = lax.ppermute(own, "stream", [(i, TOP[i // 8] * 8 + i % 8) for i in range(layers)])
    out = call(
        functools.partial(down_kernel, len(ACROSS)),
        f32(8, 2, DOF),
        smem=True,
        scratch=(pltpu.VMEM((2, FACE, LANES), F32), pltpu.VMEM((2, FACE, LANES), F32)),
        operands=(above, own, got, *owns, *gots, zin, zout, solved, swap),
    )
    return out[None, None]


def solution(mesh):
    in_specs = (
        P("stream", "span", None, None, None),
        P("stream", "span", None, None, None),
        P("stream", "span", None, None, None),
        P("stream", "span", None, None, None),
        P("stream", "span", None, None, None),
        P("stream", "span", None, None, None),
        P("stream", "span", None, None, None),
        P("stream", "span", None),
    )
    out_specs = P("stream", "span", None, None, None)
    return jax.shard_map(
        per_device, mesh=mesh, in_specs=in_specs, out_specs=out_specs, check_vma=False
    )
```

time: 377 us -> 97.8 us (0.26)
  the two profiles are of different devices: /device:TPU:1 before, /device:TPU:64 now
where the time goes in v1:
time: 97.8 us; the launch traced here: 97.2 us
  starting transfers between devices  42.9 us (44%)
  waiting for transfers between devices  33 us (34%)
  Pallas kernels  14.8 us (15%)
  local copies, waits for them, and re-layouts  6.18 us (6%)
    ppermute x5, starting transfers between devices, per_device(): got = lax.ppermute(own, 'stream', [(i, i ^ across) for i in range(layers)])  28.7 us
    ppermute x5, waiting for transfers between devices, per_device(): got = lax.ppermute(own, 'stream', [(i, i ^ across) for i in range(layers)])  26.6 us
    pallas_call x8, Pallas kernels, call(): pl.pallas_call(kernel, out_shape=out_shape, in_specs=specs, scratch_shape...  14.8 us
    ppermute x1, starting transfers between devices, per_device(): from_east = lax.ppermute(own_guess, 'span', [(b, a) for a, b in ring])  7.05 us
    unnamed x26, local copies, waits for them, and re-layouts  6.16 us
    ppermute x1, waiting for transfers between devices, per_device(): lax.ppermute(own, 'stream', [(i, TOP[i // 8] * 8 + i % 8) for i in range(...  4.61 us
    ppermute x1, starting transfers between devices, per_device(): lax.ppermute(own, 'stream', [(i, TOP[i // 8] * 8 + i % 8) for i in range(...  3.93 us
  transfers between devices with their start and end apart: 9, of which 7 were waited for; matrix products, arithmetic and copies ran while one was open for 0% of the time, Pallas kernels for 1%

profile of v1, /device:TPU:64, one launch (start us, length us, event | category | flops | bytes accessed | tf_op | source)
XLA Modules:
  0.0 97.2 jit_solution(10807176364991011894)
XLA Ops:
  0.0 7.1 %collective-permute-start.1 = (f32[8,2,320]{2,1,0:T(2,128)}, f32[8,2,320]{2,1,0:T(2,128)S(1)}, u32[]{:S(2)}, u32[]{:S(2)}) collective-permute-start(f32[8,2,320]{2,1,0:T(2,128)} %bitcast.18), channel_id=1, source_target_pairs={{1,0},{2,1},{3,2},{4,3},{5,4},{6,5},{7,6},{0,7},{9,8},{10,9},{11,1... | collective-permute-start | bytes 61448 | tf_op jit(solution)/shard_map/ppermute | solution.py:319
  7.1 1.9 %collective-permute-start = (f32[8,2,320]{2,1,0:T(2,128)}, f32[8,2,320]{2,1,0:T(2,128)S(1)}, u32[]{:S(2)}, u32[]{:S(2)}) collective-permute-start(f32[8,2,320]{2,1,0:T(2,128)} %bitcast.19), channel_id=1, source_target_pairs={{0,1},{1,2},{2,3},{3,4},{4,5},{5,6},{6,7},{7,0},{8,9},{9,10},{10,1... | collective-permute-start | bytes 61448 | tf_op jit(solution)/shard_map/ppermute | solution.py:318
  9.1 0.7 copy-done.11
  9.8 1.2 %copy-done = f32[1,1,2,320,320]{4,3,2,1,0:T(8,128)S(1)} copy-done((f32[1,1,2,320,320]{4,3,2,1,0:T(8,128)S(1)}, f32[1,1,2,320,320]{4,3,2,1,0:T(8,128)}, u32[]{:S(2)}) %copy-start) | copy-done | bytes 819224
  11.0 0.9 copy-done.1
  11.9 0.9 copy-done.3
  12.8 0.9 copy-done.4
  13.6 0.9 copy-done.9
  14.5 0.0 copy-start.8
  14.6 1.3 %shard_map.118 = (f32[2,320,80]{2,1,0:T(8,128)S(1)}, f32[2,320,80]{2,1,0:T(8,128)S(1)}, f32[2,3,80,80]{3,2,1,0:T(8,128)S(1)}, f32[2,8,80]{2,1,0:T(8,128)S(1)}) custom-call(f32[2,320,320]{2,1,0:T(8,128)S(1)} %bitcast.10, f32[2,80,80]{2,1,0:T(8,128)S(1)} %bitcast.16, f32[2,80,80]{2,1,0:T(8,128)S(1)} %bitcast.12, f32[8,2,320]{2,1,0:T(2,128)S(1)} %bitcast.20, ...), custom_call_target="tpu_custom_call" | custom-call | tf_op jit(solution)/shard_map/pallas_call | solution.py:292
  15.9 1.3 %collective-permute-start.2 = (f32[2,8,80]{2,1,0:T(8,128)S(1)}, f32[2,8,80]{2,1,0:T(8,128)S(1)}, u32[]{:S(2)}, u32[]{:S(2)}) collective-permute-start(f32[2,8,80]{2,1,0:T(8,128)S(1)} %get-tuple-element.11), channel_id=1, source_target_pairs={{8,0},{16,8},{24,16},{32,24},{40,32},{48,40},{56,48},{64,56},{72,6... | collective-permute-start | bytes 15368 | tf_op jit(solution)/shard_map/ppermute | solution.py:331
  17.2 1.8 %collective-permute-done.2.lag = f32[2,8,80]{2,1,0:T(8,128)S(1)} collective-permute-done((f32[2,8,80]{2,1,0:T(8,128)S(1)}, f32[2,8,80]{2,1,0:T(8,128)S(1)}, u32[]{:S(2)}, u32[]{:S(2)}) %collective-permute-start.2) | collective-permute-done | bytes 5152 | tf_op jit(solution)/shard_map/ppermute | solution.py:331
  19.0 0.7 copy-done.10
  19.7 2.7 %shard_map.119 = (f32[2,8,320]{2,1,0:T(8,128)S(1)}, f32[328,128]{1,0:T(8,128)S(1)}) custom-call(f32[2,320,320]{2,1,0:T(8,128)S(1)} %bitcast.11, f32[2,80,80]{2,1,0:T(8,128)S(1)} %bitcast.13, f32[8,2,320]{2,1,0:T(2,128)S(1)} %bitcast.17, f32[2,80,80]{2,1,0:T(8,128)S(1)} %bitcast.14, f32[2,80,80]{2,1,0:T(8,128)S(1)} %bitcast.15, ...), custom_call_target="tpu_custom_call" | custom-call | tf_op jit(solution)/shard_map/pallas_call | solution.py:292
  22.4 4.3 %collective-permute-start.3 = (f32[328,128]{1,0:T(8,128)S(1)}, f32[328,128]{1,0:T(8,128)S(1)}, u32[]{:S(2)}, u32[]{:S(2)}) collective-permute-start(f32[328,128]{1,0:T(8,128)S(1)} %get-tuple-element.14.own.rest_0_), channel_id=1, source_target_pairs={{0,8},{8,0},{16,24},{24,16},{32,40},{40,32},{48,56},{56,48},{64,72... | collective-permute-start | bytes 503816 | tf_op jit(solution)/shard_map/ppermute | solution.py:342
  26.7 1.0 %collective-permute-done.3.got.rest_5_ = f32[328,128]{1,0:T(8,128)S(1)} collective-permute-done((f32[328,128]{1,0:T(8,128)S(1)}, f32[328,128]{1,0:T(8,128)S(1)}, u32[]{:S(2)}, u32[]{:S(2)}) %collective-permute-start.3) | collective-permute-done | bytes 167968 | tf_op jit(solution)/shard_map/ppermute | solution.py:342
  27.7 1.1 %shard_map.120.own.rest_1_ = f32[328,128]{1,0:T(8,128)S(1)} custom-call(s32[6]{0:T(128)S(1)} %shift-right-arithmetic_and_fusion.above, f32[328,128]{1,0:T(8,128)S(1)} %get-tuple-element.14.own.rest_0_, f32[328,128]{1,0:T(8,128)S(1)} %collective-permute-done.3.got.rest_5_), custom_call_target="tpu_custom_call" | custom-call | tf_op jit(solution)/shard_map/pallas_call | solution.py:292
  28.9 6.4 %collective-permute-start.4 = (f32[328,128]{1,0:T(8,128)S(1)}, f32[328,128]{1,0:T(8,128)S(1)}, u32[]{:S(2)}, u32[]{:S(2)}) collective-permute-start(f32[328,128]{1,0:T(8,128)S(1)} %shard_map.120.own.rest_1_), channel_id=1, source_target_pairs={{0,16},{8,24},{16,0},{24,8},{32,48},{40,56},{48,32},{56,40},{64,80... | collective-permute-start | bytes 503816 | tf_op jit(solution)/shard_map/ppermute | solution.py:342
  35.3 7.6 %collective-permute-done.4.got.rest_6_ = f32[328,128]{1,0:T(8,128)S(1)} collective-permute-done((f32[328,128]{1,0:T(8,128)S(1)}, f32[328,128]{1,0:T(8,128)S(1)}, u32[]{:S(2)}, u32[]{:S(2)}) %collective-permute-start.4) | collective-permute-done | bytes 167968 | tf_op jit(solution)/shard_map/ppermute | solution.py:342
  42.9 1.1 %shard_map.121.own.rest_2_ = f32[328,128]{1,0:T(8,128)S(1)} custom-call(s32[6]{0:T(128)S(1)} %shift-right-arithmetic_and_fusion.above, f32[328,128]{1,0:T(8,128)S(1)} %shard_map.120.own.rest_1_, f32[328,128]{1,0:T(8,128)S(1)} %collective-permute-done.4.got.rest_6_), custom_call_target="tpu_custom_call" | custom-call | tf_op jit(solution)/shard_map/pallas_call | solution.py:292
  44.0 8.6 %collective-permute-start.5 = (f32[328,128]{1,0:T(8,128)S(1)}, f32[328,128]{1,0:T(8,128)S(1)}, u32[]{:S(2)}, u32[]{:S(2)}) collective-permute-start(f32[328,128]{1,0:T(8,128)S(1)} %shard_map.121.own.rest_2_), channel_id=1, source_target_pairs={{0,48},{8,56},{16,32},{24,40},{32,16},{40,24},{48,0},{56,8},{64,11... | collective-permute-start | bytes 503816 | tf_op jit(solution)/shard_map/ppermute | solution.py:342
  52.7 6.5 %collective-permute-done.5.got.rest_7_ = f32[328,128]{1,0:T(8,128)S(1)} collective-permute-done((f32[328,128]{1,0:T(8,128)S(1)}, f32[328,128]{1,0:T(8,128)S(1)}, u32[]{:S(2)}, u32[]{:S(2)}) %collective-permute-start.5) | collective-permute-done | bytes 167968 | tf_op jit(solution)/shard_map/ppermute | solution.py:342
  59.2 1.1 %shard_map.122.own.rest_3_ = f32[328,128]{1,0:T(8,128)S(1)} custom-call(s32[6]{0:T(128)S(1)} %shift-right-arithmetic_and_fusion.above, f32[328,128]{1,0:T(8,128)S(1)} %shard_map.121.own.rest_2_, f32[328,128]{1,0:T(8,128)S(1)} %collective-permute-done.5.got.rest_7_), custom_call_target="tpu_custom_call" | custom-call | tf_op jit(solution)/shard_map/pallas_call | solution.py:292
  60.3 4.6 %collective-permute-start.6 = (f32[328,128]{1,0:T(8,128)S(1)}, f32[328,128]{1,0:T(8,128)S(1)}, u32[]{:S(2)}, u32[]{:S(2)}) collective-permute-start(f32[328,128]{1,0:T(8,128)S(1)} %shard_map.122.own.rest_3_), channel_id=1, source_target_pairs={{0,64},{8,72},{16,80},{24,88},{32,96},{40,104},{48,112},{56,120},{... | collective-permute-start | bytes 503816 | tf_op jit(solution)/shard_map/ppermute | solution.py:342
  64.9 4.3 %collective-permute-done.6.got.rest_8_ = f32[328,128]{1,0:T(8,128)S(1)} collective-permute-done((f32[328,128]{1,0:T(8,128)S(1)}, f32[328,128]{1,0:T(8,128)S(1)}, u32[]{:S(2)}, u32[]{:S(2)}) %collective-permute-start.6) | collective-permute-done | bytes 167968 | tf_op jit(solution)/shard_map/ppermute | solution.py:342
  69.2 1.1 %shard_map.123.own.rest_4_ = f32[328,128]{1,0:T(8,128)S(1)} custom-call(s32[6]{0:T(128)S(1)} %shift-right-arithmetic_and_fusion.above, f32[328,128]{1,0:T(8,128)S(1)} %shard_map.122.own.rest_3_, f32[328,128]{1,0:T(8,128)S(1)} %collective-permute-done.6.got.rest_8_), custom_call_target="tpu_custom_call" | custom-call | tf_op jit(solution)/shard_map/pallas_call | solution.py:292
  70.3 4.8 %collective-permute-start.7 = (f32[328,128]{1,0:T(8,128)S(1)}, f32[328,128]{1,0:T(8,128)S(1)}, u32[]{:S(2)}, u32[]{:S(2)}) collective-permute-start(f32[328,128]{1,0:T(8,128)S(1)} %shard_map.123.own.rest_4_), channel_id=1, source_target_pairs={{0,128},{8,136},{16,144},{24,152},{32,160},{40,168},{48,176},{56,1... | collective-permute-start | bytes 503816 | tf_op jit(solution)/shard_map/ppermute | solution.py:342
  75.1 7.2 %collective-permute-done.7.got.rest_9_ = f32[328,128]{1,0:T(8,128)S(1)} collective-permute-done((f32[328,128]{1,0:T(8,128)S(1)}, f32[328,128]{1,0:T(8,128)S(1)}, u32[]{:S(2)}, u32[]{:S(2)}) %collective-permute-start.7) | collective-permute-done | bytes 167968 | tf_op jit(solution)/shard_map/ppermute | solution.py:342
  82.3 1.2 %shard_map.124.own_top = f32[160,128]{1,0:T(8,128)S(1)} custom-call(s32[6]{0:T(128)S(1)} %shift-right-arithmetic_and_fusion.above, f32[328,128]{1,0:T(8,128)S(1)} %shard_map.123.own.rest_4_, f32[328,128]{1,0:T(8,128)S(1)} %collective-permute-done.7.got.rest_9_), custom_call_target="tpu_custom_call" | custom-call | tf_op jit(solution)/shard_map/pallas_call | solution.py:292
  83.5 3.9 %collective-permute-start.8 = (f32[160,128]{1,0:T(8,128)S(1)}, f32[160,128]{1,0:T(8,128)S(1)}, u32[]{:S(2)}, u32[]{:S(2)}) collective-permute-start(f32[160,128]{1,0:T(8,128)S(1)} %shard_map.124.own_top), channel_id=1, source_target_pairs={{0,384},{8,392},{16,400},{24,408},{32,416},{40,424},{48,432},{56,4... | collective-permute-start | bytes 245768 | tf_op jit(solution)/shard_map/ppermute | solution.py:352
  87.5 4.6 %collective-permute-done.8.got_top = f32[160,128]{1,0:T(8,128)S(1)} collective-permute-done((f32[160,128]{1,0:T(8,128)S(1)}, f32[160,128]{1,0:T(8,128)S(1)}, u32[]{:S(2)}, u32[]{:S(2)}) %collective-permute-start.8) | collective-permute-done | bytes 81952 | tf_op jit(solution)/shard_map/ppermute | solution.py:352
  92.1 5.1 %shard_map.125 = f32[8,2,320]{2,1,0:T(2,128)} custom-call(s32[6]{0:T(128)S(1)} %shift-right-arithmetic_and_fusion.above, f32[160,128]{1,0:T(8,128)S(1)} %shard_map.124.own_top, f32[160,128]{1,0:T(8,128)S(1)} %collective-permute-done.8.got_top, f32[328,128]{1,0:T(8,128)S(1)} %get-tuple-element.14.own.rest_0_, f32[328,128]{1,0:T(8,128)S(1)} %shard_map.120.own.rest_1_, ...), custom_call_target="tpu_custom_call" | custom-call | tf_op jit(solution)/shard_map/pallas_call | solution.py:292
  (23 shorter events, 0.1 us)
Async XLA Ops:
  0.0 9.0 %copy-start.12 = (s32[1,1,2]{2,1,0:T(1,128)S(1)}, s32[1,1,2]{2,1,0:T(1,128)}, u32[]{:S(2)}) copy-start(s32[1,1,2]{2,1,0:T(1,128)} %param.19) | copy-start | bytes 28
  0.0 19.0 %collective-permute-start.1 = (f32[8,2,320]{2,1,0:T(2,128)}, f32[8,2,320]{2,1,0:T(2,128)S(1)}, u32[]{:S(2)}, u32[]{:S(2)}) collective-permute-start(f32[8,2,320]{2,1,0:T(2,128)} %bitcast.18), channel_id=1, source_target_pairs={{1,0},{2,1},{3,2},{4,3},{5,4},{6,5},{7,6},{0,7},{9,8},{10,9},{11,1... | collective-permute-start | bytes 61448 | tf_op jit(solution)/shard_map/ppermute | solution.py:319
  7.1 11.9 %collective-permute-start = (f32[8,2,320]{2,1,0:T(2,128)}, f32[8,2,320]{2,1,0:T(2,128)S(1)}, u32[]{:S(2)}, u32[]{:S(2)}) collective-permute-start(f32[8,2,320]{2,1,0:T(2,128)} %bitcast.19), channel_id=1, source_target_pairs={{0,1},{1,2},{2,3},{3,4},{4,5},{5,6},{6,7},{7,0},{8,9},{9,10},{10,1... | collective-permute-start | bytes 61448 | tf_op jit(solution)/shard_map/ppermute | solution.py:318
  9.0 0.7 copy-start.11
  9.8 1.2 %copy-start = (f32[1,1,2,320,320]{4,3,2,1,0:T(8,128)S(1)}, f32[1,1,2,320,320]{4,3,2,1,0:T(8,128)}, u32[]{:S(2)}) copy-start(f32[1,1,2,320,320]{4,3,2,1,0:T(8,128)} %param.14) | copy-start | bytes 2457604
  11.0 0.9 copy-start.1
  11.9 0.9 copy-start.3
  12.8 0.9 copy-start.4
  13.6 0.9 copy-start.9
  14.5 4.5 %copy-start.2 = (f32[1,1,2,80,80]{4,3,2,1,0:T(8,128)S(1)}, f32[1,1,2,80,80]{4,3,2,1,0:T(8,128)}, u32[]{:S(2)}) copy-start(f32[1,1,2,80,80]{4,3,2,1,0:T(8,128)} %param.16) | copy-start | bytes 153604
  14.5 4.5 %copy-start.5 = (f32[1,1,2,80,80]{4,3,2,1,0:T(8,128)S(1)}, f32[1,1,2,80,80]{4,3,2,1,0:T(8,128)}, u32[]{:S(2)}) copy-start(f32[1,1,2,80,80]{4,3,2,1,0:T(8,128)} %param.17) | copy-start | bytes 153604
  14.5 4.5 %copy-start.6 = (f32[1,1,2,80,80]{4,3,2,1,0:T(8,128)S(1)}, f32[1,1,2,80,80]{4,3,2,1,0:T(8,128)}, u32[]{:S(2)}) copy-start(f32[1,1,2,80,80]{4,3,2,1,0:T(8,128)} %param.18) | copy-start | bytes 153604
  14.5 4.5 %copy-start.7 = (bf16[320,80]{1,0:T(8,128)(2,1)S(1)}, bf16[320,80]{1,0:T(8,128)(2,1)}, u32[]{:S(2)}) copy-start(bf16[320,80]{1,0:T(8,128)(2,1)} %constant.19.clone.pick_e) | copy-start | bytes 153604
  14.5 4.5 %copy-start.8 = (bf16[320,80]{1,0:T(8,128)(2,1)S(1)}, bf16[320,80]{1,0:T(8,128)(2,1)}, u32[]{:S(2)}) copy-start(bf16[320,80]{1,0:T(8,128)(2,1)} %constant.18.clone.pick_w) | copy-start | bytes 153604
  15.9 3.1 %collective-permute-start.2 = (f32[2,8,80]{2,1,0:T(8,128)S(1)}, f32[2,8,80]{2,1,0:T(8,128)S(1)}, u32[]{:S(2)}, u32[]{:S(2)}) collective-permute-start(f32[2,8,80]{2,1,0:T(8,128)S(1)} %get-tuple-element.11), channel_id=1, source_target_pairs={{8,0},{16,8},{24,16},{32,24},{40,32},{48,40},{56,48},{64,56},{72,6... | collective-permute-start | bytes 15368 | tf_op jit(solution)/shard_map/ppermute | solution.py:331
  19.0 0.7 copy-start.10
  22.4 5.3 %collective-permute-start.3 = (f32[328,128]{1,0:T(8,128)S(1)}, f32[328,128]{1,0:T(8,128)S(1)}, u32[]{:S(2)}, u32[]{:S(2)}) collective-permute-start(f32[328,128]{1,0:T(8,128)S(1)} %get-tuple-element.14.own.rest_0_), channel_id=1, source_target_pairs={{0,8},{8,0},{16,24},{24,16},{32,40},{40,32},{48,56},{56,48},{64,72... | collective-permute-start | bytes 503816 | tf_op jit(solution)/shard_map/ppermute | solution.py:342
  28.9 14.1 %collective-permute-start.4 = (f32[328,128]{1,0:T(8,128)S(1)}, f32[328,128]{1,0:T(8,128)S(1)}, u32[]{:S(2)}, u32[]{:S(2)}) collective-permute-start(f32[328,128]{1,0:T(8,128)S(1)} %shard_map.120.own.rest_1_), channel_id=1, source_target_pairs={{0,16},{8,24},{16,0},{24,8},{32,48},{40,56},{48,32},{56,40},{64,80... | collective-permute-start | bytes 503816 | tf_op jit(solution)/shard_map/ppermute | solution.py:342
  44.0 15.1 %collective-permute-start.5 = (f32[328,128]{1,0:T(8,128)S(1)}, f32[328,128]{1,0:T(8,128)S(1)}, u32[]{:S(2)}, u32[]{:S(2)}) collective-permute-start(f32[328,128]{1,0:T(8,128)S(1)} %shard_map.121.own.rest_2_), channel_id=1, source_target_pairs={{0,48},{8,56},{16,32},{24,40},{32,16},{40,24},{48,0},{56,8},{64,11... | collective-permute-start | bytes 503816 | tf_op jit(solution)/shard_map/ppermute | solution.py:342
  60.3 8.9 %collective-permute-start.6 = (f32[328,128]{1,0:T(8,128)S(1)}, f32[328,128]{1,0:T(8,128)S(1)}, u32[]{:S(2)}, u32[]{:S(2)}) collective-permute-start(f32[328,128]{1,0:T(8,128)S(1)} %shard_map.122.own.rest_3_), channel_id=1, source_target_pairs={{0,64},{8,72},{16,80},{24,88},{32,96},{40,104},{48,112},{56,120},{... | collective-permute-start | bytes 503816 | tf_op jit(solution)/shard_map/ppermute | solution.py:342
  70.3 12.0 %collective-permute-start.7 = (f32[328,128]{1,0:T(8,128)S(1)}, f32[328,128]{1,0:T(8,128)S(1)}, u32[]{:S(2)}, u32[]{:S(2)}) collective-permute-start(f32[328,128]{1,0:T(8,128)S(1)} %shard_map.123.own.rest_4_), channel_id=1, source_target_pairs={{0,128},{8,136},{16,144},{24,152},{32,160},{40,168},{48,176},{56,1... | collective-permute-start | bytes 503816 | tf_op jit(solution)/shard_map/ppermute | solution.py:342
  83.5 8.5 %collective-permute-start.8 = (f32[160,128]{1,0:T(8,128)S(1)}, f32[160,128]{1,0:T(8,128)S(1)}, u32[]{:S(2)}, u32[]{:S(2)}) collective-permute-start(f32[160,128]{1,0:T(8,128)S(1)} %shard_map.124.own_top), channel_id=1, source_target_pairs={{0,384},{8,392},{16,400},{24,408},{32,416},{40,424},{48,432},{56,4... | collective-permute-start | bytes 245768 | tf_op jit(solution)/shard_map/ppermute | solution.py:352

commit v2 on v1

v2 whole, which is shorter than its diff:
```python
import functools

import jax
import jax.numpy as jnp
import numpy as np
from jax import lax
from jax.experimental import pallas as pl
from jax.experimental.pallas import tpu as pltpu
from jax.sharding import PartitionSpec as P

NVAR = 5
NB = 4
FACE = 80
DOF = 320
LANES = 128
VEC = FACE
REST = FACE + 8
HALF = LANES - REST
BF16 = jnp.bfloat16
F32 = jnp.float32
NN = (((1,), (0,)), ((), ()))
NT = (((1,), (1,)), ((), ()))


def split(x):
    hi = x.astype(BF16)
    return hi, (x - hi.astype(F32)).astype(BF16)


def dot(a, b, dims=NN):
    ah, al = split(a)
    bh, bl = split(b)
    one = functools.partial(lax.dot_general, dimension_numbers=dims, preferred_element_type=F32)
    return one(ah, bh) + (one(ah, bl) + one(al, bh))


def pick(x, onehot, dims=NN):
    hi = x.astype(BF16)
    rest = x - hi.astype(F32)
    mid = rest.astype(BF16)
    low = (rest - mid.astype(F32)).astype(BF16)
    one = functools.partial(lax.dot_general, dimension_numbers=dims, preferred_element_type=F32)
    return one(hi, onehot) + one(mid, onehot) + one(low, onehot)


def put(onehot, x):
    hi = x.astype(BF16)
    rest = x - hi.astype(F32)
    mid = rest.astype(BF16)
    low = (rest - mid.astype(F32)).astype(BF16)
    one = functools.partial(lax.dot_general, dimension_numbers=NN, preferred_element_type=F32)
    return one(onehot, hi) + one(onehot, mid) + one(onehot, low)


def stream_pick(j):
    s = np.zeros((NVAR, NB, NB * NB, FACE), np.float32)
    for v in range(NVAR):
        for q in range(NB * NB):
            s[v, j, q, v * NB * NB + q] = 1
    return s.reshape(DOF, FACE)


def span_pick(j):
    s = np.zeros((NVAR, NB, NB, NB, FACE), np.float32)
    for v in range(NVAR):
        for a in range(NB):
            for c in range(NB):
                s[v, a, j, c, (v * NB + a) * NB + c] = 1
    return s.reshape(DOF, FACE)


def stream_rows(x, j):
    step = NB * NB
    return jnp.concatenate(
        [x[(v * NB + j) * step : (v * NB + j + 1) * step] for v in range(NVAR)], axis=0
    )


def place_rows(x, j):
    step = NB * NB
    zeros = jnp.zeros((step, x.shape[1]), x.dtype)
    parts = []
    for v in range(NVAR):
        for a in range(NB):
            parts.append(x[v * step : (v + 1) * step] if a == j else zeros)
    return jnp.concatenate(parts, axis=0)


def lane_of(shape):
    return lax.broadcasted_iota(jnp.int32, shape, 1)


def pack(ab, be, d):
    lane = lane_of(ab.shape)
    left = jnp.where(lane < REST, ab, pltpu.roll(d, REST, 1))
    right = jnp.where(lane < REST, be, pltpu.roll(d, REST - HALF, 1))
    return left, right


def unpack_d(left, right):
    lane = lane_of(left.shape)
    return jnp.where(
        lane < HALF, pltpu.roll(left, LANES - REST, 1), pltpu.roll(right, LANES - REST + HALF, 1)
    )


def tall(x):
    return jnp.concatenate([x, jnp.zeros((LANES - FACE, x.shape[1]), x.dtype)], axis=0)


def widen(x):
    return jnp.concatenate([x, jnp.zeros((x.shape[0], LANES - x.shape[1]), x.dtype)], axis=1)


def side(x):
    x = widen(x)
    before = jnp.zeros((VEC, LANES), x.dtype)
    after = jnp.zeros((LANES - REST, LANES), x.dtype)
    return jnp.concatenate([before, x, after], axis=0)


def vec_only(x):
    lane = lane_of(x.shape)
    return jnp.where((lane >= VEC) & (lane < REST), x, 0.0)


class Segment:
    def __init__(self, left, right, swap):
        self.left, self.right, self.swap = left, right, swap

    @staticmethod
    def of(ref):
        left = [ref[2 * p * FACE : (2 * p + 1) * FACE] for p in range(2)]
        right = [ref[(2 * p + 1) * FACE : (2 * p + 2) * FACE] for p in range(2)]
        return Segment(left, right, ref[4 * FACE :])

    def write(self, ref):
        for p in range(2):
            ref[2 * p * FACE : (2 * p + 1) * FACE] = self.left[p]
            ref[(2 * p + 1) * FACE : (2 * p + 2) * FACE] = self.right[p]
        ref[4 * FACE :] = self.swap

    def top(self, ref):
        for p in range(2):
            left, right = self.left[p], self.right[p]
            lane = lane_of(left.shape)
            tile = jnp.where(lane < VEC, unpack_d(left, right), left)
            tile = jnp.where(lane < REST, tile, pltpu.roll(right, 8, 1))
            ref[p * FACE : (p + 1) * FACE] = jnp.where(lane < REST + 8, tile, self.swap[:1])


def behind(swap, pair, p):
    return jnp.where(swap[:1] > 0.5, pair[1 - p], pair[p])


def join(first, second):
    lefts, rights = [], []
    for p in range(2):
        left1, right1 = first.left[p], first.right[p]
        left2, right2 = behind(first.swap, second.left, p), behind(first.swap, second.right, p)
        d1, d2 = unpack_d(left1, right1), unpack_d(left2, right2)
        lane = lane_of(left1.shape)
        through = dot(jnp.concatenate([left2, d2], axis=0), tall(left1))
        ab = through[:FACE] + vec_only(left2)
        back = through[FACE:] + vec_only(right2)
        both = dot(right1, tall(jnp.concatenate([right2, back], axis=1)))
        be = jnp.where(lane < VEC, both[:, :LANES], right1 + both[:, LANES:])
        left, right = pack(ab, be, d1 + both[:, LANES:])
        lefts.append(left)
        rights.append(right)
    return Segment(lefts, rights, jnp.abs(first.swap - second.swap))


def ordered(upper, own, got):
    up = upper[...][:1] > 0.5

    def pair(a, b):
        return jnp.where(up, a, b)

    def seg(a, b):
        return Segment(
            [pair(a.left[p], b.left[p]) for p in range(2)],
            [pair(a.right[p], b.right[p]) for p in range(2)],
            pair(a.swap, b.swap),
        )

    return seg(got, own), seg(own, got)


def fetch(pairs, sems):
    copies = [pltpu.make_async_copy(a, b, sems.at[i]) for i, (a, b) in enumerate(pairs)]
    for copy in copies:
        copy.start()
    for copy in copies:
        copy.wait()


def faces_kernel(guess_hbm, up_hbm, map_hbm, pin, pw, pe, west, east, lag, swap, guess, up, which, sems):
    fetch([(guess_hbm, guess), (up_hbm, up), (map_hbm, which)], sems)
    flag = jnp.full((8, LANES), which[0, 0, 0].astype(F32), F32)
    swap[...] = flag
    swapped = flag[:, :FACE] > 0.5
    made = []
    for n in range(2):
        mine = guess[0, 0, :, n, :]
        west[n] = pick(mine, pw[...])
        east[n] = pick(mine, pe[...])
        made.append(dot(pick(mine, pin[...]), up[0, 0, n], NT))
    for p in range(2):
        lag[p] = jnp.where(swapped, made[1 - p], made[p])


def maps_kernel(
    inv_hbm, low_hbm, up_hbm, west_hbm, east_hbm, rhs_hbm, swap, pout, pw, pe,
    own, zin, zout, zwest, zeast, kwest, keast, solved,
    inv, low, up, west, east, rhs, sems,
):
    fetch(
        [(inv_hbm, inv), (low_hbm, low), (up_hbm, up), (west_hbm, west), (east_hbm, east), (rhs_hbm, rhs)],
        sems,
    )
    made = []
    for n in range(2):
        m, u = inv[0, 0, n], up[0, 0, n]
        sides = jnp.concatenate(
            [
                widen(place_rows(low[0, 0, n], 0)),
                widen(put(pw[...], west[0, 0, n])),
                widen(put(pe[...], east[0, 0, n])),
            ],
            axis=1,
        )
        z = dot(m, sides)
        z_in, z_west, z_east = z[:, :LANES], z[:, LANES : 2 * LANES], z[:, 2 * LANES :]
        z_out = pick(m, pout[...])
        zin[n], zout[n], zwest[n], zeast[n] = z_in, z_out, z_west, z_east
        coupled = dot(
            u, jnp.concatenate([stream_rows(a, 0) for a in (z_in, z_out, z_west, z_east)], axis=1)
        )
        kwest[n] = coupled[:, 2 * LANES : 3 * LANES]
        keast[n] = coupled[:, 3 * LANES :]
        y = dot(rhs[0, 0, :, n, :], m, NT)
        solved[n] = y
        y_in, y_out = [
            jnp.concatenate(
                [y[:, (v * NB + j) * NB * NB : (v * NB + j + 1) * NB * NB] for v in range(NVAR)], axis=1
            )
            for j in (0, 3)
        ]
        b = side(y_out).T[:FACE]
        e = dot(u, side(y_in)[:, :FACE], NT)
        made.append(pack(b - stream_rows(z_in, 3), e - coupled[:, LANES : 2 * LANES], -coupled[:, :LANES]))
    flag = swap[...]
    Segment(
        [behind(flag, [made[0][0], made[1][0]], p) for p in range(2)],
        [behind(flag, [made[0][1], made[1][1]], p) for p in range(2)],
        flag,
    ).write(own)


def vectors_kernel(maps, zout, zwest, zeast, kwest, keast, from_west, from_east, lag, own):
    seg = Segment.of(maps)
    b, e = [], []
    for n in range(2):
        far_west, far_east = side(from_west[n]), side(from_east[n])
        into = jnp.concatenate([stream_rows(z[n], 3) for z in (zwest, zeast, zout)], axis=1)
        b.append(dot(into, jnp.concatenate([far_west, far_east, side(lag[n])], axis=1), NT))
        back = jnp.concatenate([kwest[n], keast[n]], axis=1)
        e.append(dot(back, jnp.concatenate([far_west, far_east], axis=1), NT))
    Segment(
        [seg.left[p] - behind(seg.swap, b, p) for p in range(2)],
        [seg.right[p] - behind(seg.swap, e, p) for p in range(2)],
        seg.swap,
    ).write(own)


def pair_kernel(last, upper, own, got, out):
    both = join(*ordered(upper, Segment.of(own), Segment.of(got)))
    if last:
        both.top(out)
    else:
        both.write(out)


def four_kernel(got, out, halves):
    halves_of = [join(Segment.of(got.at[2 * i]), Segment.of(got.at[2 * i + 1])) for i in range(2)]
    join(*halves_of).write(out)
    for i in range(2):
        halves_of[i].write(halves.at[i])


def start_place():
    eye = (lax.broadcasted_iota(jnp.int32, (FACE, LANES), 0) == lane_of((FACE, LANES))).astype(F32)
    zero = jnp.zeros((FACE, LANES), F32)
    return [[eye, zero, eye] for _ in range(2)]


def widen_place(place, upper, own, got):
    lane = lane_of((FACE, LANES))
    keep = lane < REST
    up = upper[:1] > 0.5
    made = []
    for p in range(2):
        near = [behind(got.swap, [place[0][i], place[1][i]], p) for i in range(3)]
        sib = tall(got.left[p])
        moved = dot(jnp.concatenate([near[0], near[1]], axis=0), sib)
        above = [
            jnp.where(keep, moved[:FACE], 0.0) + vec_only(near[0]),
            jnp.where(keep, moved[FACE:], 0.0) + vec_only(near[1]),
            near[2],
        ]
        left2, right2 = behind(own.swap, got.left, p), behind(own.swap, got.right, p)
        back = dot(unpack_d(left2, right2), tall(own.left[p])) + vec_only(right2)
        turned = dot(place[p][2], tall(jnp.concatenate([back, right2], axis=1)))
        below = [
            place[p][0],
            place[p][1] + jnp.where(keep, turned[:, :LANES], 0.0),
            jnp.where(lane < VEC, turned[:, LANES:], 0.0),
        ]
        made.append([jnp.where(up, above[i], below[i]) for i in range(3)])
    return made


def read_place(ref):
    return [[ref[p, i] for i in range(3)] for p in range(2)]


def write_place(ref, place):
    for p in range(2):
        for i in range(3):
            ref[p, i] = place[p][i]


def first_place_kernel(upper, own, got, out, swap_out):
    mine, other = Segment.of(own), Segment.of(got)
    write_place(out, widen_place(start_place(), upper[...], mine, other))
    swap_out[...] = jnp.abs(mine.swap - jnp.where(upper[...] > 0.5, other.swap, 0.0))


def place_kernel(upper, own, got, place, swap, out, swap_out):
    mine, other = Segment.of(own), Segment.of(got)
    write_place(out, widen_place(read_place(place), upper[...], mine, other))
    swap_out[...] = jnp.abs(swap[...] - jnp.where(upper[...] > 0.5, other.swap, 0.0))


def four_place_kernel(at, uppers, got, halves, place, swap, out, swap_out):
    j = at[0]
    half = j // 2
    mine, other = Segment.of(got.at[j]), Segment.of(got.at[j + 1 - 2 * (j - 2 * half)])
    made = widen_place(read_place(place), uppers[0], mine, other)
    x = jnp.abs(swap[...] - jnp.where(uppers[0] > 0.5, other.swap, 0.0))
    mine, other = Segment.of(halves.at[half]), Segment.of(halves.at[1 - half])
    write_place(out, widen_place(made, uppers[1], mine, other))
    swap_out[...] = jnp.abs(x - jnp.where(uppers[1] > 0.5, other.swap, 0.0))


def answer_kernel(
    upper, own, got, place, swap, zin, zout, zwest, zeast, from_west, from_east, solved,
    fixed, free, turn,
):
    mine, other = Segment.of(own), Segment.of(got)
    made = widen_place(read_place(place), upper[0], mine, other)
    x = jnp.abs(swap[...] - jnp.where(upper[0] > 0.5, other.swap, 0.0))
    turn[...] = x
    up = upper[1][:1] > 0.5
    for n in range(2):
        p0, q0, r0 = [behind(x, [made[0][i], made[1][i]], n) for i in range(3)]
        t = jnp.where(up, p0, vec_only(p0))
        c = jnp.where(up, q0, jnp.where(lane_of(r0.shape) < VEC, r0, 0.0) + vec_only(q0))
        f = dot(jnp.concatenate([zin[n], zout[n]], axis=1), jnp.concatenate([tall(t), tall(c)], axis=0))
        free[n] = f
        sides = jnp.concatenate([widen(from_west[n]), widen(from_east[n])], axis=1)
        fixed[n] = (
            solved[n]
            - dot(sides, jnp.concatenate([zwest[n], zeast[n]], axis=1), NT)
            - f.T[VEC:REST]
        )


def last_kernel(upper, swap, own, got, fixed, free, out):
    up = upper[...][:1] > 0.5
    mine = [own[p * FACE : (p + 1) * FACE] for p in range(2)]
    far = [got[p * FACE : (p + 1) * FACE] for p in range(2)]
    own_swap = jnp.broadcast_to(mine[0][:1, LANES - 1 :], (1, LANES))
    far_swap = jnp.broadcast_to(far[0][:1, LANES - 1 :], (1, LANES))
    unknown = []
    for p in range(2):
        above = behind(far_swap, far, p)
        sib = behind(own_swap, far, p)
        below = dot(sib, tall(vec_only(mine[p]))) + pltpu.roll(sib, LANES - 8, 1)
        unknown.append(jnp.where(up, above, below).T[VEC:REST])
    for n in range(2):
        x = widen(behind(swap[...][:, :FACE], unknown, n))
        out[:, n, :] = fixed[n] - dot(x, free[n], NT)


ANY = pl.BlockSpec(memory_space=pl.ANY)
VMEM = pl.BlockSpec(memory_space=pltpu.VMEM)
SMEM = pl.BlockSpec(memory_space=pltpu.SMEM)


def call(kernel, out_shape, *operands, any_first=0, smem_first=0, scratch=(), flops=0):
    specs = [ANY if i < any_first else SMEM if i < smem_first else VMEM for i in range(len(operands))]
    several = isinstance(out_shape, tuple)
    return pl.pallas_call(
        kernel,
        out_shape=out_shape,
        in_specs=specs,
        out_specs=tuple(VMEM for _ in out_shape) if several else VMEM,
        scratch_shapes=list(scratch),
        cost_estimate=pl.CostEstimate(flops=flops, bytes_accessed=1 << 20, transcendentals=0),
        compiler_params=pltpu.CompilerParams(vmem_limit_bytes=24 * 1024 * 1024),
    )(*operands)


def f32(*shape):
    return jax.ShapeDtypeStruct(shape, F32)


ROWS = 4 * FACE + 8
TOP = (6, 7, 4, 5, 2, 3, 0, 1)


def per_device(
    rhs_field, guess, inverse_diag, lower_block, upper_block, west_block, east_block, inflow_map
):
    wide = lax.axis_size("span")
    layers = lax.axis_size("stream")
    place = lax.axis_index("stream")
    bits = (place >> jnp.arange(6, dtype=jnp.int32)) & 1
    upper = jnp.broadcast_to(bits.astype(F32)[:, None, None], (6, 8, LANES))
    pin, pout = jnp.asarray(stream_pick(0), BF16), jnp.asarray(np.pad(stream_pick(3), ((0, 0), (0, LANES - FACE))), BF16)
    pw, pe = jnp.asarray(span_pick(0), BF16), jnp.asarray(span_pick(3), BF16)
    dma = pltpu.SemaphoreType.DMA
    west_face, east_face, lag_out, swap = call(
        faces_kernel,
        (f32(2, 8, FACE), f32(2, 8, FACE), f32(2, 8, FACE), f32(8, LANES)),
        guess, upper_block, inflow_map, pin, pw, pe,
        any_first=3,
        scratch=(
            pltpu.VMEM(guess.shape, F32), pltpu.VMEM(upper_block.shape, F32),
            pltpu.SMEM(inflow_map.shape, jnp.int32), dma((3,)),
        ),
    )
    ring = [(i, (i + 1) % wide) for i in range(wide)]
    from_west = lax.ppermute(east_face, "span", ring)
    from_east = lax.ppermute(west_face, "span", [(b, a) for a, b in ring])
    lag = lax.ppermute(lag_out, "stream", [(i + 1, i) for i in range(layers - 1)])
    maps, zin, zout, zwest, zeast, kwest, keast, solved = call(
        maps_kernel,
        (
            f32(ROWS, LANES), *(f32(2, DOF, LANES) for _ in range(4)),
            f32(2, FACE, LANES), f32(2, FACE, LANES), f32(2, 8, DOF),
        ),
        inverse_diag, lower_block, upper_block, west_block, east_block, rhs_field, swap, pout, pw, pe,
        any_first=6,
        scratch=(
            *(pltpu.VMEM(a.shape, F32) for a in (inverse_diag, lower_block, upper_block, west_block, east_block, rhs_field)),
            dma((6,)),
        ),
    )
    own = call(
        vectors_kernel, f32(ROWS, LANES),
        maps, zout, zwest, zeast, kwest, keast, from_west, from_east, lag,
    )

    def across(x, distance):
        return lax.ppermute(x, "stream", [(i, i ^ distance) for i in range(layers)])

    got = across(own, 1)
    pair = call(functools.partial(pair_kernel, False), f32(ROWS, LANES), upper[0], own, got)
    here = (f32(2, 3, FACE, LANES), f32(8, LANES))
    spot, turn = call(first_place_kernel, here, upper[0], own, got)
    groups = [[8 * g + c + 2 * j for j in range(4)] for g in range(layers // 8) for c in range(2)]
    four = lax.all_to_all(
        jnp.broadcast_to(pair[None], (4, ROWS, LANES)), "stream", 0, 0, axis_index_groups=groups
    )
    eight, halves = call(four_kernel, (f32(ROWS, LANES), f32(2, ROWS, LANES)), four)
    got = across(eight, 8)
    spot, turn = call(
        four_place_kernel, here,
        ((place >> 1) & 3).reshape(1), upper[1:3], four, halves, spot, turn,
        smem_first=1,
    )
    got, spot, turn = lax.optimization_barrier((got, spot, turn))
    sixteen = call(functools.partial(pair_kernel, False), f32(ROWS, LANES), upper[3], eight, got)
    got2 = across(sixteen, 16)
    spot, turn = call(place_kernel, here, upper[3], eight, got, spot, turn)
    got2, spot, turn = lax.optimization_barrier((got2, spot, turn))
    half = call(functools.partial(pair_kernel, True), f32(2 * FACE, LANES), upper[4], sixteen, got2)
    got3 = lax.ppermute(half, "stream", [(i, TOP[i // 8] * 8 + i % 8) for i in range(layers)])
    fixed, free, turn = call(
        answer_kernel, (f32(2, 8, DOF), f32(2, DOF, LANES), f32(8, LANES)),
        upper[4:6], sixteen, got2, spot, turn, zin, zout, zwest, zeast, from_west, from_east, solved,
    )
    out = call(last_kernel, f32(8, 2, DOF), upper[5], turn, half, got3, fixed, free)
    return out[None, None]


def solution(mesh):
    in_specs = (
        P("stream", "span", None, None, None),
        P("stream", "span", None, None, None),
        P("stream", "span", None, None, None),
        P("stream", "span", None, None, None),
        P("stream", "span", None, None, None),
        P("stream", "span", None, None, None),
        P("stream", "span", None, None, None),
        P("stream", "span", None),
    )
    out_specs = P("stream", "span", None, None, None)
    return jax.shard_map(
        per_device, mesh=mesh, in_specs=in_specs, out_specs=out_specs, check_vma=False
    )
```

time: 97.8 us -> 94.9 us (0.970)
  the two profiles are of different devices: /device:TPU:64 before, /device:TPU:144 now
where the time goes in v2:
time: 94.9 us; the launch traced here: 94.1 us
  starting transfers between devices  36.2 us (38%)
  waiting for transfers between devices  30.2 us (32%)
  Pallas kernels  14.5 us (15%)
  local copies, waits for them, and re-layouts  13 us (14%)
    all_to_all x1, waiting for transfers between devices, per_device(): lax.all_to_all(jnp.broadcast_to(pair[None], (4, ROWS, LANES)), 'stream',...  18.4 us
    pallas_call x12, Pallas kernels, call(): pl.pallas_call(kernel, out_shape=out_shape, in_specs=specs, out_specs=tup...  14.5 us
    all_to_all x1, starting transfers between devices, per_device(): lax.all_to_all(jnp.broadcast_to(pair[None], (4, ROWS, LANES)), 'stream',...  9.4 us
    ppermute x3, waiting for transfers between devices, across(): return lax.ppermute(x, 'stream', [(i, i ^ distance) for i in range(layers)])  9.03 us
    unnamed x30, local copies, waits for them, and re-layouts  8.81 us
    ppermute x1, starting transfers between devices, per_device(): lax.ppermute(half, 'stream', [(i, TOP[i // 8] * 8 + i % 8) for i in range...  8.56 us
    ppermute x3, starting transfers between devices, across(): return lax.ppermute(x, 'stream', [(i, i ^ distance) for i in range(layers)])  7.92 us
    ppermute x1, starting transfers between devices, per_device(): from_west = lax.ppermute(east_face, 'span', ring)  4.28 us
  transfers between devices with their start and end apart: 8, of which 5 were waited for; matrix products, arithmetic and copies ran while one was open for 1% of the time, Pallas kernels for 9%

profile of v2, /device:TPU:144, one launch (start us, length us, event | category | flops | bytes accessed | tf_op | source)
XLA Modules:
  0.0 94.1 jit_solution(6328114876920762751)
XLA Ops:
  0.0 0.9 copy-done.1
  0.9 0.9 copy-done.3
  1.8 0.9 copy-done.5
  2.7 0.9 copy-done.11
  3.6 0.7 copy-done.12
  4.3 0.7 copy-done.14
  5.0 1.4 %shard_map.118 = (f32[2,8,80]{2,1,0:T(8,128)S(1)}, f32[2,8,80]{2,1,0:T(8,128)S(1)}, f32[2,8,80]{2,1,0:T(8,128)S(1)}, f32[8,128]{1,0:T(8,128)S(1)}) custom-call(f32[1,1,8,2,320]{4,3,2,1,0:T(2,128)S(1)} %copy-done.12, f32[1,1,2,80,80]{4,3,2,1,0:T(8,128)S(1)} %copy-done.1, s32[1,1,2]{2,1,0:T(1,128)S(1)} %copy-done.14, bf16[320,80]{1,0:T(8,128)(2,1)S(1)} %copy-done.11, ...), custom_call_target="tpu_custom_call" | custom-call | bytes 1048576 | tf_op jit(solution)/shard_map/pallas_call | solution.py:405
  6.4 4.3 %collective-permute-start = (f32[2,8,80]{2,1,0:T(8,128)S(1)}, f32[2,8,80]{2,1,0:T(8,128)S(1)}, u32[]{:S(2)}, u32[]{:S(2)}) collective-permute-start(f32[2,8,80]{2,1,0:T(8,128)S(1)} %get-tuple-element.41), channel_id=1, source_target_pairs={{0,1},{1,2},{2,3},{3,4},{4,5},{5,6},{6,7},{7,0},{8,9},{9,10},{10,1... | collective-permute-start | bytes 15368 | tf_op jit(solution)/shard_map/ppermute | solution.py:446
  10.7 4.1 %collective-permute-start.1 = (f32[2,8,80]{2,1,0:T(8,128)S(1)}, f32[2,8,80]{2,1,0:T(8,128)S(1)}, u32[]{:S(2)}, u32[]{:S(2)}) collective-permute-start(f32[2,8,80]{2,1,0:T(8,128)S(1)} %get-tuple-element.42), channel_id=1, source_target_pairs={{1,0},{2,1},{3,2},{4,3},{5,4},{6,5},{7,6},{0,7},{9,8},{10,9},{11,1... | collective-permute-start | bytes 15368 | tf_op jit(solution)/shard_map/ppermute | solution.py:447
  14.8 1.9 %collective-permute-start.2 = (f32[2,8,80]{2,1,0:T(8,128)S(1)}, f32[2,8,80]{2,1,0:T(8,128)S(1)}, u32[]{:S(2)}, u32[]{:S(2)}) collective-permute-start(f32[2,8,80]{2,1,0:T(8,128)S(1)} %get-tuple-element.43), channel_id=1, source_target_pairs={{8,0},{16,8},{24,16},{32,24},{40,32},{48,40},{56,48},{64,56},{72,6... | collective-permute-start | bytes 15368 | tf_op jit(solution)/shard_map/ppermute | solution.py:448
  16.8 1.2 %copy-done = f32[1,1,2,320,320]{4,3,2,1,0:T(8,128)S(1)} copy-done((f32[1,1,2,320,320]{4,3,2,1,0:T(8,128)S(1)}, f32[1,1,2,320,320]{4,3,2,1,0:T(8,128)}, u32[]{:S(2)}) %copy-start) | copy-done | bytes 819224
  18.0 0.9 copy-done.8
  18.9 0.9 copy-done.9
  19.8 0.9 copy-done.10
  20.6 4.4 %shard_map.119 = (f32[328,128]{1,0:T(8,128)S(1)}, f32[2,320,128]{2,1,0:T(8,128)S(1)}, f32[2,320,128]{2,1,0:T(8,128)S(1)}, f32[2,320,128]{2,1,0:T(8,128)S(1)}, f3...) custom-call(f32[1,1,2,320,320]{4,3,2,1,0:T(8,128)S(1)} %copy-done, ...), custom_call_target="tpu_custom_call" | custom-call | bytes 1048576 | tf_op jit(solution)/shard_map/pallas_call | solution.py:405
  25.5 2.4 %collective-permute-start.3 = (f32[328,128]{1,0:T(8,128)S(1)}, f32[328,128]{1,0:T(8,128)S(1)}, u32[]{:S(2)}, u32[]{:S(2)}) collective-permute-start(f32[328,128]{1,0:T(8,128)S(1)} %shard_map.120.own), channel_id=1, source_target_pairs={{0,8},{8,0},{16,24},{24,16},{32,40},{40,32},{48,56},{56,48},{64,72... | collective-permute-start | bytes 503816 | tf_op jit(solution)/shard_map/ppermute | solution.py:468
  30.1 0.9 broadcast_in_dim.40
  31.0 9.4 %all-to-all-start = ((f32[4,328,128]{2,1,0:T(8,128)}), f32[4,328,128]{2,1,0:T(8,128)S(1)}, u32[]{:S(2)}, u32[]{:S(2)}) async-start(f32[4,328,128]{2,1,0:T(8,128)} %broadcast_in_dim.40), calls=%async_computation | async-start | bytes 1343488 | tf_op jit(solution)/shard_map/all_to_all | solution.py:475
  40.4 18.4 %all-to-all-done.got = f32[4,328,128]{2,1,0:T(8,128)S(1)} async-done(((f32[4,328,128]{2,1,0:T(8,128)}), f32[4,328,128]{2,1,0:T(8,128)S(1)}, u32[]{:S(2)}, u32[]{:S(2)}) %all-to-all-start) | async-done | bytes 671776 | tf_op jit(solution)/shard_map/all_to_all | solution.py:475
  58.8 1.3 %shard_map.122 = (f32[328,128]{1,0:T(8,128)S(1)}, f32[2,328,128]{2,1,0:T(8,128)S(1)}) custom-call(f32[4,328,128]{2,1,0:T(8,128)S(1)} %all-to-all-done.got), custom_call_target="tpu_custom_call" | custom-call | bytes 1048576 | tf_op jit(solution)/shard_map/pallas_call | solution.py:405
  60.1 3.4 %collective-permute-start.4 = (f32[328,128]{1,0:T(8,128)S(1)}, f32[328,128]{1,0:T(8,128)S(1)}, u32[]{:S(2)}, u32[]{:S(2)}) collective-permute-start(f32[328,128]{1,0:T(8,128)S(1)} %get-tuple-element.44.own), channel_id=1, source_target_pairs={{0,64},{8,72},{16,80},{24,88},{32,96},{40,104},{48,112},{56,120},{... | collective-permute-start | bytes 503816 | tf_op jit(solution)/shard_map/ppermute | solution.py:468
  63.6 0.6 shard_map.123
  64.3 1.3 %shard_map.124 = (f32[2,3,80,128]{3,2,1,0:T(8,128)S(1)}, f32[8,128]{1,0:T(8,128)S(1)}) custom-call(s32[1]{0:T(128)} %bitcast.4.at, f32[2,8,128]{2,1,0:T(8,128)S(1)} %broadcast_in_dim.41.uppers, f32[4,328,128]{2,1,0:T(8,128)S(1)} %all-to-all-done.got, f32[2,328,128]{2,1,0:T(8,128)S(1)} %get-tuple-element.45.halves, ...), custom_call_target="tpu_custom_call" | custom-call | bytes 1048576 | tf_op jit(solution)/shard_map/pallas_call | solution.py:405
  65.6 2.6 %collective-permute-done.4.got = f32[328,128]{1,0:T(8,128)S(1)} collective-permute-done((f32[328,128]{1,0:T(8,128)S(1)}, f32[328,128]{1,0:T(8,128)S(1)}, u32[]{:S(2)}, u32[]{:S(2)}) %collective-permute-start.4) | collective-permute-done | bytes 167968 | tf_op jit(solution)/shard_map/ppermute | solution.py:468
  69.4 2.1 %collective-permute-start.5 = (f32[328,128]{1,0:T(8,128)S(1)}, f32[328,128]{1,0:T(8,128)S(1)}, u32[]{:S(2)}, u32[]{:S(2)}) collective-permute-start(f32[328,128]{1,0:T(8,128)S(1)} %shard_map.125.own), channel_id=1, source_target_pairs={{0,128},{8,136},{16,144},{24,152},{32,160},{40,168},{48,176},{56,1... | collective-permute-start | bytes 503816 | tf_op jit(solution)/shard_map/ppermute | solution.py:468
  71.4 0.6 shard_map.126
  72.1 6.1 %collective-permute-done.5.got = f32[328,128]{1,0:T(8,128)S(1)} collective-permute-done((f32[328,128]{1,0:T(8,128)S(1)}, f32[328,128]{1,0:T(8,128)S(1)}, u32[]{:S(2)}, u32[]{:S(2)}) %collective-permute-start.5) | collective-permute-done | bytes 167968 | tf_op jit(solution)/shard_map/ppermute | solution.py:468
  78.9 0.7 shard_map.128.own
  79.5 8.6 %collective-permute-start.6 = (f32[160,128]{1,0:T(8,128)S(1)}, f32[160,128]{1,0:T(8,128)S(1)}, u32[]{:S(2)}, u32[]{:S(2)}) collective-permute-start(f32[160,128]{1,0:T(8,128)S(1)} %shard_map.128.own), channel_id=1, source_target_pairs={{0,384},{8,392},{16,400},{24,408},{32,416},{40,424},{48,432},{56,4... | collective-permute-start | bytes 245768 | tf_op jit(solution)/shard_map/ppermute | solution.py:491
  88.2 1.3 %shard_map.127 = (f32[2,8,320]{2,1,0:T(8,128)S(1)}, f32[2,320,128]{2,1,0:T(8,128)S(1)}, f32[8,128]{1,0:T(8,128)S(1)}) custom-call(f32[2,8,128]{2,1,0:T(8,128)S(1)} %broadcast_in_dim.35.upper, f32[328,128]{1,0:T(8,128)S(1)} %shard_map.125.own, f32[328,128]{1,0:T(8,128)S(1)} %collective-permute-done.5.got, f32[2,3,80,128]{3,2,1,0:T(8,128)S(1)} %get-tuple-element.56.place, ...), custom_call_target="tpu_custom_call" | custom-call | bytes 1048576 | tf_op jit(solution)/shard_map/pallas_call | solution.py:405
  89.5 2.8 %collective-permute-done.6.got = f32[160,128]{1,0:T(8,128)S(1)} collective-permute-done((f32[160,128]{1,0:T(8,128)S(1)}, f32[160,128]{1,0:T(8,128)S(1)}, u32[]{:S(2)}, u32[]{:S(2)}) %collective-permute-start.6) | collective-permute-done | bytes 81952 | tf_op jit(solution)/shard_map/ppermute | solution.py:491
  92.9 1.3 %shard_map.129 = f32[8,2,320]{2,1,0:T(2,128)} custom-call(f32[8,128]{1,0:T(8,128)S(1)} %broadcast_in_dim.34.upper, f32[8,128]{1,0:T(8,128)S(1)} %get-tuple-element.60.swap, f32[160,128]{1,0:T(8,128)S(1)} %shard_map.128.own, f32[160,128]{1,0:T(8,128)S(1)} %collective-permute-done.6.got, f32[2,8,320]{2,1,0:T(8,128)S(1)} %get-tuple-element.61.fixed, ...), custom_call_target="tpu_custom_call" | custom-call | bytes 1048576 | tf_op jit(solution)/shard_map/pallas_call | solution.py:405
  (36 shorter events, 5.3 us)
Async XLA Ops:
  0.0 0.9 copy-start.1
  0.9 0.9 copy-start.3
  1.8 0.9 copy-start.5
  2.7 0.9 copy-start.11
  3.5 0.7 copy-start.12
  4.3 0.7 copy-start.14
  4.9 11.8 %copy-start.2 = (f32[1,1,2,80,80]{4,3,2,1,0:T(8,128)S(1)}, f32[1,1,2,80,80]{4,3,2,1,0:T(8,128)}, u32[]{:S(2)}) copy-start(f32[1,1,2,80,80]{4,3,2,1,0:T(8,128)} %up_hbm.3) | copy-start | bytes 153604
  4.9 11.8 %copy-start.4 = (bf16[320,80]{1,0:T(8,128)(2,1)S(1)}, bf16[320,80]{1,0:T(8,128)(2,1)}, u32[]{:S(2)}) copy-start(bf16[320,80]{1,0:T(8,128)(2,1)} %constant.21.clone.pw) | copy-start | bytes 153604
  4.9 11.8 %copy-start.6 = (bf16[320,80]{1,0:T(8,128)(2,1)S(1)}, bf16[320,80]{1,0:T(8,128)(2,1)}, u32[]{:S(2)}) copy-start(bf16[320,80]{1,0:T(8,128)(2,1)} %constant.22.clone.pe) | copy-start | bytes 153604
  5.0 11.8 %copy-start.7 = (f32[1,1,2,80,80]{4,3,2,1,0:T(8,128)S(1)}, f32[1,1,2,80,80]{4,3,2,1,0:T(8,128)}, u32[]{:S(2)}) copy-start(f32[1,1,2,80,80]{4,3,2,1,0:T(8,128)} %low_hbm.1) | copy-start | bytes 153604
  5.0 11.8 %copy-start.13 = (f32[1,1,8,2,320]{4,3,2,1,0:T(2,128)S(1)}, f32[1,1,8,2,320]{4,3,2,1,0:T(2,128)}, u32[]{:S(2)}) copy-start(f32[1,1,8,2,320]{4,3,2,1,0:T(2,128)} %rhs_hbm.1) | copy-start | bytes 61444
  6.4 18.7 %collective-permute-start = (f32[2,8,80]{2,1,0:T(8,128)S(1)}, f32[2,8,80]{2,1,0:T(8,128)S(1)}, u32[]{:S(2)}, u32[]{:S(2)}) collective-permute-start(f32[2,8,80]{2,1,0:T(8,128)S(1)} %get-tuple-element.41), channel_id=1, source_target_pairs={{0,1},{1,2},{2,3},{3,4},{4,5},{5,6},{6,7},{7,0},{8,9},{9,10},{10,1... | collective-permute-start | bytes 15368 | tf_op jit(solution)/shard_map/ppermute | solution.py:446
  10.7 14.4 %collective-permute-start.1 = (f32[2,8,80]{2,1,0:T(8,128)S(1)}, f32[2,8,80]{2,1,0:T(8,128)S(1)}, u32[]{:S(2)}, u32[]{:S(2)}) collective-permute-start(f32[2,8,80]{2,1,0:T(8,128)S(1)} %get-tuple-element.42), channel_id=1, source_target_pairs={{1,0},{2,1},{3,2},{4,3},{5,4},{6,5},{7,6},{0,7},{9,8},{10,9},{11,1... | collective-permute-start | bytes 15368 | tf_op jit(solution)/shard_map/ppermute | solution.py:447
  14.8 10.3 %collective-permute-start.2 = (f32[2,8,80]{2,1,0:T(8,128)S(1)}, f32[2,8,80]{2,1,0:T(8,128)S(1)}, u32[]{:S(2)}, u32[]{:S(2)}) collective-permute-start(f32[2,8,80]{2,1,0:T(8,128)S(1)} %get-tuple-element.43), channel_id=1, source_target_pairs={{8,0},{16,8},{24,16},{32,24},{40,32},{48,40},{56,48},{64,56},{72,6... | collective-permute-start | bytes 15368 | tf_op jit(solution)/shard_map/ppermute | solution.py:448
  16.8 1.2 %copy-start = (f32[1,1,2,320,320]{4,3,2,1,0:T(8,128)S(1)}, f32[1,1,2,320,320]{4,3,2,1,0:T(8,128)}, u32[]{:S(2)}) copy-start(f32[1,1,2,320,320]{4,3,2,1,0:T(8,128)} %inv_hbm.1) | copy-start | bytes 2457604
  18.0 0.9 copy-start.8
  18.9 0.9 copy-start.9
  19.7 0.9 copy-start.10
  25.5 3.4 %collective-permute-start.3 = (f32[328,128]{1,0:T(8,128)S(1)}, f32[328,128]{1,0:T(8,128)S(1)}, u32[]{:S(2)}, u32[]{:S(2)}) collective-permute-start(f32[328,128]{1,0:T(8,128)S(1)} %shard_map.120.own), channel_id=1, source_target_pairs={{0,8},{8,0},{16,24},{24,16},{32,40},{40,32},{48,56},{56,48},{64,72... | collective-permute-start | bytes 503816 | tf_op jit(solution)/shard_map/ppermute | solution.py:468
  31.0 27.8 %all-to-all-start = ((f32[4,328,128]{2,1,0:T(8,128)}), f32[4,328,128]{2,1,0:T(8,128)S(1)}, u32[]{:S(2)}, u32[]{:S(2)}) async-start(f32[4,328,128]{2,1,0:T(8,128)} %broadcast_in_dim.40), calls=%async_computation | async-start | bytes 1343488 | tf_op jit(solution)/shard_map/all_to_all | solution.py:475
  60.1 8.1 %collective-permute-start.4 = (f32[328,128]{1,0:T(8,128)S(1)}, f32[328,128]{1,0:T(8,128)S(1)}, u32[]{:S(2)}, u32[]{:S(2)}) collective-permute-start(f32[328,128]{1,0:T(8,128)S(1)} %get-tuple-element.44.own), channel_id=1, source_target_pairs={{0,64},{8,72},{16,80},{24,88},{32,96},{40,104},{48,112},{56,120},{... | collective-permute-start | bytes 503816 | tf_op jit(solution)/shard_map/ppermute | solution.py:468
  69.4 8.8 %collective-permute-start.5 = (f32[328,128]{1,0:T(8,128)S(1)}, f32[328,128]{1,0:T(8,128)S(1)}, u32[]{:S(2)}, u32[]{:S(2)}) collective-permute-start(f32[328,128]{1,0:T(8,128)S(1)} %shard_map.125.own), channel_id=1, source_target_pairs={{0,128},{8,136},{16,144},{24,152},{32,160},{40,168},{48,176},{56,1... | collective-permute-start | bytes 503816 | tf_op jit(solution)/shard_map/ppermute | solution.py:468
  79.5 12.7 %collective-permute-start.6 = (f32[160,128]{1,0:T(8,128)S(1)}, f32[160,128]{1,0:T(8,128)S(1)}, u32[]{:S(2)}, u32[]{:S(2)}) collective-permute-start(f32[160,128]{1,0:T(8,128)S(1)} %shard_map.128.own), channel_id=1, source_target_pairs={{0,384},{8,392},{16,400},{24,408},{32,416},{40,424},{48,432},{56,4... | collective-permute-start | bytes 245768 | tf_op jit(solution)/shard_map/ppermute | solution.py:491

commit v3 on v2

v3 whole, which is shorter than its diff:
```python
import functools

import jax
import jax.numpy as jnp
from jax import lax
from jax.experimental import pallas as pl
from jax.experimental.pallas import tpu as pltpu
from jax.sharding import PartitionSpec as P

NVAR = 5
NB = 4
FACE = 80
DOF = 320
LANES = 128
VEC = FACE
REST = FACE + 8
HALF = LANES - REST
BF16 = jnp.bfloat16
F32 = jnp.float32
NN = (((1,), (0,)), ((), ()))
NT = (((1,), (1,)), ((), ()))


def split(x):
    hi = x.astype(BF16)
    return hi, (x - hi.astype(F32)).astype(BF16)


def dot(a, b, dims=NN):
    ah, al = split(a)
    bh, bl = split(b)
    one = functools.partial(lax.dot_general, dimension_numbers=dims, preferred_element_type=F32)
    return one(ah, bh) + (one(ah, bl) + one(al, bh))


def pick(x, onehot, dims=NN):
    hi = x.astype(BF16).astype(F32)
    mid = (x - hi).astype(BF16).astype(F32)
    low = x - hi - mid
    rows = x.shape[0]
    parts = jnp.concatenate([hi, mid, low], axis=0).astype(BF16)
    made = lax.dot_general(parts, onehot, dimension_numbers=dims, preferred_element_type=F32)
    return made[:rows] + made[rows : 2 * rows] + made[2 * rows :]


def stream_pick(j, width=FACE):
    d = lax.broadcasted_iota(jnp.int32, (DOF, width), 0)
    f = lax.broadcasted_iota(jnp.int32, (DOF, width), 1)
    step = NB * NB
    return ((d == (f // step) * (NB * step) + j * step + f % step) & (f < FACE)).astype(F32).astype(BF16)


def span_pick(j, width=FACE):
    d = lax.broadcasted_iota(jnp.int32, (DOF, width), 0)
    f = lax.broadcasted_iota(jnp.int32, (DOF, width), 1)
    return ((d == (f // NB) * (NB * NB) + j * NB + f % NB) & (f < FACE)).astype(F32).astype(BF16)


def stream_rows(x, j):
    step = NB * NB
    return jnp.concatenate(
        [x[(v * NB + j) * step : (v * NB + j + 1) * step] for v in range(NVAR)], axis=0
    )


def place_rows(x, j):
    step = NB * NB
    zeros = jnp.zeros((step, x.shape[1]), x.dtype)
    parts = []
    for v in range(NVAR):
        for a in range(NB):
            parts.append(x[v * step : (v + 1) * step] if a == j else zeros)
    return jnp.concatenate(parts, axis=0)


def lane_of(shape):
    return lax.broadcasted_iota(jnp.int32, shape, 1)


def pack(ab, be, d):
    lane = lane_of(ab.shape)
    left = jnp.where(lane < REST, ab, pltpu.roll(d, REST, 1))
    right = jnp.where(lane < REST, be, pltpu.roll(d, REST - HALF, 1))
    return left, right


def unpack_d(left, right):
    lane = lane_of(left.shape)
    return jnp.where(
        lane < HALF, pltpu.roll(left, LANES - REST, 1), pltpu.roll(right, LANES - REST + HALF, 1)
    )


def tall(x):
    return jnp.concatenate([x, jnp.zeros((LANES - FACE, x.shape[1]), x.dtype)], axis=0)


def widen(x):
    return jnp.concatenate([x, jnp.zeros((x.shape[0], LANES - x.shape[1]), x.dtype)], axis=1)


def side(x):
    x = widen(x)
    before = jnp.zeros((VEC, LANES), x.dtype)
    after = jnp.zeros((LANES - REST, LANES), x.dtype)
    return jnp.concatenate([before, x, after], axis=0)


def vec_only(x):
    lane = lane_of(x.shape)
    return jnp.where((lane >= VEC) & (lane < REST), x, 0.0)


class Segment:
    def __init__(self, left, right, swap):
        self.left, self.right, self.swap = left, right, swap

    @staticmethod
    def of(ref):
        left = [ref[2 * p * FACE : (2 * p + 1) * FACE] for p in range(2)]
        right = [ref[(2 * p + 1) * FACE : (2 * p + 2) * FACE] for p in range(2)]
        return Segment(left, right, ref[4 * FACE : 4 * FACE + 8])

    def write(self, ref):
        for p in range(2):
            ref[2 * p * FACE : (2 * p + 1) * FACE] = self.left[p]
            ref[(2 * p + 1) * FACE : (2 * p + 2) * FACE] = self.right[p]
        ref[4 * FACE : 4 * FACE + 8] = self.swap

    def top(self, ref):
        for p in range(2):
            left, right = self.left[p], self.right[p]
            lane = lane_of(left.shape)
            tile = jnp.where(lane < VEC, unpack_d(left, right), left)
            tile = jnp.where(lane < REST, tile, pltpu.roll(right, 8, 1))
            ref[p * FACE : (p + 1) * FACE] = jnp.where(lane < REST + 8, tile, self.swap[:1])


def tails_of(ref):
    return [ref[ROWS + p * FACE : ROWS + (p + 1) * FACE] for p in range(2)]


def write_tails(ref, tails):
    for p in range(2):
        ref[ROWS + p * FACE : ROWS + (p + 1) * FACE] = tails[p]


def lagged_left(seg, tails, after):
    return [seg.left[p] - vec_only(dot(tails[p], tall(behind(seg.swap, after, p)))) for p in range(2)]


def behind(swap, pair, p):
    return jnp.where(swap[:1] > 0.5, pair[1 - p], pair[p])


def join(first, second):
    lefts, rights = [], []
    for p in range(2):
        left1, right1 = first.left[p], first.right[p]
        left2, right2 = behind(first.swap, second.left, p), behind(first.swap, second.right, p)
        d1, d2 = unpack_d(left1, right1), unpack_d(left2, right2)
        lane = lane_of(left1.shape)
        through = dot(jnp.concatenate([left2, d2], axis=0), tall(left1))
        ab = through[:FACE] + vec_only(left2)
        back = through[FACE:] + vec_only(right2)
        both = dot(right1, tall(jnp.concatenate([right2, back], axis=1)))
        be = jnp.where(lane < VEC, both[:, :LANES], right1 + both[:, LANES:])
        left, right = pack(ab, be, d1 + both[:, LANES:])
        lefts.append(left)
        rights.append(right)
    return Segment(lefts, rights, jnp.abs(first.swap - second.swap))


def ordered(upper, own, got):
    up = upper[:1] > 0.5

    def pair(a, b):
        return jnp.where(up, a, b)

    def seg(a, b):
        return Segment(
            [pair(a.left[p], b.left[p]) for p in range(2)],
            [pair(a.right[p], b.right[p]) for p in range(2)],
            pair(a.swap, b.swap),
        )

    return seg(got, own), seg(own, got)


def fetch(pairs, sems):
    copies = [pltpu.make_async_copy(a, b, sems.at[i]) for i, (a, b) in enumerate(pairs)]
    for copy in copies:
        copy.start()
    for copy in copies:
        copy.wait()


def columns_of(rows):
    before = jnp.zeros((VEC, DOF), F32)
    after = jnp.zeros((LANES - REST, DOF), F32)
    return jnp.concatenate([before, rows, after], axis=0).T


def make_maps(inv, low, up, rhs, coupled, flag, own):
    tables = jnp.concatenate([span_pick(0, LANES), span_pick(3, LANES), stream_pick(3, LANES)], axis=1)
    lane = lane_of((FACE, LANES))
    made, corners = [], []
    for n in range(2):
        m, u = inv[0, 0, n], up[0, 0, n]
        both = jnp.concatenate([stream_rows(m, 3), dot(u, stream_rows(m, 0))], axis=0)
        z = dot(both, widen(place_rows(low[0, 0, n], 0)) + columns_of(rhs[0, 0, :, n, :]))
        cut = pick(both, tables)
        for i in range(2):
            at = LONG + (2 * n + i) * 2 * FACE
            own[at : at + 2 * FACE] = cut[:, i * LANES : (i + 1) * LANES]
        corners.append(cut[:FACE, 2 * LANES :])
        ahead, down = z[:FACE], z[FACE:]
        made.append(
            pack(
                jnp.where(lane < VEC, -ahead, ahead),
                jnp.where(lane < VEC, -cut[FACE:, 2 * LANES :], down),
                -down,
            )
        )
    Segment(
        [behind(flag, [made[0][0], made[1][0]], p) for p in range(2)],
        [behind(flag, [made[0][1], made[1][1]], p) for p in range(2)],
        flag,
    ).write(own)
    write_tails(own, [behind(flag, corners, p) + side(coupled[p]).T[:FACE] for p in range(2)])


def flag_of(which):
    return jnp.full((8, LANES), which[0, 0, 0].astype(F32), F32)


def faces_kernel(
    guess_hbm, up_hbm, map_hbm, place, west, east, lag, swap, upper, guess, up, which, sems
):
    copies = [
        pltpu.make_async_copy(a, b, sems.at[i])
        for i, (a, b) in enumerate([(guess_hbm, guess), (up_hbm, up), (map_hbm, which)])
    ]
    for copy in copies:
        copy.start()
    for level in range(LEVELS):
        bit = (place[0] >> level) & 1
        upper[level] = jnp.full((8, LANES), bit.astype(F32), F32)
    tables = jnp.concatenate([stream_pick(0, LANES), span_pick(0, LANES), span_pick(3, LANES)], axis=1)
    for copy in copies:
        copy.wait()
    both = pick(jnp.concatenate([guess[0, 0, :, n, :] for n in range(2)], axis=0), tables)
    flag = flag_of(which)
    swap[...] = flag
    swapped = flag[:, :FACE] > 0.5
    made = []
    for n in range(2):
        mine = both[8 * n : 8 * n + 8]
        west[n] = mine[:, LANES : LANES + FACE]
        east[n] = mine[:, 2 * LANES : 2 * LANES + FACE]
        made.append(dot(mine[:, :FACE], up[0, 0, n], NT))
    for p in range(2):
        lag[p] = jnp.where(swapped, made[1 - p], made[p])


def maps_kernel(inv_hbm, low_hbm, up_hbm, rhs_hbm, ahead, swap, own, inv, low, up, rhs, sems):
    fetch([(inv_hbm, inv), (low_hbm, low), (up_hbm, up), (rhs_hbm, rhs)], sems)
    make_maps(inv, low, up, rhs, ahead, swap[...], own)


def vectors_kernel(maps, west, east, from_west, from_east, relayed, own, terms):
    b, e = [], []
    for n in range(2):
        from_w = dot(from_west[n], west[0, 0, n], NT)
        from_e = dot(from_east[n], east[0, 0, n], NT)
        terms[0, 8 * n : 8 * n + 8] = from_w
        terms[1, 8 * n : 8 * n + 8] = from_e
        far = jnp.concatenate([side(from_w), side(from_e)], axis=1)
        at = LONG + 2 * n * 2 * FACE
        cuts = jnp.concatenate([maps[at + i * 2 * FACE : at + (i + 1) * 2 * FACE] for i in range(2)], axis=1)
        both = dot(cuts, far, NT)
        b.append(both[:FACE])
        e.append(both[FACE:])
    seg = Segment.of(maps)
    Segment(
        [seg.left[p] - behind(seg.swap, b, p) for p in range(2)],
        [seg.right[p] - behind(seg.swap, e, p) for p in range(2)],
        seg.swap,
    ).write(own)
    tails = tails_of(maps)
    write_tails(own, [tails[p] + pltpu.roll(side(relayed[p]).T[:FACE], 8, 1) for p in range(2)])


def rest_kernel(inv_hbm, low_hbm, rhs_hbm, terms, zin, zout, base, inv, low, rhs, sems):
    fetch([(inv_hbm, inv), (low_hbm, low), (rhs_hbm, rhs)], sems)
    pout = stream_pick(3, LANES)
    lane = lane_of((DOF, LANES))
    halo = pick(terms[0], span_pick(0), NT) + pick(terms[1], span_pick(3), NT)
    for n in range(2):
        m = inv[0, 0, n]
        h = rhs[0, 0, :, n, :] - halo[8 * n : 8 * n + 8]
        z = dot(m, widen(place_rows(low[0, 0, n], 0)) + columns_of(h))
        zout[n] = pick(m, pout)
        zin[n] = jnp.where(lane < VEC, z, 0.0)
        base[n] = vec_only(z)


def pair_kernel(level, form, upper, own, got, out):
    both = join(*ordered(upper[level], Segment.of(own), Segment.of(got)))
    if form == "top":
        both.top(out)
    else:
        both.write(out)


def first_pair_kernel(upper, own, got, out, lefts):
    first, second = ordered(upper[0], Segment.of(own), Segment.of(got))
    up = upper[0][:1] > 0.5
    mine, other = tails_of(own), tails_of(got)
    tails1 = [jnp.where(up, other[p], mine[p]) for p in range(2)]
    tails2 = [jnp.where(up, mine[p], other[p]) for p in range(2)]
    first = Segment(lagged_left(first, tails1, tails2), first.right, first.swap)
    both = join(first, second)
    lane = lane_of((FACE, LANES))
    tails = [jnp.where(lane < VEC, behind(first.swap, tails2, p), tails1[p]) for p in range(2)]
    for p in range(2):
        lefts[p] = first.left[p]
    both.write(out)
    write_tails(out, tails)


def four_kernel(got, out, halves, parts):
    tails = [tails_of(got.at[i]) for i in range(4)]
    last = [pltpu.roll(tails[0][p], LANES - 8, 1) for p in range(2)]
    segs = []
    for i in range(4):
        seg = Segment.of(got.at[i])
        seg = Segment(lagged_left(seg, tails[i], tails[i + 1] if i < 3 else last), seg.right, seg.swap)
        seg.write(parts.at[i])
        segs.append(seg)
    both = [join(segs[2 * i], segs[2 * i + 1]) for i in range(2)]
    join(*both).write(out)
    for i in range(2):
        both[i].write(halves.at[i])


def start_place():
    eye = (lax.broadcasted_iota(jnp.int32, (FACE, LANES), 0) == lane_of((FACE, LANES))).astype(F32)
    zero = jnp.zeros((FACE, LANES), F32)
    return [[eye, zero, eye] for _ in range(2)]


def widen_place(place, upper, own, got):
    lane = lane_of((FACE, LANES))
    keep = lane < REST
    up = upper[:1] > 0.5
    made = []
    for p in range(2):
        near = [behind(got.swap, [place[0][i], place[1][i]], p) for i in range(3)]
        sib = tall(got.left[p])
        moved = dot(jnp.concatenate([near[0], near[1]], axis=0), sib)
        above = [
            jnp.where(keep, moved[:FACE], 0.0) + vec_only(near[0]),
            jnp.where(keep, moved[FACE:], 0.0) + vec_only(near[1]),
            near[2],
        ]
        left2, right2 = behind(own.swap, got.left, p), behind(own.swap, got.right, p)
        back = dot(unpack_d(left2, right2), tall(own.left[p])) + vec_only(right2)
        turned = dot(place[p][2], tall(jnp.concatenate([back, right2], axis=1)))
        below = [
            place[p][0],
            place[p][1] + jnp.where(keep, turned[:, :LANES], 0.0),
            jnp.where(lane < VEC, turned[:, LANES:], 0.0),
        ]
        made.append([jnp.where(up, above[i], below[i]) for i in range(3)])
    return made


def read_place(ref):
    return [[ref[p, i] for i in range(3)] for p in range(2)]


def write_place(ref, place):
    for p in range(2):
        for i in range(3):
            ref[p, i] = place[p][i]


def place_kernel(level, upper, own, got, place, swap, out, swap_out):
    mine, other = Segment.of(own), Segment.of(got)
    write_place(out, widen_place(read_place(place), upper[level], mine, other))
    swap_out[...] = jnp.abs(swap[...] - jnp.where(upper[level] > 0.5, other.swap, 0.0))


def four_place_kernel(at, upper, one, one_got, lefts, got, halves, out, swap_out):
    mine, other = Segment.of(one), Segment.of(one_got)
    up = upper[0][:1] > 0.5
    mine.left = [jnp.where(up, mine.left[p], lefts[p]) for p in range(2)]
    other.left = [jnp.where(up, lefts[p], other.left[p]) for p in range(2)]
    made = widen_place(start_place(), upper[0], mine, other)
    x = jnp.abs(mine.swap - jnp.where(upper[0] > 0.5, other.swap, 0.0))
    j = (at[0] >> 1) & 3
    half = j >> 1
    mine, other = Segment.of(got.at[j]), Segment.of(got.at[j ^ 1])
    made = widen_place(made, upper[1], mine, other)
    x = jnp.abs(x - jnp.where(upper[1] > 0.5, other.swap, 0.0))
    mine, other = Segment.of(halves.at[half]), Segment.of(halves.at[1 - half])
    write_place(out, widen_place(made, upper[2], mine, other))
    swap_out[...] = jnp.abs(x - jnp.where(upper[2] > 0.5, other.swap, 0.0))


def answer_kernel(upper, own, got, place, swap, zin, zout, base, fixed, free, turn):
    mine, other = Segment.of(own), Segment.of(got)
    made = widen_place(read_place(place), upper[4], mine, other)
    x = jnp.abs(swap[...] - jnp.where(upper[4] > 0.5, other.swap, 0.0))
    turn[...] = x
    up = upper[5][:1] > 0.5
    for n in range(2):
        p0, q0, r0 = [behind(x, [made[0][i], made[1][i]], n) for i in range(3)]
        t = jnp.where(up, p0, vec_only(p0))
        c = jnp.where(up, q0, jnp.where(lane_of(r0.shape) < VEC, r0, 0.0) + vec_only(q0))
        f = dot(jnp.concatenate([zin[n], zout[n]], axis=1), jnp.concatenate([tall(t), tall(c)], axis=0))
        free[n] = f
        fixed[n] = (base[n] - f).T[VEC:REST]


def last_kernel(upper, swap, own, got, fixed, free, out):
    up = upper[5][:1] > 0.5
    mine = [own[p * FACE : (p + 1) * FACE] for p in range(2)]
    far = [got[p * FACE : (p + 1) * FACE] for p in range(2)]
    own_swap = jnp.broadcast_to(mine[0][:1, LANES - 1 :], (1, LANES))
    far_swap = jnp.broadcast_to(far[0][:1, LANES - 1 :], (1, LANES))
    unknown = []
    for p in range(2):
        above = behind(far_swap, far, p)
        sib = behind(own_swap, far, p)
        below = dot(sib, tall(vec_only(mine[p]))) + pltpu.roll(sib, LANES - 8, 1)
        unknown.append(jnp.where(up, above, below).T[VEC:REST])
    for n in range(2):
        x = widen(behind(swap[...][:, :FACE], unknown, n))
        out[:, n, :] = fixed[n] - dot(x, free[n], NT)


HBM = pl.BlockSpec(memory_space=pltpu.HBM)
VMEM = pl.BlockSpec(memory_space=pltpu.VMEM)
SMEM = pl.BlockSpec(memory_space=pltpu.SMEM)


def call(kernel, out_shape, *operands, hbm=(), smem=(), scratch=(), flops=0):
    specs = [HBM if i in hbm else SMEM if i in smem else VMEM for i in range(len(operands))]
    several = isinstance(out_shape, tuple)
    operands = [
        pltpu.with_memory_space_constraint(x, pltpu.HBM) if i in hbm else x for i, x in enumerate(operands)
    ]
    return pl.pallas_call(
        kernel,
        out_shape=out_shape,
        in_specs=specs,
        out_specs=tuple(VMEM for _ in out_shape) if several else VMEM,
        scratch_shapes=list(scratch),
        cost_estimate=pl.CostEstimate(flops=flops, bytes_accessed=1 << 20, transcendentals=0),
        compiler_params=pltpu.CompilerParams(vmem_limit_bytes=24 * 1024 * 1024),
    )(*operands)


def f32(*shape):
    return jax.ShapeDtypeStruct(shape, F32)


LEVELS = 6
ROWS = 4 * FACE + 8
LONG = ROWS + 2 * FACE
TOP = (6, 7, 4, 5, 2, 3, 0, 1)


def per_device(
    rhs_field, guess, inverse_diag, lower_block, upper_block, west_block, east_block, inflow_map
):
    wide = lax.axis_size("span")
    layers = lax.axis_size("stream")
    place = lax.axis_index("stream").astype(jnp.int32).reshape(1)
    dma = pltpu.SemaphoreType.DMA

    def room(*arrays):
        held = [
            pltpu.SMEM(a.shape, a.dtype) if a.dtype == jnp.int32 else pltpu.VMEM(a.shape, F32) for a in arrays
        ]
        return (*held, dma((len(arrays),)))

    face = f32(2, 8, FACE)
    args = (guess, upper_block, inflow_map)
    west_face, east_face, ahead, swap, upper = call(
        faces_kernel, (face, face, face, f32(8, LANES), f32(LEVELS, 8, LANES)), *args, place,
        hbm=range(3), smem=(3,), scratch=room(*args),
    )
    ring = [(i, (i + 1) % wide) for i in range(wide)]
    from_west = lax.ppermute(east_face, "span", ring)
    from_east = lax.ppermute(west_face, "span", [(b, a) for a, b in ring])
    relayed = lax.ppermute(ahead, "stream", [(i + 8, i) for i in range(0, layers - 8, 8)])
    args = (inverse_diag, lower_block, upper_block, rhs_field)
    maps = call(
        maps_kernel, f32(LONG + 8 * FACE, LANES), *args, ahead, swap, hbm=range(4), scratch=room(*args)
    )
    own, terms = call(
        vectors_kernel, (f32(LONG, LANES), f32(2, 16, FACE)),
        maps, west_block, east_block, from_west, from_east, relayed,
    )

    def across(x, distance):
        return lax.ppermute(x, "stream", [(i, i ^ distance) for i in range(layers)])

    got = across(own, 1)
    pairs, lefts = call(
        first_pair_kernel, (f32(LONG, LANES), f32(2, FACE, LANES)), upper, own, got
    )
    groups = [[8 * g + c + 2 * j for j in range(4)] for g in range(layers // 8) for c in range(2)]
    four = lax.all_gather(pairs, "stream", axis_index_groups=groups)
    eight, halves, parts = call(
        four_kernel, (f32(ROWS, LANES), f32(2, ROWS, LANES), f32(4, ROWS, LANES)), four
    )
    here = (f32(2, 3, FACE, LANES), f32(8, LANES))
    got8 = across(eight, 8)
    spot, turn = call(four_place_kernel, here, place, upper, own, got, lefts, parts, halves, smem=(0,))
    got8, spot, turn = lax.optimization_barrier((got8, spot, turn))
    sixteen = call(functools.partial(pair_kernel, 3, ""), f32(ROWS, LANES), upper, eight, got8)
    got16 = across(sixteen, 16)
    args = (inverse_diag, lower_block, rhs_field)
    terms, sixteen = lax.optimization_barrier((terms, sixteen))
    zin, zout, base = call(
        rest_kernel, tuple(f32(2, DOF, LANES) for _ in range(3)), *args, terms,
        hbm=range(3), scratch=room(*args),
    )
    spot, turn = call(functools.partial(place_kernel, 3), here, upper, eight, got8, spot, turn)
    got16, spot, turn, zin, zout, base = lax.optimization_barrier((got16, spot, turn, zin, zout, base))
    half = call(functools.partial(pair_kernel, 4, "top"), f32(2 * FACE, LANES), upper, sixteen, got16)
    got32 = lax.ppermute(half, "stream", [(i, TOP[i // 8] * 8 + i % 8) for i in range(layers)])
    fixed, free, turn = call(
        answer_kernel, (f32(2, 8, DOF), f32(2, DOF, LANES), f32(8, LANES)),
        upper, sixteen, got16, spot, turn, zin, zout, base,
    )
    out = call(last_kernel, f32(8, 2, DOF), upper, turn, half, got32, fixed, free)
    return out[None, None]


def solution(mesh):
    in_specs = (
        P("stream", "span", None, None, None),
        P("stream", "span", None, None, None),
        P("stream", "span", None, None, None),
        P("stream", "span", None, None, None),
        P("stream", "span", None, None, None),
        P("stream", "span", None, None, None),
        P("stream", "span", None, None, None),
        P("stream", "span", None),
    )
    out_specs = P("stream", "span", None, None, None)
    return jax.shard_map(
        per_device, mesh=mesh, in_specs=in_specs, out_specs=out_specs, check_vma=False
    )
```

time: 94.9 us -> 77.6 us (0.82)
  the two profiles are of different devices: /device:TPU:144 before, /device:TPU:1 now
where the time goes in v3:
time: 77.6 us; the launch traced here: 76.3 us
  starting transfers between devices  30.8 us (40%)
  blocking collectives  20.2 us (26%)
  Pallas kernels  15.3 us (20%)
  waiting for transfers between devices  9.71 us (13%)
    all_gather x1, blocking collectives, per_device(): four = lax.all_gather(pairs, 'stream', axis_index_groups=groups)  20.2 us
    ppermute x3, starting transfers between devices, across(): return lax.ppermute(x, 'stream', [(i, i ^ distance) for i in range(layers)])  16.9 us
    pallas_call x12, Pallas kernels, call(): pl.pallas_call(kernel, out_shape=out_shape, in_specs=specs, out_specs=tup...  15.3 us
    ppermute x3, waiting for transfers between devices, across(): return lax.ppermute(x, 'stream', [(i, i ^ distance) for i in range(layers)])  7.81 us
    ppermute x1, starting transfers between devices, per_device(): from_west = lax.ppermute(east_face, 'span', ring)  4.83 us
    ppermute x1, starting transfers between devices, per_device(): lax.ppermute(half, 'stream', [(i, TOP[i // 8] * 8 + i % 8) for i in range...  4.35 us
    ppermute x1, starting transfers between devices, per_device(): from_east = lax.ppermute(west_face, 'span', [(b, a) for a, b in ring])  4.12 us
    ppermute x1, waiting for transfers between devices, per_device(): lax.ppermute(half, 'stream', [(i, TOP[i // 8] * 8 + i % 8) for i in range...  1.89 us
  transfers between devices with their start and end apart: 7, of which 4 were waited for; matrix products, arithmetic and copies ran while one was open for 0% of the time, Pallas kernels for 11%

profile of v3, /device:TPU:1, one launch (start us, length us, event | category | flops | bytes accessed | tf_op | source)
XLA Modules:
  0.0 76.3 jit_solution(3148880140912829344)
XLA Ops:
  0.0 1.3 %shard_map.82 = (f32[2,8,80]{2,1,0:T(8,128)S(1)}, f32[2,8,80]{2,1,0:T(8,128)S(1)}, f32[2,8,80]{2,1,0:T(8,128)S(1)}, f32[8,128]{1,0:T(8,128)S(1)}, f32[6,8,128]{2,1,0:T(8,128)S(1)}) custom-call(f32[1,1,8,2,320]{4,3,2,1,0:T(2,128)} %guess_hbm.1, f32[1,1,2,80,80]{4,3,2,1,0:T(8,128)} %up_hbm.3, s32[1,1,2]{2,1,0:T(1,128)} %map_hbm.1, s32[1]{0:T(128)} %bitcast.place.at), custom_call_target="tpu_custom_call" | custom-call | bytes 1048576 | tf_op jit(solution)/shard_map/pallas_call | solution.py:455
  1.3 4.8 %collective-permute-start = (f32[2,8,80]{2,1,0:T(8,128)S(1)}, f32[2,8,80]{2,1,0:T(8,128)S(1)}, u32[]{:S(2)}, u32[]{:S(2)}) collective-permute-start(f32[2,8,80]{2,1,0:T(8,128)S(1)} %get-tuple-element.41), channel_id=1, source_target_pairs={{0,1},{1,2},{2,3},{3,4},{4,5},{5,6},{6,7},{7,0},{8,9},{9,10},{10,1... | collective-permute-start | bytes 15368 | tf_op jit(solution)/shard_map/ppermute | solution.py:497
  6.1 4.1 %collective-permute-start.1 = (f32[2,8,80]{2,1,0:T(8,128)S(1)}, f32[2,8,80]{2,1,0:T(8,128)S(1)}, u32[]{:S(2)}, u32[]{:S(2)}) collective-permute-start(f32[2,8,80]{2,1,0:T(8,128)S(1)} %get-tuple-element.42), channel_id=1, source_target_pairs={{1,0},{2,1},{3,2},{4,3},{5,4},{6,5},{7,6},{0,7},{9,8},{10,9},{11,1... | collective-permute-start | bytes 15368 | tf_op jit(solution)/shard_map/ppermute | solution.py:498
  10.2 0.7 collective-permute-start.2
  10.9 0.0 copy-start
  10.9 0.0 copy-start.1
  10.9 2.5 %shard_map.83.maps = f32[1128,128]{1,0:T(8,128)S(1)} custom-call(f32[1,1,2,320,320]{4,3,2,1,0:T(8,128)} %inv_hbm.3, f32[1,1,2,80,80]{4,3,2,1,0:T(8,128)} %low_hbm.3, f32[1,1,2,80,80]{4,3,2,1,0:T(8,128)} %up_hbm.3, f32[1,1,8,2,320]{4,3,2,1,0:T(2,128)} %rhs_hbm.3, f32[2,8,80]{2,1,0:T(8,128)S(1)} %get-tuple-element.39.ahead, f32[8,128]{1,0:T(8,128)S(1)} %get-tuple-element.40.swap), custom_call_target="tpu_custom_call" | custom-call | bytes 1048576 | tf_op jit(solution)/shard_map/pallas_call | solution.py:455
  13.4 0.0 collective-permute-done.from_west
  13.4 0.0 collective-permute-done.1.from_east
  13.4 0.0 collective-permute-done.2.relayed
  13.4 0.0 copy-done
  13.4 0.0 copy-done.1
  13.5 0.7 shard_map.84
  14.2 10.1 %collective-permute-start.3 = (f32[488,128]{1,0:T(8,128)S(1)}, f32[488,128]{1,0:T(8,128)S(1)}, u32[]{:S(2)}, u32[]{:S(2)}) collective-permute-start(f32[488,128]{1,0:T(8,128)S(1)} %get-tuple-element.44.own.one), channel_id=1, source_target_pairs={{0,8},{8,0},{16,24},{24,16},{32,40},{40,32},{48,56},{56,48},{64,72... | collective-permute-start | bytes 749576 | tf_op jit(solution)/shard_map/ppermute | solution.py:510
  24.3 1.1 %collective-permute-done.3.got.one_got = f32[488,128]{1,0:T(8,128)S(1)} collective-permute-done((f32[488,128]{1,0:T(8,128)S(1)}, f32[488,128]{1,0:T(8,128)S(1)}, u32[]{:S(2)}, u32[]{:S(2)}) %collective-permute-start.3) | collective-permute-done | bytes 249888 | tf_op jit(solution)/shard_map/ppermute | solution.py:510
  25.5 0.7 shard_map.85
  26.2 20.2 %all-gather = f32[1952,128]{1,0:T(8,128)S(1)} all-gather(f32[488,128]{1,0:T(8,128)S(1)} %get-tuple-element.45), channel_id=2, replica_groups={{0,16,32,48},{8,24,40,56},{64,80,96,112},{72,88,104,120},{128,144,160,1..., dimensions={0}, use_global_device_ids=true | all-gather | bytes 1249280 | tf_op jit(solution)/shard_map/all_gather | solution.py:517
  46.4 1.6 %shard_map.86 = (f32[328,128]{1,0:T(8,128)S(1)}, f32[2,328,128]{2,1,0:T(8,128)S(1)}, f32[4,328,128]{2,1,0:T(8,128)S(1)}) custom-call(f32[4,488,128]{2,1,0:T(8,128)S(1)} %bitcast.3), custom_call_target="tpu_custom_call" | custom-call | bytes 1048576 | tf_op jit(solution)/shard_map/pallas_call | solution.py:455
  48.0 2.8 %collective-permute-start.4 = (f32[328,128]{1,0:T(8,128)S(1)}, f32[328,128]{1,0:T(8,128)S(1)}, u32[]{:S(2)}, u32[]{:S(2)}) collective-permute-start(f32[328,128]{1,0:T(8,128)S(1)} %get-tuple-element.46.own), channel_id=1, source_target_pairs={{0,64},{8,72},{16,80},{24,88},{32,96},{40,104},{48,112},{56,120},{... | collective-permute-start | bytes 503816 | tf_op jit(solution)/shard_map/ppermute | solution.py:510
  50.8 1.9 %shard_map.87 = (f32[2,3,80,128]{3,2,1,0:T(8,128)S(1)}, f32[8,128]{1,0:T(8,128)S(1)}) custom-call(s32[1]{0:T(128)} %bitcast.place.at, f32[6,8,128]{2,1,0:T(8,128)S(1)} %get-tuple-element.38.upper, f32[488,128]{1,0:T(8,128)S(1)} %get-tuple-element.44.own.one, f32[488,128]{1,0:T(8,128)S(1)} %collective-permute-done.3.got.one_got, ...), custom_call_target="tpu_custom_call" | custom-call | bytes 1048576 | tf_op jit(solution)/shard_map/pallas_call | solution.py:455
  52.7 1.9 %collective-permute-done.4.got = f32[328,128]{1,0:T(8,128)S(1)} collective-permute-done((f32[328,128]{1,0:T(8,128)S(1)}, f32[328,128]{1,0:T(8,128)S(1)}, u32[]{:S(2)}, u32[]{:S(2)}) %collective-permute-start.4) | collective-permute-done | bytes 167968 | tf_op jit(solution)/shard_map/ppermute | solution.py:510
  54.6 0.6 shard_map.88.own
  55.2 3.9 %collective-permute-start.5 = (f32[328,128]{1,0:T(8,128)S(1)}, f32[328,128]{1,0:T(8,128)S(1)}, u32[]{:S(2)}, u32[]{:S(2)}) collective-permute-start(f32[328,128]{1,0:T(8,128)S(1)} %shard_map.88.own), channel_id=1, source_target_pairs={{0,128},{8,136},{16,144},{24,152},{32,160},{40,168},{48,176},{56,1... | collective-permute-start | bytes 503816 | tf_op jit(solution)/shard_map/ppermute | solution.py:510
  59.1 2.5 %shard_map.90 = (f32[2,320,128]{2,1,0:T(8,128)S(1)}, f32[2,320,128]{2,1,0:T(8,128)S(1)}, f32[2,320,128]{2,1,0:T(8,128)S(1)}) custom-call(f32[1,1,2,320,320]{4,3,2,1,0:T(8,128)} %inv_hbm.3, f32[1,1,2,80,80]{4,3,2,1,0:T(8,128)} %low_hbm.3, f32[1,1,8,2,320]{4,3,2,1,0:T(2,128)} %rhs_hbm.3, f32[2,16,80]{2,1,0:T(8,128)S(1)} %get-tuple-element.58.terms), custom_call_target="tpu_custom_call" | custom-call | bytes 1048576 | tf_op jit(solution)/shard_map/pallas_call | solution.py:455
  61.6 0.7 shard_map.89
  62.3 4.7 %collective-permute-done.5.got = f32[328,128]{1,0:T(8,128)S(1)} collective-permute-done((f32[328,128]{1,0:T(8,128)S(1)}, f32[328,128]{1,0:T(8,128)S(1)}, u32[]{:S(2)}, u32[]{:S(2)}) %collective-permute-start.5) | collective-permute-done | bytes 167968 | tf_op jit(solution)/shard_map/ppermute | solution.py:510
  67.0 0.7 shard_map.92.own
  67.7 4.4 %collective-permute-start.6 = (f32[160,128]{1,0:T(8,128)S(1)}, f32[160,128]{1,0:T(8,128)S(1)}, u32[]{:S(2)}, u32[]{:S(2)}) collective-permute-start(f32[160,128]{1,0:T(8,128)S(1)} %shard_map.92.own), channel_id=1, source_target_pairs={{0,384},{8,392},{16,400},{24,408},{32,416},{40,424},{48,432},{56,4... | collective-permute-start | bytes 245768 | tf_op jit(solution)/shard_map/ppermute | solution.py:536
  72.0 1.1 %shard_map.91 = (f32[2,8,320]{2,1,0:T(8,128)S(1)}, f32[2,320,128]{2,1,0:T(8,128)S(1)}, f32[8,128]{1,0:T(8,128)S(1)}) custom-call(f32[6,8,128]{2,1,0:T(8,128)S(1)} %get-tuple-element.38.upper, f32[328,128]{1,0:T(8,128)S(1)} %shard_map.88.own, f32[328,128]{1,0:T(8,128)S(1)} %collective-permute-done.5.got, f32[2,3,80,128]{3,2,1,0:T(8,128)S(1)} %get-tuple-element.63.place, ...), custom_call_target="tpu_custom_call" | custom-call | bytes 1048576 | tf_op jit(solution)/shard_map/pallas_call | solution.py:455
  73.2 1.9 %collective-permute-done.6.got = f32[160,128]{1,0:T(8,128)S(1)} collective-permute-done((f32[160,128]{1,0:T(8,128)S(1)}, f32[160,128]{1,0:T(8,128)S(1)}, u32[]{:S(2)}, u32[]{:S(2)}) %collective-permute-start.6) | collective-permute-done | bytes 81952 | tf_op jit(solution)/shard_map/ppermute | solution.py:536
  75.1 1.3 %shard_map.93 = f32[8,2,320]{2,1,0:T(2,128)} custom-call(f32[6,8,128]{2,1,0:T(8,128)S(1)} %get-tuple-element.38.upper, f32[8,128]{1,0:T(8,128)S(1)} %get-tuple-element.68.swap, f32[160,128]{1,0:T(8,128)S(1)} %shard_map.92.own, f32[160,128]{1,0:T(8,128)S(1)} %collective-permute-done.6.got, f32[2,8,320]{2,1,0:T(8,128)S(1)} %get-tuple-element.69.fixed, ...), custom_call_target="tpu_custom_call" | custom-call | bytes 1048576 | tf_op jit(solution)/shard_map/pallas_call | solution.py:455
Async XLA Ops:
  1.3 12.1 %collective-permute-start = (f32[2,8,80]{2,1,0:T(8,128)S(1)}, f32[2,8,80]{2,1,0:T(8,128)S(1)}, u32[]{:S(2)}, u32[]{:S(2)}) collective-permute-start(f32[2,8,80]{2,1,0:T(8,128)S(1)} %get-tuple-element.41), channel_id=1, source_target_pairs={{0,1},{1,2},{2,3},{3,4},{4,5},{5,6},{6,7},{7,0},{8,9},{9,10},{10,1... | collective-permute-start | bytes 15368 | tf_op jit(solution)/shard_map/ppermute | solution.py:497
  6.1 7.3 %collective-permute-start.1 = (f32[2,8,80]{2,1,0:T(8,128)S(1)}, f32[2,8,80]{2,1,0:T(8,128)S(1)}, u32[]{:S(2)}, u32[]{:S(2)}) collective-permute-start(f32[2,8,80]{2,1,0:T(8,128)S(1)} %get-tuple-element.42), channel_id=1, source_target_pairs={{1,0},{2,1},{3,2},{4,3},{5,4},{6,5},{7,6},{0,7},{9,8},{10,9},{11,1... | collective-permute-start | bytes 15368 | tf_op jit(solution)/shard_map/ppermute | solution.py:498
  10.2 3.2 %collective-permute-start.2 = (f32[2,8,80]{2,1,0:T(8,128)S(1)}, f32[2,8,80]{2,1,0:T(8,128)S(1)}, u32[]{:S(2)}, u32[]{:S(2)}) collective-permute-start(f32[2,8,80]{2,1,0:T(8,128)S(1)} %get-tuple-element.39.ahead), channel_id=1, source_target_pairs={{64,0},{128,64},{192,128},{256,192},{320,256},{384,320},{448,384},... | collective-permute-start | bytes 15368 | tf_op jit(solution)/shard_map/ppermute | solution.py:499
  10.9 2.5 %copy-start = (f32[1,1,2,80,80]{4,3,2,1,0:T(8,128)S(1)}, f32[1,1,2,80,80]{4,3,2,1,0:T(8,128)}, u32[]{:S(2)}) copy-start(f32[1,1,2,80,80]{4,3,2,1,0:T(8,128)} %west.1) | copy-start | bytes 153604
  10.9 2.5 %copy-start.1 = (f32[1,1,2,80,80]{4,3,2,1,0:T(8,128)S(1)}, f32[1,1,2,80,80]{4,3,2,1,0:T(8,128)}, u32[]{:S(2)}) copy-start(f32[1,1,2,80,80]{4,3,2,1,0:T(8,128)} %east.1) | copy-start | bytes 153604
  14.2 11.3 %collective-permute-start.3 = (f32[488,128]{1,0:T(8,128)S(1)}, f32[488,128]{1,0:T(8,128)S(1)}, u32[]{:S(2)}, u32[]{:S(2)}) collective-permute-start(f32[488,128]{1,0:T(8,128)S(1)} %get-tuple-element.44.own.one), channel_id=1, source_target_pairs={{0,8},{8,0},{16,24},{24,16},{32,40},{40,32},{48,56},{56,48},{64,72... | collective-permute-start | bytes 749576 | tf_op jit(solution)/shard_map/ppermute | solution.py:510
  48.0 6.6 %collective-permute-start.4 = (f32[328,128]{1,0:T(8,128)S(1)}, f32[328,128]{1,0:T(8,128)S(1)}, u32[]{:S(2)}, u32[]{:S(2)}) collective-permute-start(f32[328,128]{1,0:T(8,128)S(1)} %get-tuple-element.46.own), channel_id=1, source_target_pairs={{0,64},{8,72},{16,80},{24,88},{32,96},{40,104},{48,112},{56,120},{... | collective-permute-start | bytes 503816 | tf_op jit(solution)/shard_map/ppermute | solution.py:510
  55.2 11.8 %collective-permute-start.5 = (f32[328,128]{1,0:T(8,128)S(1)}, f32[328,128]{1,0:T(8,128)S(1)}, u32[]{:S(2)}, u32[]{:S(2)}) collective-permute-start(f32[328,128]{1,0:T(8,128)S(1)} %shard_map.88.own), channel_id=1, source_target_pairs={{0,128},{8,136},{16,144},{24,152},{32,160},{40,168},{48,176},{56,1... | collective-permute-start | bytes 503816 | tf_op jit(solution)/shard_map/ppermute | solution.py:510
  67.7 7.4 %collective-permute-start.6 = (f32[160,128]{1,0:T(8,128)S(1)}, f32[160,128]{1,0:T(8,128)S(1)}, u32[]{:S(2)}, u32[]{:S(2)}) collective-permute-start(f32[160,128]{1,0:T(8,128)S(1)} %shard_map.92.own), channel_id=1, source_target_pairs={{0,384},{8,392},{16,400},{24,408},{32,416},{40,424},{48,432},{56,4... | collective-permute-start | bytes 245768 | tf_op jit(solution)/shard_map/ppermute | solution.py:536

commit v4 on v3

--- a/solution.py
+++ b/solution.py
@@ -235,7 +235,7 @@
 
 
 def faces_kernel(
-    guess_hbm, up_hbm, map_hbm, place, west, east, lag, swap, upper, guess, up, which, sems
+    guess_hbm, up_hbm, map_hbm, place, along, near, far, lag, swap, upper, guess, up, which, sems
 ):
     copies = [
         pltpu.make_async_copy(a, b, sems.at[i])
@@ -246,6 +246,8 @@
     for level in range(LEVELS):
         bit = (place[0] >> level) & 1
         upper[level] = jnp.full((8, LANES), bit.astype(F32), F32)
+    upper[LEVELS] = jnp.full((8, LANES), (along[0] & 1).astype(F32), F32)
+    odd = upper[LEVELS][:, :FACE] > 0.5
     tables = jnp.concatenate([stream_pick(0, LANES), span_pick(0, LANES), span_pick(3, LANES)], axis=1)
     for copy in copies:
         copy.wait()
@@ -256,8 +258,10 @@
     made = []
     for n in range(2):
         mine = both[8 * n : 8 * n + 8]
-        west[n] = mine[:, LANES : LANES + FACE]
-        east[n] = mine[:, 2 * LANES : 2 * LANES + FACE]
+        west = mine[:, LANES : LANES + FACE]
+        east = mine[:, 2 * LANES : 2 * LANES + FACE]
+        near[n] = jnp.where(odd, west, east)
+        far[n] = jnp.where(odd, east, west)
         made.append(dot(mine[:, :FACE], up[0, 0, n], NT))
     for p in range(2):
         lag[p] = jnp.where(swapped, made[1 - p], made[p])
@@ -268,17 +272,18 @@
     make_maps(inv, low, up, rhs, ahead, swap[...], own)
 
 
-def vectors_kernel(maps, west, east, from_west, from_east, relayed, own, terms):
+def vectors_kernel(maps, west, east, upper, from_near, from_far, relayed, own, terms):
+    odd = upper[LEVELS][:, :FACE] > 0.5
     b, e = [], []
     for n in range(2):
-        from_w = dot(from_west[n], west[0, 0, n], NT)
-        from_e = dot(from_east[n], east[0, 0, n], NT)
+        from_w = dot(jnp.where(odd, from_near[n], from_far[n]), west[0, 0, n], NT)
+        from_e = dot(jnp.where(odd, from_far[n], from_near[n]), east[0, 0, n], NT)
         terms[0, 8 * n : 8 * n + 8] = from_w
         terms[1, 8 * n : 8 * n + 8] = from_e
-        far = jnp.concatenate([side(from_w), side(from_e)], axis=1)
+        sides = jnp.concatenate([side(from_w), side(from_e)], axis=1)
         at = LONG + 2 * n * 2 * FACE
         cuts = jnp.concatenate([maps[at + i * 2 * FACE : at + (i + 1) * 2 * FACE] for i in range(2)], axis=1)
-        both = dot(cuts, far, NT)
+        both = dot(cuts, sides, NT)
         b.append(both[:FACE])
         e.append(both[FACE:])
     seg = Segment.of(maps)
@@ -287,8 +292,7 @@
         [seg.right[p] - behind(seg.swap, e, p) for p in range(2)],
         seg.swap,
     ).write(own)
-    tails = tails_of(maps)
-    write_tails(own, [tails[p] + pltpu.roll(side(relayed[p]).T[:FACE], 8, 1) for p in range(2)])
+    write_tails(own, tails_of(maps))
 
 
 def rest_kernel(inv_hbm, low_hbm, rhs_hbm, terms, zin, zout, base, inv, low, rhs, sems):
@@ -313,7 +317,7 @@
         both.write(out)
 
 
-def first_pair_kernel(upper, own, got, out, lefts):
+def first_pair_kernel(upper, own, got, relayed, out, lefts):
     first, second = ordered(upper[0], Segment.of(own), Segment.of(got))
     up = upper[0][:1] > 0.5
     mine, other = tails_of(own), tails_of(got)
@@ -323,18 +327,23 @@
     both = join(first, second)
     lane = lane_of((FACE, LANES))
     tails = [jnp.where(lane < VEC, behind(first.swap, tails2, p), tails1[p]) for p in range(2)]
+    behind_eight = sum(pltpu.roll(side(relayed[p]).T[:FACE], 8 * (p + 1), 1) for p in range(2))
     for p in range(2):
         lefts[p] = first.left[p]
-    both.write(out)
-    write_tails(out, tails)
+    for i, pair in enumerate((both.left, both.right, tails)):
+        out[i * FACE : (i + 1) * FACE] = jnp.where(up, pair[1], pair[0]) + (behind_eight if i == 2 else 0.0)
+    out[3 * FACE :] = both.swap
 
 
 def four_kernel(got, out, halves, parts):
-    tails = [tails_of(got.at[i]) for i in range(4)]
-    last = [pltpu.roll(tails[0][p], LANES - 8, 1) for p in range(2)]
+    def chain(i, p, tile):
+        return got[2 * i + p, tile * FACE : (tile + 1) * FACE]
+
+    tails = [[chain(i, p, 2) for p in range(2)] for i in range(4)]
+    last = [pltpu.roll(tails[0][0], LANES - 8 * (p + 1), 1) for p in range(2)]
     segs = []
     for i in range(4):
-        seg = Segment.of(got.at[i])
+        seg = Segment([chain(i, p, 0) for p in range(2)], [chain(i, p, 1) for p in range(2)], got[2 * i, 3 * FACE :])
         seg = Segment(lagged_left(seg, tails[i], tails[i + 1] if i < 3 else last), seg.right, seg.swap)
         seg.write(parts.at[i])
         segs.append(seg)
@@ -446,7 +455,7 @@
 SMEM = pl.BlockSpec(memory_space=pltpu.SMEM)
 
 
-def call(kernel, out_shape, *operands, hbm=(), smem=(), scratch=(), flops=0):
+def call(kernel, out_shape, *operands, hbm=(), smem=(), scratch=(), moved=1 << 20):
     specs = [HBM if i in hbm else SMEM if i in smem else VMEM for i in range(len(operands))]
     several = isinstance(out_shape, tuple)
     operands = [
@@ -458,7 +467,7 @@
         in_specs=specs,
         out_specs=tuple(VMEM for _ in out_shape) if several else VMEM,
         scratch_shapes=list(scratch),
-        cost_estimate=pl.CostEstimate(flops=flops, bytes_accessed=1 << 20, transcendentals=0),
+        cost_estimate=pl.CostEstimate(flops=0, bytes_accessed=moved, transcendentals=0),
         compiler_params=pltpu.CompilerParams(vmem_limit_bytes=24 * 1024 * 1024),
     )(*operands)
 
@@ -479,6 +488,7 @@
     wide = lax.axis_size("span")
     layers = lax.axis_size("stream")
     place = lax.axis_index("stream").astype(jnp.int32).reshape(1)
+    along = lax.axis_index("span").astype(jnp.int32).reshape(1)
     dma = pltpu.SemaphoreType.DMA
 
     def room(*arrays):
@@ -489,34 +499,34 @@
 
     face = f32(2, 8, FACE)
     args = (guess, upper_block, inflow_map)
-    west_face, east_face, ahead, swap, upper = call(
-        faces_kernel, (face, face, face, f32(8, LANES), f32(LEVELS, 8, LANES)), *args, place,
-        hbm=range(3), smem=(3,), scratch=room(*args),
-    )
-    ring = [(i, (i + 1) % wide) for i in range(wide)]
-    from_west = lax.ppermute(east_face, "span", ring)
-    from_east = lax.ppermute(west_face, "span", [(b, a) for a, b in ring])
-    relayed = lax.ppermute(ahead, "stream", [(i + 8, i) for i in range(0, layers - 8, 8)])
+    near_face, far_face, ahead, swap, upper = call(
+        faces_kernel, (face, face, face, f32(8, LANES), f32(LEVELS + 1, 8, LANES)), *args, place, along,
+        hbm=range(3), smem=(3, 4), scratch=room(*args),
+    )
+    from_near = lax.ppermute(near_face, "span", [(i, i ^ 1) for i in range(wide)])
+    from_far = lax.ppermute(far_face, "span", [(i, (i - 1 + 2 * (i & 1)) % wide) for i in range(wide)])
     args = (inverse_diag, lower_block, upper_block, rhs_field)
     maps = call(
-        maps_kernel, f32(LONG + 8 * FACE, LANES), *args, ahead, swap, hbm=range(4), scratch=room(*args)
-    )
+        maps_kernel, f32(LONG + 8 * FACE, LANES), *args, ahead, swap,
+        hbm=range(4), scratch=room(*args), moved=0,
+    )
+    relayed = lax.ppermute(ahead, "stream", [(i + 8, i) for i in range(0, layers - 8, 8)])
     own, terms = call(
         vectors_kernel, (f32(LONG, LANES), f32(2, 16, FACE)),
-        maps, west_block, east_block, from_west, from_east, relayed,
+        maps, west_block, east_block, upper, from_near, from_far, relayed,
     )
 
     def across(x, distance):
         return lax.ppermute(x, "stream", [(i, i ^ distance) for i in range(layers)])
 
     got = across(own, 1)
-    pairs, lefts = call(
-        first_pair_kernel, (f32(LONG, LANES), f32(2, FACE, LANES)), upper, own, got
-    )
-    groups = [[8 * g + c + 2 * j for j in range(4)] for g in range(layers // 8) for c in range(2)]
-    four = lax.all_gather(pairs, "stream", axis_index_groups=groups)
+    chain, lefts = call(
+        first_pair_kernel, (f32(3 * FACE + 8, LANES), f32(2, FACE, LANES)), upper, own, got, relayed
+    )
+    groups = [[8 * g + j for j in range(8)] for g in range(layers // 8)]
+    chains = lax.all_gather(chain, "stream", axis_index_groups=groups)
     eight, halves, parts = call(
-        four_kernel, (f32(ROWS, LANES), f32(2, ROWS, LANES), f32(4, ROWS, LANES)), four
+        four_kernel, (f32(ROWS, LANES), f32(2, ROWS, LANES), f32(4, ROWS, LANES)), chains
     )
     here = (f32(2, 3, FACE, LANES), f32(8, LANES))
     got8 = across(eight, 8)

time: 77.6 us -> 74.8 us (0.964)
  the two profiles are of different devices: /device:TPU:1 before, /device:TPU:16 now
where the time goes in v4:
time: 74.8 us; the launch traced here: 74.4 us
  starting transfers between devices  27.2 us (36%)
  blocking collectives  19.7 us (26%)
  Pallas kernels  15.4 us (21%)
  waiting for transfers between devices  12 us (16%)
    all_gather x1, blocking collectives, per_device(): chains = lax.all_gather(chain, 'stream', axis_index_groups=groups)  19.7 us
    pallas_call x12, Pallas kernels, call(): pl.pallas_call(kernel, out_shape=out_shape, in_specs=specs, out_specs=tup...  15.4 us
    ppermute x1, starting transfers between devices, per_device(): lax.ppermute(half, 'stream', [(i, TOP[i // 8] * 8 + i % 8) for i in range...  8.73 us
    ppermute x3, waiting for transfers between devices, across(): return lax.ppermute(x, 'stream', [(i, i ^ distance) for i in range(layers)])  8.23 us
    ppermute x3, starting transfers between devices, across(): return lax.ppermute(x, 'stream', [(i, i ^ distance) for i in range(layers)])  7.67 us
    ppermute x1, starting transfers between devices, per_device(): lax.ppermute(near_face, 'span', [(i, i ^ 1) for i in range(wide)])  4.28 us
    ppermute x1, starting transfers between devices, per_device(): lax.ppermute(far_face, 'span', [(i, (i - 1 + 2 * (i & 1)) % wide) for i i...  4.12 us
    ppermute x1, waiting for transfers between devices, per_device(): lax.ppermute(half, 'stream', [(i, TOP[i // 8] * 8 + i % 8) for i in range...  3.12 us
  transfers between devices with their start and end apart: 7, of which 5 were waited for; matrix products, arithmetic and copies ran while one was open for 0% of the time, Pallas kernels for 12%

profile of v4, /device:TPU:16, one launch (start us, length us, event | category | flops | bytes accessed | tf_op | source)
XLA Modules:
  0.0 74.4 jit_solution(18130487851500289096)
XLA Ops:
  0.0 1.3 %shard_map.82 = (f32[2,8,80]{2,1,0:T(8,128)S(1)}, f32[2,8,80]{2,1,0:T(8,128)S(1)}, f32[2,8,80]{2,1,0:T(8,128)S(1)}, f32[8,128]{1,0:T(8,128)S(1)}, f32[7,8,128]{2,1,0:T(8,128)S(1)}) custom-call(f32[1,1,8,2,320]{4,3,2,1,0:T(2,128)} %guess_hbm.1, f32[1,1,2,80,80]{4,3,2,1,0:T(8,128)} %up_hbm.3, s32[1,1,2]{2,1,0:T(1,128)} %map_hbm.1, s32[1]{0:T(128)} %bitcast.place.at, ...), custom_call_target="tpu_custom_call" | custom-call | bytes 1048576 | tf_op jit(solution)/shard_map/pallas_call | solution.py:464
  1.3 4.3 %collective-permute-start = (f32[2,8,80]{2,1,0:T(8,128)S(1)}, f32[2,8,80]{2,1,0:T(8,128)S(1)}, u32[]{:S(2)}, u32[]{:S(2)}) collective-permute-start(f32[2,8,80]{2,1,0:T(8,128)S(1)} %get-tuple-element.41), channel_id=1, source_target_pairs={{0,1},{1,0},{2,3},{3,2},{4,5},{5,4},{6,7},{7,6},{8,9},{9,8},{10,11... | collective-permute-start | bytes 15368 | tf_op jit(solution)/shard_map/ppermute | solution.py:506
  5.6 4.1 %collective-permute-start.1 = (f32[2,8,80]{2,1,0:T(8,128)S(1)}, f32[2,8,80]{2,1,0:T(8,128)S(1)}, u32[]{:S(2)}, u32[]{:S(2)}) collective-permute-start(f32[2,8,80]{2,1,0:T(8,128)S(1)} %get-tuple-element.42), channel_id=1, source_target_pairs={{0,7},{1,2},{2,1},{3,4},{4,3},{5,6},{6,5},{7,0},{8,15},{9,10},{10,... | collective-permute-start | bytes 15368 | tf_op jit(solution)/shard_map/ppermute | solution.py:507
  9.7 2.4 %collective-permute-start.2 = (f32[2,8,80]{2,1,0:T(8,128)S(1)}, f32[2,8,80]{2,1,0:T(8,128)S(1)}, u32[]{:S(2)}, u32[]{:S(2)}) collective-permute-start(f32[2,8,80]{2,1,0:T(8,128)S(1)} %get-tuple-element.39.ahead), channel_id=1, source_target_pairs={{64,0},{128,64},{192,128},{256,192},{320,256},{384,320},{448,384},... | collective-permute-start | bytes 15368 | tf_op jit(solution)/shard_map/ppermute | solution.py:513
  12.0 0.0 copy-start
  12.1 0.0 copy-start.1
  12.1 2.5 %shard_map.83.maps = f32[1128,128]{1,0:T(8,128)S(1)} custom-call(f32[1,1,2,320,320]{4,3,2,1,0:T(8,128)} %inv_hbm.3, f32[1,1,2,80,80]{4,3,2,1,0:T(8,128)} %low_hbm.3, f32[1,1,2,80,80]{4,3,2,1,0:T(8,128)} %up_hbm.3, f32[1,1,8,2,320]{4,3,2,1,0:T(2,128)} %rhs_hbm.3, f32[2,8,80]{2,1,0:T(8,128)S(1)} %get-tuple-element.39.ahead, f32[8,128]{1,0:T(8,128)S(1)} %get-tuple-element.40.swap), custom_call_target="tpu_custom_call" | custom-call | tf_op jit(solution)/shard_map/pallas_call | solution.py:464
  14.5 0.0 collective-permute-done.from_near
  14.6 0.0 collective-permute-done.1.from_far
  14.6 0.7 collective-permute-done.2.relayed
  15.2 0.0 copy-done
  15.2 0.0 copy-done.1
  15.2 0.7 shard_map.84
  16.0 1.9 %collective-permute-start.3 = (f32[488,128]{1,0:T(8,128)S(1)}, f32[488,128]{1,0:T(8,128)S(1)}, u32[]{:S(2)}, u32[]{:S(2)}) collective-permute-start(f32[488,128]{1,0:T(8,128)S(1)} %get-tuple-element.44.own.one), channel_id=1, source_target_pairs={{0,8},{8,0},{16,24},{24,16},{32,40},{40,32},{48,56},{56,48},{64,72... | collective-permute-start | bytes 749576 | tf_op jit(solution)/shard_map/ppermute | solution.py:520
  17.9 1.5 %collective-permute-done.3.got.one_got = f32[488,128]{1,0:T(8,128)S(1)} collective-permute-done((f32[488,128]{1,0:T(8,128)S(1)}, f32[488,128]{1,0:T(8,128)S(1)}, u32[]{:S(2)}, u32[]{:S(2)}) %collective-permute-start.3) | collective-permute-done | bytes 249888 | tf_op jit(solution)/shard_map/ppermute | solution.py:520
  19.4 0.7 shard_map.85
  20.1 19.7 %all-gather = f32[1984,128]{1,0:T(8,128)S(1)} all-gather(f32[248,128]{1,0:T(8,128)S(1)} %get-tuple-element.45), channel_id=2, replica_groups={{0,8,16,24,32,40,48,56},{64,72,80,88,96,104,112,120},{128,136,144,152,1..., dimensions={0}, use_global_device_ids=true | all-gather | bytes 1142784 | tf_op jit(solution)/shard_map/all_gather | solution.py:527
  39.8 1.6 %shard_map.86 = (f32[328,128]{1,0:T(8,128)S(1)}, f32[2,328,128]{2,1,0:T(8,128)S(1)}, f32[4,328,128]{2,1,0:T(8,128)S(1)}) custom-call(f32[8,248,128]{2,1,0:T(8,128)S(1)} %bitcast.4), custom_call_target="tpu_custom_call" | custom-call | bytes 1048576 | tf_op jit(solution)/shard_map/pallas_call | solution.py:464
  41.4 3.5 %collective-permute-start.4 = (f32[328,128]{1,0:T(8,128)S(1)}, f32[328,128]{1,0:T(8,128)S(1)}, u32[]{:S(2)}, u32[]{:S(2)}) collective-permute-start(f32[328,128]{1,0:T(8,128)S(1)} %get-tuple-element.46.own), channel_id=1, source_target_pairs={{0,64},{8,72},{16,80},{24,88},{32,96},{40,104},{48,112},{56,120},{... | collective-permute-start | bytes 503816 | tf_op jit(solution)/shard_map/ppermute | solution.py:520
  44.9 1.9 %shard_map.87 = (f32[2,3,80,128]{3,2,1,0:T(8,128)S(1)}, f32[8,128]{1,0:T(8,128)S(1)}) custom-call(s32[1]{0:T(128)} %bitcast.place.at, f32[7,8,128]{2,1,0:T(8,128)S(1)} %get-tuple-element.38.upper, f32[488,128]{1,0:T(8,128)S(1)} %get-tuple-element.44.own.one, f32[488,128]{1,0:T(8,128)S(1)} %collective-permute-done.3.got.one_got, ...), custom_call_target="tpu_custom_call" | custom-call | bytes 1048576 | tf_op jit(solution)/shard_map/pallas_call | solution.py:464
  46.8 3.0 %collective-permute-done.4.got = f32[328,128]{1,0:T(8,128)S(1)} collective-permute-done((f32[328,128]{1,0:T(8,128)S(1)}, f32[328,128]{1,0:T(8,128)S(1)}, u32[]{:S(2)}, u32[]{:S(2)}) %collective-permute-start.4) | collective-permute-done | bytes 167968 | tf_op jit(solution)/shard_map/ppermute | solution.py:520
  49.8 0.6 shard_map.88.own
  50.4 2.3 %collective-permute-start.5 = (f32[328,128]{1,0:T(8,128)S(1)}, f32[328,128]{1,0:T(8,128)S(1)}, u32[]{:S(2)}, u32[]{:S(2)}) collective-permute-start(f32[328,128]{1,0:T(8,128)S(1)} %shard_map.88.own), channel_id=1, source_target_pairs={{0,128},{8,136},{16,144},{24,152},{32,160},{40,168},{48,176},{56,1... | collective-permute-start | bytes 503816 | tf_op jit(solution)/shard_map/ppermute | solution.py:520
  52.7 2.5 %shard_map.90 = (f32[2,320,128]{2,1,0:T(8,128)S(1)}, f32[2,320,128]{2,1,0:T(8,128)S(1)}, f32[2,320,128]{2,1,0:T(8,128)S(1)}) custom-call(f32[1,1,2,320,320]{4,3,2,1,0:T(8,128)} %inv_hbm.3, f32[1,1,2,80,80]{4,3,2,1,0:T(8,128)} %low_hbm.3, f32[1,1,8,2,320]{4,3,2,1,0:T(2,128)} %rhs_hbm.3, f32[2,16,80]{2,1,0:T(8,128)S(1)} %get-tuple-element.58.terms), custom_call_target="tpu_custom_call" | custom-call | bytes 1048576 | tf_op jit(solution)/shard_map/pallas_call | solution.py:464
  55.1 0.7 shard_map.89
  55.8 3.7 %collective-permute-done.5.got = f32[328,128]{1,0:T(8,128)S(1)} collective-permute-done((f32[328,128]{1,0:T(8,128)S(1)}, f32[328,128]{1,0:T(8,128)S(1)}, u32[]{:S(2)}, u32[]{:S(2)}) %collective-permute-start.5) | collective-permute-done | bytes 167968 | tf_op jit(solution)/shard_map/ppermute | solution.py:520
  59.5 0.7 shard_map.92.own
  60.2 8.7 %collective-permute-start.6 = (f32[160,128]{1,0:T(8,128)S(1)}, f32[160,128]{1,0:T(8,128)S(1)}, u32[]{:S(2)}, u32[]{:S(2)}) collective-permute-start(f32[160,128]{1,0:T(8,128)S(1)} %shard_map.92.own), channel_id=1, source_target_pairs={{0,384},{8,392},{16,400},{24,408},{32,416},{40,424},{48,432},{56,4... | collective-permute-start | bytes 245768 | tf_op jit(solution)/shard_map/ppermute | solution.py:546
  68.9 1.1 %shard_map.91 = (f32[2,8,320]{2,1,0:T(8,128)S(1)}, f32[2,320,128]{2,1,0:T(8,128)S(1)}, f32[8,128]{1,0:T(8,128)S(1)}) custom-call(f32[7,8,128]{2,1,0:T(8,128)S(1)} %get-tuple-element.38.upper, f32[328,128]{1,0:T(8,128)S(1)} %shard_map.88.own, f32[328,128]{1,0:T(8,128)S(1)} %collective-permute-done.5.got, f32[2,3,80,128]{3,2,1,0:T(8,128)S(1)} %get-tuple-element.63.place, ...), custom_call_target="tpu_custom_call" | custom-call | bytes 1048576 | tf_op jit(solution)/shard_map/pallas_call | solution.py:464
  70.0 3.1 %collective-permute-done.6.got = f32[160,128]{1,0:T(8,128)S(1)} collective-permute-done((f32[160,128]{1,0:T(8,128)S(1)}, f32[160,128]{1,0:T(8,128)S(1)}, u32[]{:S(2)}, u32[]{:S(2)}) %collective-permute-start.6) | collective-permute-done | bytes 81952 | tf_op jit(solution)/shard_map/ppermute | solution.py:546
  73.2 1.2 %shard_map.93 = f32[8,2,320]{2,1,0:T(2,128)} custom-call(f32[7,8,128]{2,1,0:T(8,128)S(1)} %get-tuple-element.38.upper, f32[8,128]{1,0:T(8,128)S(1)} %get-tuple-element.68.swap, f32[160,128]{1,0:T(8,128)S(1)} %shard_map.92.own, f32[160,128]{1,0:T(8,128)S(1)} %collective-permute-done.6.got, f32[2,8,320]{2,1,0:T(8,128)S(1)} %get-tuple-element.69.fixed, ...), custom_call_target="tpu_custom_call" | custom-call | bytes 1048576 | tf_op jit(solution)/shard_map/pallas_call | solution.py:464
Async XLA Ops:
  1.3 13.3 %collective-permute-start = (f32[2,8,80]{2,1,0:T(8,128)S(1)}, f32[2,8,80]{2,1,0:T(8,128)S(1)}, u32[]{:S(2)}, u32[]{:S(2)}) collective-permute-start(f32[2,8,80]{2,1,0:T(8,128)S(1)} %get-tuple-element.41), channel_id=1, source_target_pairs={{0,1},{1,0},{2,3},{3,2},{4,5},{5,4},{6,7},{7,6},{8,9},{9,8},{10,11... | collective-permute-start | bytes 15368 | tf_op jit(solution)/shard_map/ppermute | solution.py:506
  5.6 9.0 %collective-permute-start.1 = (f32[2,8,80]{2,1,0:T(8,128)S(1)}, f32[2,8,80]{2,1,0:T(8,128)S(1)}, u32[]{:S(2)}, u32[]{:S(2)}) collective-permute-start(f32[2,8,80]{2,1,0:T(8,128)S(1)} %get-tuple-element.42), channel_id=1, source_target_pairs={{0,7},{1,2},{2,1},{3,4},{4,3},{5,6},{6,5},{7,0},{8,15},{9,10},{10,... | collective-permute-start | bytes 15368 | tf_op jit(solution)/shard_map/ppermute | solution.py:507
  9.7 5.5 %collective-permute-start.2 = (f32[2,8,80]{2,1,0:T(8,128)S(1)}, f32[2,8,80]{2,1,0:T(8,128)S(1)}, u32[]{:S(2)}, u32[]{:S(2)}) collective-permute-start(f32[2,8,80]{2,1,0:T(8,128)S(1)} %get-tuple-element.39.ahead), channel_id=1, source_target_pairs={{64,0},{128,64},{192,128},{256,192},{320,256},{384,320},{448,384},... | collective-permute-start | bytes 15368 | tf_op jit(solution)/shard_map/ppermute | solution.py:513
  12.0 3.2 %copy-start = (f32[1,1,2,80,80]{4,3,2,1,0:T(8,128)S(1)}, f32[1,1,2,80,80]{4,3,2,1,0:T(8,128)}, u32[]{:S(2)}) copy-start(f32[1,1,2,80,80]{4,3,2,1,0:T(8,128)} %west.1) | copy-start | bytes 153604
  12.1 3.2 %copy-start.1 = (f32[1,1,2,80,80]{4,3,2,1,0:T(8,128)S(1)}, f32[1,1,2,80,80]{4,3,2,1,0:T(8,128)}, u32[]{:S(2)}) copy-start(f32[1,1,2,80,80]{4,3,2,1,0:T(8,128)} %east.1) | copy-start | bytes 153604
  16.0 3.4 %collective-permute-start.3 = (f32[488,128]{1,0:T(8,128)S(1)}, f32[488,128]{1,0:T(8,128)S(1)}, u32[]{:S(2)}, u32[]{:S(2)}) collective-permute-start(f32[488,128]{1,0:T(8,128)S(1)} %get-tuple-element.44.own.one), channel_id=1, source_target_pairs={{0,8},{8,0},{16,24},{24,16},{32,40},{40,32},{48,56},{56,48},{64,72... | collective-permute-start | bytes 749576 | tf_op jit(solution)/shard_map/ppermute | solution.py:520
  41.4 8.4 %collective-permute-start.4 = (f32[328,128]{1,0:T(8,128)S(1)}, f32[328,128]{1,0:T(8,128)S(1)}, u32[]{:S(2)}, u32[]{:S(2)}) collective-permute-start(f32[328,128]{1,0:T(8,128)S(1)} %get-tuple-element.46.own), channel_id=1, source_target_pairs={{0,64},{8,72},{16,80},{24,88},{32,96},{40,104},{48,112},{56,120},{... | collective-permute-start | bytes 503816 | tf_op jit(solution)/shard_map/ppermute | solution.py:520
  50.4 9.1 %collective-permute-start.5 = (f32[328,128]{1,0:T(8,128)S(1)}, f32[328,128]{1,0:T(8,128)S(1)}, u32[]{:S(2)}, u32[]{:S(2)}) collective-permute-start(f32[328,128]{1,0:T(8,128)S(1)} %shard_map.88.own), channel_id=1, source_target_pairs={{0,128},{8,136},{16,144},{24,152},{32,160},{40,168},{48,176},{56,1... | collective-permute-start | bytes 503816 | tf_op jit(solution)/shard_map/ppermute | solution.py:520
  60.2 13.0 %collective-permute-start.6 = (f32[160,128]{1,0:T(8,128)S(1)}, f32[160,128]{1,0:T(8,128)S(1)}, u32[]{:S(2)}, u32[]{:S(2)}) collective-permute-start(f32[160,128]{1,0:T(8,128)S(1)} %shard_map.92.own), channel_id=1, source_target_pairs={{0,384},{8,392},{16,400},{24,408},{32,416},{40,424},{48,432},{56,4... | collective-permute-start | bytes 245768 | tf_op jit(solution)/shard_map/ppermute | solution.py:546

commit v5 on v4

--- a/solution.py
+++ b/solution.py
@@ -126,14 +126,6 @@
             ref[2 * p * FACE : (2 * p + 1) * FACE] = self.left[p]
             ref[(2 * p + 1) * FACE : (2 * p + 2) * FACE] = self.right[p]
         ref[4 * FACE : 4 * FACE + 8] = self.swap
-
-    def top(self, ref):
-        for p in range(2):
-            left, right = self.left[p], self.right[p]
-            lane = lane_of(left.shape)
-            tile = jnp.where(lane < VEC, unpack_d(left, right), left)
-            tile = jnp.where(lane < REST, tile, pltpu.roll(right, 8, 1))
-            ref[p * FACE : (p + 1) * FACE] = jnp.where(lane < REST + 8, tile, self.swap[:1])
 
 
 def tails_of(ref):
@@ -185,14 +177,6 @@
         )
 
     return seg(got, own), seg(own, got)
-
-
-def fetch(pairs, sems):
-    copies = [pltpu.make_async_copy(a, b, sems.at[i]) for i, (a, b) in enumerate(pairs)]
-    for copy in copies:
-        copy.start()
-    for copy in copies:
-        copy.wait()
 
 
 def columns_of(rows):
@@ -235,12 +219,11 @@
 
 
 def faces_kernel(
-    guess_hbm, up_hbm, map_hbm, place, along, near, far, lag, swap, upper, guess, up, which, sems
+    guess_hbm, up_hbm, map_hbm, inv_hbm, low_hbm, rhs_hbm, place, along,
+    near, far, lag, swap, upper, inv, low, up, rhs, guess, which, sems,
 ):
-    copies = [
-        pltpu.make_async_copy(a, b, sems.at[i])
-        for i, (a, b) in enumerate([(guess_hbm, guess), (up_hbm, up), (map_hbm, which)])
-    ]
+    pairs = [(guess_hbm, guess), (up_hbm, up), (map_hbm, which), (inv_hbm, inv), (low_hbm, low), (rhs_hbm, rhs)]
+    copies = [pltpu.make_async_copy(a, b, sems.at[i]) for i, (a, b) in enumerate(pairs)]
     for copy in copies:
         copy.start()
     for level in range(LEVELS):
@@ -249,7 +232,7 @@
     upper[LEVELS] = jnp.full((8, LANES), (along[0] & 1).astype(F32), F32)
     odd = upper[LEVELS][:, :FACE] > 0.5
     tables = jnp.concatenate([stream_pick(0, LANES), span_pick(0, LANES), span_pick(3, LANES)], axis=1)
-    for copy in copies:
+    for copy in copies[:3]:
         copy.wait()
     both = pick(jnp.concatenate([guess[0, 0, :, n, :] for n in range(2)], axis=0), tables)
     flag = flag_of(which)
@@ -265,14 +248,15 @@
         made.append(dot(mine[:, :FACE], up[0, 0, n], NT))
     for p in range(2):
         lag[p] = jnp.where(swapped, made[1 - p], made[p])
-
-
-def maps_kernel(inv_hbm, low_hbm, up_hbm, rhs_hbm, ahead, swap, own, inv, low, up, rhs, sems):
-    fetch([(inv_hbm, inv), (low_hbm, low), (up_hbm, up), (rhs_hbm, rhs)], sems)
+    for copy in copies[3:]:
+        copy.wait()
+
+
+def maps_kernel(inv, low, up, rhs, ahead, swap, own):
     make_maps(inv, low, up, rhs, ahead, swap[...], own)
 
 
-def vectors_kernel(maps, west, east, upper, from_near, from_far, relayed, own, terms):
+def vectors_kernel(maps, west, east, upper, from_far, from_near, relayed, own, terms):
     odd = upper[LEVELS][:, :FACE] > 0.5
     b, e = [], []
     for n in range(2):
@@ -295,8 +279,7 @@
     write_tails(own, tails_of(maps))
 
 
-def rest_kernel(inv_hbm, low_hbm, rhs_hbm, terms, zin, zout, base, inv, low, rhs, sems):
-    fetch([(inv_hbm, inv), (low_hbm, low), (rhs_hbm, rhs)], sems)
+def rest_kernel(inv, low, rhs, terms, zin, zout, base):
     pout = stream_pick(3, LANES)
     lane = lane_of((DOF, LANES))
     halo = pick(terms[0], span_pick(0), NT) + pick(terms[1], span_pick(3), NT)
@@ -309,12 +292,12 @@
         base[n] = vec_only(z)
 
 
-def pair_kernel(level, form, upper, own, got, out):
-    both = join(*ordered(upper[level], Segment.of(own), Segment.of(got)))
-    if form == "top":
-        both.top(out)
-    else:
-        both.write(out)
+def sixteen_kernel(upper, own, got, out):
+    both = join(*ordered(upper[3], Segment.of(own), Segment.of(got)))
+    second = upper[0][:1] > 0.5
+    for i, pair in enumerate((both.left, both.right)):
+        out[i * FACE : (i + 1) * FACE] = jnp.where(second, pair[1], pair[0])
+    out[2 * FACE :] = both.swap
 
 
 def first_pair_kernel(upper, own, got, relayed, out, lefts):
@@ -335,17 +318,18 @@
     out[3 * FACE :] = both.swap
 
 
-def four_kernel(got, out, halves, parts):
+def four_kernel(got, out, halves, lefts):
     def chain(i, p, tile):
         return got[2 * i + p, tile * FACE : (tile + 1) * FACE]
 
     tails = [[chain(i, p, 2) for p in range(2)] for i in range(4)]
-    last = [pltpu.roll(tails[0][0], LANES - 8 * (p + 1), 1) for p in range(2)]
+    last = [pltpu.roll(tails[0][1], LANES - 8 * (p + 1), 1) for p in range(2)]
     segs = []
     for i in range(4):
         seg = Segment([chain(i, p, 0) for p in range(2)], [chain(i, p, 1) for p in range(2)], got[2 * i, 3 * FACE :])
         seg = Segment(lagged_left(seg, tails[i], tails[i + 1] if i < 3 else last), seg.right, seg.swap)
-        seg.write(parts.at[i])
+        for p in range(2):
+            lefts[i, p] = seg.left[p]
         segs.append(seg)
     both = [join(segs[2 * i], segs[2 * i + 1]) for i in range(2)]
     join(*both).write(out)
@@ -395,13 +379,7 @@
             ref[p, i] = place[p][i]
 
 
-def place_kernel(level, upper, own, got, place, swap, out, swap_out):
-    mine, other = Segment.of(own), Segment.of(got)
-    write_place(out, widen_place(read_place(place), upper[level], mine, other))
-    swap_out[...] = jnp.abs(swap[...] - jnp.where(upper[level] > 0.5, other.swap, 0.0))
-
-
-def four_place_kernel(at, upper, one, one_got, lefts, got, halves, out, swap_out):
+def four_place_kernel(at, upper, one, one_got, lefts, got, pair_lefts, halves, out, swap_out):
     mine, other = Segment.of(one), Segment.of(one_got)
     up = upper[0][:1] > 0.5
     mine.left = [jnp.where(up, mine.left[p], lefts[p]) for p in range(2)]
@@ -410,7 +388,12 @@
     x = jnp.abs(mine.swap - jnp.where(upper[0] > 0.5, other.swap, 0.0))
     j = (at[0] >> 1) & 3
     half = j >> 1
-    mine, other = Segment.of(got.at[j]), Segment.of(got.at[j ^ 1])
+
+    def pair_of(i):
+        right = [got[2 * i + p, FACE : 2 * FACE] for p in range(2)]
+        return Segment([pair_lefts[i, p] for p in range(2)], right, got[2 * i, 3 * FACE :])
+
+    mine, other = pair_of(j), pair_of(j ^ 1)
     made = widen_place(made, upper[1], mine, other)
     x = jnp.abs(x - jnp.where(upper[1] > 0.5, other.swap, 0.0))
     mine, other = Segment.of(halves.at[half]), Segment.of(halves.at[1 - half])
@@ -418,36 +401,71 @@
     swap_out[...] = jnp.abs(x - jnp.where(upper[2] > 0.5, other.swap, 0.0))
 
 
-def answer_kernel(upper, own, got, place, swap, zin, zout, base, fixed, free, turn):
-    mine, other = Segment.of(own), Segment.of(got)
-    made = widen_place(read_place(place), upper[4], mine, other)
-    x = jnp.abs(swap[...] - jnp.where(upper[4] > 0.5, other.swap, 0.0))
-    turn[...] = x
-    up = upper[5][:1] > 0.5
+def answer_kernel(place, turn, zin, zout, base, fixed, free):
+    made = read_place(place)
+    x = turn[...]
     for n in range(2):
         p0, q0, r0 = [behind(x, [made[0][i], made[1][i]], n) for i in range(3)]
-        t = jnp.where(up, p0, vec_only(p0))
-        c = jnp.where(up, q0, jnp.where(lane_of(r0.shape) < VEC, r0, 0.0) + vec_only(q0))
-        f = dot(jnp.concatenate([zin[n], zout[n]], axis=1), jnp.concatenate([tall(t), tall(c)], axis=0))
-        free[n] = f
+        f = dot(jnp.concatenate([zin[n], zout[n]], axis=1), jnp.concatenate([tall(p0), tall(q0)], axis=0))
+        free[n] = jnp.concatenate([f, dot(zout[n], tall(r0))], axis=1)
         fixed[n] = (base[n] - f).T[VEC:REST]
 
 
-def last_kernel(upper, swap, own, got, fixed, free, out):
-    up = upper[5][:1] > 0.5
-    mine = [own[p * FACE : (p + 1) * FACE] for p in range(2)]
-    far = [got[p * FACE : (p + 1) * FACE] for p in range(2)]
-    own_swap = jnp.broadcast_to(mine[0][:1, LANES - 1 :], (1, LANES))
-    far_swap = jnp.broadcast_to(far[0][:1, LANES - 1 :], (1, LANES))
-    unknown = []
-    for p in range(2):
-        above = behind(far_swap, far, p)
-        sib = behind(own_swap, far, p)
-        below = dot(sib, tall(vec_only(mine[p]))) + pltpu.roll(sib, LANES - 8, 1)
-        unknown.append(jnp.where(up, above, below).T[VEC:REST])
+def last_kernel(upper, got, own, got8, turn, fixed, free, out):
+    def chain(i, p, tile):
+        return got[2 * i + p, tile * FACE : (tile + 1) * FACE]
+
+    segs = [
+        Segment([chain(i, p, 0) for p in range(2)], [chain(i, p, 1) for p in range(2)], got[2 * i, 2 * FACE :])
+        for i in range(4)
+    ]
+    zero = jnp.zeros((FACE, LANES), F32)
+    t, ahead = [[zero, zero]], [None]
+    first = [vec_only(segs[0].left[p]) for p in range(2)]
+    t.append([behind(segs[0].swap, first, p) for p in range(2)])
+    for i in (1, 2, 3):
+        through, down = [], []
+        for p in range(2):
+            left, right = segs[i].left[p], segs[i].right[p]
+            both = dot(jnp.concatenate([unpack_d(left, right), left], axis=0), tall(t[i][p]))
+            down.append(both[:FACE] + vec_only(right))
+            through.append(vec_only(both[FACE:] + left))
+        ahead.append(down)
+        if i < 3:
+            t.append([behind(segs[i].swap, through, p) for p in range(2)])
+    c = [None, None, None, [zero, zero]]
+    for i in (2, 1, 0):
+        arriving = [
+            vec_only(ahead[i + 1][p] + (dot(segs[i + 1].right[p], tall(c[i + 1][p])) if i < 2 else 0.0))
+            for p in range(2)
+        ]
+        c[i] = [behind(segs[i].swap, arriving, p) for p in range(2)]
+
+    def here(pairs):
+        low, high = upper[4][:1] > 0.5, upper[5][:1] > 0.5
+        return [
+            jnp.where(high, jnp.where(low, pairs[3][p], pairs[2][p]), jnp.where(low, pairs[1][p], pairs[0][p]))
+            for p in range(2)
+        ]
+
+    t_in, c_out = here(t), here(c)
+    mine, other = Segment.of(own), Segment.of(got8)
+    up = upper[3][:1] > 0.5
+    lower = [jnp.where(up, other.left[p], mine.left[p]) for p in range(2)]
+    swap = jnp.where(up, other.swap, mine.swap)
+    middle = [vec_only(dot(lower[p], tall(t_in[p])) + lower[p]) for p in range(2)]
+    t_at, c_at = [], []
+    for p in range(2):
+        left, right = behind(mine.swap, other.left, p), behind(mine.swap, other.right, p)
+        back = dot(
+            jnp.concatenate([unpack_d(left, right), right], axis=1),
+            jnp.concatenate([tall(middle[p]), tall(c_out[p])], axis=0),
+        )
+        t_at.append(jnp.where(up, behind(swap, middle, p), t_in[p]))
+        c_at.append(jnp.where(up, behind(swap, c_out, p), vec_only(back + right)))
     for n in range(2):
-        x = widen(behind(swap[...][:, :FACE], unknown, n))
-        out[:, n, :] = fixed[n] - dot(x, free[n], NT)
+        rows = [widen(behind(turn[...], pair, n).T[VEC:REST]) for pair in (t_at, c_at)]
+        out[:, n, :] = fixed[n] - dot(jnp.concatenate(rows, axis=1), free[n], NT)
 
 
 HBM = pl.BlockSpec(memory_space=pltpu.HBM)
@@ -455,7 +473,7 @@
 SMEM = pl.BlockSpec(memory_space=pltpu.SMEM)
 
 
-def call(kernel, out_shape, *operands, hbm=(), smem=(), scratch=(), moved=1 << 20):
+def call(kernel, out_shape, *operands, hbm=(), smem=(), scratch=()):
     specs = [HBM if i in hbm else SMEM if i in smem else VMEM for i in range(len(operands))]
     several = isinstance(out_shape, tuple)
     operands = [
@@ -467,7 +485,7 @@
         in_specs=specs,
         out_specs=tuple(VMEM for _ in out_shape) if several else VMEM,
         scratch_shapes=list(scratch),
-        cost_estimate=pl.CostEstimate(flops=0, bytes_accessed=moved, transcendentals=0),
+        cost_estimate=pl.CostEstimate(flops=0, bytes_accessed=1 << 20, transcendentals=0),
         compiler_params=pltpu.CompilerParams(vmem_limit_bytes=24 * 1024 * 1024),
     )(*operands)
 
@@ -479,7 +497,6 @@
 LEVELS = 6
 ROWS = 4 * FACE + 8
 LONG = ROWS + 2 * FACE
-TOP = (6, 7, 4, 5, 2, 3, 0, 1)
 
 
 def per_device(
@@ -489,31 +506,25 @@
     layers = lax.axis_size("stream")
     place = lax.axis_index("stream").astype(jnp.int32).reshape(1)
     along = lax.axis_index("span").astype(jnp.int32).reshape(1)
-    dma = pltpu.SemaphoreType.DMA
-
-    def room(*arrays):
-        held = [
-            pltpu.SMEM(a.shape, a.dtype) if a.dtype == jnp.int32 else pltpu.VMEM(a.shape, F32) for a in arrays
-        ]
-        return (*held, dma((len(arrays),)))
-
     face = f32(2, 8, FACE)
-    args = (guess, upper_block, inflow_map)
-    near_face, far_face, ahead, swap, upper = call(
-        faces_kernel, (face, face, face, f32(8, LANES), f32(LEVELS + 1, 8, LANES)), *args, place, along,
-        hbm=range(3), smem=(3, 4), scratch=room(*args),
-    )
+    args = (guess, upper_block, inflow_map, inverse_diag, lower_block, rhs_field)
+    near_face, far_face, ahead, swap, upper, inv, low, up, rhs = call(
+        faces_kernel,
+        (
+            face, face, face, f32(8, LANES), f32(LEVELS + 1, 8, LANES),
+            *(f32(*a.shape) for a in (inverse_diag, lower_block, upper_block, rhs_field)),
+        ),
+        *args, place, along,
+        hbm=range(6), smem=(6, 7),
+        scratch=(pltpu.VMEM(guess.shape, F32), pltpu.SMEM(inflow_map.shape, jnp.int32), pltpu.SemaphoreType.DMA((6,))),
+    )
+    from_far = lax.ppermute(far_face, "span", [(i, (i - 1 + 2 * (i & 1)) % wide) for i in range(wide)])
     from_near = lax.ppermute(near_face, "span", [(i, i ^ 1) for i in range(wide)])
-    from_far = lax.ppermute(far_face, "span", [(i, (i - 1 + 2 * (i & 1)) % wide) for i in range(wide)])
-    args = (inverse_diag, lower_block, upper_block, rhs_field)
-    maps = call(
-        maps_kernel, f32(LONG + 8 * FACE, LANES), *args, ahead, swap,
-        hbm=range(4), scratch=room(*args), moved=0,
-    )
-    relayed = lax.ppermute(ahead, "stream", [(i + 8, i) for i in range(0, layers - 8, 8)])
+    relayed = lax.ppermute(ahead, "stream", [(i + 8, i + 1) for i in range(0, layers - 8, 8)])
+    maps = call(maps_kernel, f32(LONG + 8 * FACE, LANES), inv, low, up, rhs, ahead, swap)
     own, terms = call(
         vectors_kernel, (f32(LONG, LANES), f32(2, 16, FACE)),
-        maps, west_block, east_block, upper, from_near, from_far, relayed,
+        maps, west_block, east_block, upper, from_far, from_near, relayed,
     )
 
     def across(x, distance):
@@ -525,30 +536,26 @@
     )
     groups = [[8 * g + j for j in range(8)] for g in range(layers // 8)]
     chains = lax.all_gather(chain, "stream", axis_index_groups=groups)
-    eight, halves, parts = call(
-        four_kernel, (f32(ROWS, LANES), f32(2, ROWS, LANES), f32(4, ROWS, LANES)), chains
+    eight, halves, pair_lefts = call(
+        four_kernel, (f32(ROWS, LANES), f32(2, ROWS, LANES), f32(4, 2, FACE, LANES)), chains
     )
     here = (f32(2, 3, FACE, LANES), f32(8, LANES))
     got8 = across(eight, 8)
-    spot, turn = call(four_place_kernel, here, place, upper, own, got, lefts, parts, halves, smem=(0,))
-    got8, spot, turn = lax.optimization_barrier((got8, spot, turn))
-    sixteen = call(functools.partial(pair_kernel, 3, ""), f32(ROWS, LANES), upper, eight, got8)
-    got16 = across(sixteen, 16)
-    args = (inverse_diag, lower_block, rhs_field)
-    terms, sixteen = lax.optimization_barrier((terms, sixteen))
-    zin, zout, base = call(
-        rest_kernel, tuple(f32(2, DOF, LANES) for _ in range(3)), *args, terms,
-        hbm=range(3), scratch=room(*args),
-    )
-    spot, turn = call(functools.partial(place_kernel, 3), here, upper, eight, got8, spot, turn)
-    got16, spot, turn, zin, zout, base = lax.optimization_barrier((got16, spot, turn, zin, zout, base))
-    half = call(functools.partial(pair_kernel, 4, "top"), f32(2 * FACE, LANES), upper, sixteen, got16)
-    got32 = lax.ppermute(half, "stream", [(i, TOP[i // 8] * 8 + i % 8) for i in range(layers)])
-    fixed, free, turn = call(
-        answer_kernel, (f32(2, 8, DOF), f32(2, DOF, LANES), f32(8, LANES)),
-        upper, sixteen, got16, spot, turn, zin, zout, base,
-    )
-    out = call(last_kernel, f32(8, 2, DOF), upper, turn, half, got32, fixed, free)
+    spot, turn = call(four_place_kernel, here, place, upper, own, got, lefts, chains, pair_lefts, halves, smem=(0,))
+    terms, eight = lax.optimization_barrier((terms, eight))
+    zin, zout, base = call(rest_kernel, tuple(f32(2, DOF, LANES) for _ in range(3)), inv, low, rhs, terms)
+    fixed, free = call(
+        answer_kernel, (f32(2, 8, DOF), f32(2, DOF, 2 * LANES)), spot, turn, zin, zout, base
+    )
+    got8, fixed, free, turn = lax.optimization_barrier((got8, fixed, free, turn))
+    chain = call(sixteen_kernel, f32(2 * FACE + 8, LANES), upper, eight, got8)
+    groups = [
+        [16 * i + 8 * odd + 2 * z + c for i in range(layers // 16) for c in range(2)]
+        for odd in range(2)
+        for z in range(4)
+    ]
+    sixteens = lax.all_gather(chain, "stream", axis_index_groups=groups)
+    out = call(last_kernel, f32(8, 2, DOF), upper, sixteens, eight, got8, turn, fixed, free)
     return out[None, None]
 
 

time: 74.8 us -> 72.9 us (0.975)
  the two profiles are of different devices: /device:TPU:16 before, /device:TPU:1 now
where the time goes in v5:
time: 72.9 us; the launch traced here: 72.7 us
  blocking collectives  40.1 us (55%)
  starting transfers between devices  15.8 us (22%)
  Pallas kernels  12.2 us (17%)
  waiting for transfers between devices  4.48 us (6%)
    all_gather x1, blocking collectives, per_device(): chains = lax.all_gather(chain, 'stream', axis_index_groups=groups)  20.7 us
    all_gather x1, blocking collectives, per_device(): sixteens = lax.all_gather(chain, 'stream', axis_index_groups=groups)  19.4 us
    pallas_call x10, Pallas kernels, call(): pl.pallas_call(kernel, out_shape=out_shape, in_specs=specs, out_specs=tup...  12.2 us
    ppermute x1, starting transfers between devices, per_device(): lax.ppermute(far_face, 'span', [(i, (i - 1 + 2 * (i & 1)) % wide) for i i...  7.02 us
    ppermute x2, starting transfers between devices, across(): return lax.ppermute(x, 'stream', [(i, i ^ distance) for i in range(layers)])  5.53 us
    ppermute x1, waiting for transfers between devices, per_device(): lax.ppermute(ahead, 'stream', [(i + 8, i + 1) for i in range(0, layers -...  2.65 us
    ppermute x1, starting transfers between devices, per_device(): lax.ppermute(near_face, 'span', [(i, i ^ 1) for i in range(wide)])  1.92 us
    ppermute x2, waiting for transfers between devices, across(): return lax.ppermute(x, 'stream', [(i, i ^ distance) for i in range(layers)])  1.83 us
  transfers between devices with their start and end apart: 5, of which 3 were waited for; matrix products, arithmetic and copies ran while one was open for 0% of the time, Pallas kernels for 7%

profile of v5, /device:TPU:1, one launch (start us, length us, event | category | flops | bytes accessed | tf_op | source)
XLA Modules:
  0.0 72.7 jit_solution(7009763348820146871)
XLA Ops:
  0.0 1.3 %shard_map.82 = (f32[2,8,80]{2,1,0:T(8,128)S(1)}, f32[2,8,80]{2,1,0:T(8,128)S(1)}, f32[2,8,80]{2,1,0:T(8,128)S(1)}, f32[8,128]{1,0:T(8,128)S(1)}, f32[7,8,128]{2...) custom-call(f32[1,1,8,2,320]{4,3,2,1,0:T(2,128)} %guess_hbm.1, ...), custom_call_target="tpu_custom_call" | custom-call | bytes 1048576 | tf_op jit(solution)/shard_map/pallas_call | solution.py:482
  1.3 7.0 %collective-permute-start = (f32[2,8,80]{2,1,0:T(8,128)S(1)}, f32[2,8,80]{2,1,0:T(8,128)S(1)}, u32[]{:S(2)}, u32[]{:S(2)}) collective-permute-start(f32[2,8,80]{2,1,0:T(8,128)S(1)} %get-tuple-element.41), channel_id=1, source_target_pairs={{0,7},{1,2},{2,1},{3,4},{4,3},{5,6},{6,5},{7,0},{8,15},{9,10},{10,... | collective-permute-start | bytes 15368 | tf_op jit(solution)/shard_map/ppermute | solution.py:521
  8.4 1.9 %collective-permute-start.1 = (f32[2,8,80]{2,1,0:T(8,128)S(1)}, f32[2,8,80]{2,1,0:T(8,128)S(1)}, u32[]{:S(2)}, u32[]{:S(2)}) collective-permute-start(f32[2,8,80]{2,1,0:T(8,128)S(1)} %get-tuple-element.42), channel_id=1, source_target_pairs={{0,1},{1,0},{2,3},{3,2},{4,5},{5,4},{6,7},{7,6},{8,9},{9,8},{10,11... | collective-permute-start | bytes 15368 | tf_op jit(solution)/shard_map/ppermute | solution.py:522
  10.3 1.3 %collective-permute-start.2 = (f32[2,8,80]{2,1,0:T(8,128)S(1)}, f32[2,8,80]{2,1,0:T(8,128)S(1)}, u32[]{:S(2)}, u32[]{:S(2)}) collective-permute-start(f32[2,8,80]{2,1,0:T(8,128)S(1)} %get-tuple-element.39.ahead), channel_id=1, source_target_pairs={{64,8},{128,72},{192,136},{256,200},{320,264},{384,328},{448,392},... | collective-permute-start | bytes 15368 | tf_op jit(solution)/shard_map/ppermute | solution.py:523
  11.6 0.0 copy-start
  11.6 0.0 copy-start.1
  11.6 1.2 %shard_map.83.maps = f32[1128,128]{1,0:T(8,128)S(1)} custom-call(f32[1,1,2,320,320]{4,3,2,1,0:T(8,128)S(1)} %get-tuple-element.35.inv, f32[1,1,2,80,80]{4,3,2,1,0:T(8,128)S(1)} %get-tuple-element.36.low, f32[1,1,2,80,80]{4,3,2,1,0:T(8,128)S(1)} %get-tuple-element.37.up, f32[1,1,8,2,320]{4,3,2,1,0:T(2,128)S(1)} %get-tuple-element.38.rhs, ...), custom_call_target="tpu_custom_call" | custom-call | bytes 1048576 | tf_op jit(solution)/shard_map/pallas_call | solution.py:482
  12.8 0.0 collective-permute-done.from_far
  12.8 0.0 collective-permute-done.1.from_near
  12.8 2.6 %collective-permute-done.2.relayed = f32[2,8,80]{2,1,0:T(8,128)S(1)} collective-permute-done((f32[2,8,80]{2,1,0:T(8,128)S(1)}, f32[2,8,80]{2,1,0:T(8,128)S(1)}, u32[]{:S(2)}, u32[]{:S(2)}) %collective-permute-start.2) | collective-permute-done | bytes 5152 | tf_op jit(solution)/shard_map/ppermute | solution.py:523
  15.5 0.0 copy-done
  15.5 0.0 copy-done.1
  15.5 0.7 %shard_map.84 = (f32[488,128]{1,0:T(8,128)S(1)}, f32[2,16,80]{2,1,0:T(8,128)S(1)}) custom-call(f32[1128,128]{1,0:T(8,128)S(1)} %shard_map.83.maps, f32[1,1,2,80,80]{4,3,2,1,0:T(8,128)S(1)} %copy-done, f32[1,1,2,80,80]{4,3,2,1,0:T(8,128)S(1)} %copy-done.1, f32[7,8,128]{2,1,0:T(8,128)S(1)} %get-tuple-element.34.upper, ...), custom_call_target="tpu_custom_call" | custom-call | bytes 1048576 | tf_op jit(solution)/shard_map/pallas_call | solution.py:482
  16.2 2.3 %collective-permute-start.3 = (f32[488,128]{1,0:T(8,128)S(1)}, f32[488,128]{1,0:T(8,128)S(1)}, u32[]{:S(2)}, u32[]{:S(2)}) collective-permute-start(f32[488,128]{1,0:T(8,128)S(1)} %get-tuple-element.44.own.one), channel_id=1, source_target_pairs={{0,8},{8,0},{16,24},{24,16},{32,40},{40,32},{48,56},{56,48},{64,72... | collective-permute-start | bytes 749576 | tf_op jit(solution)/shard_map/ppermute | solution.py:531
  18.6 1.1 %collective-permute-done.3.got.one_got = f32[488,128]{1,0:T(8,128)S(1)} collective-permute-done((f32[488,128]{1,0:T(8,128)S(1)}, f32[488,128]{1,0:T(8,128)S(1)}, u32[]{:S(2)}, u32[]{:S(2)}) %collective-permute-start.3) | collective-permute-done | bytes 249888 | tf_op jit(solution)/shard_map/ppermute | solution.py:531
  19.7 0.7 shard_map.85
  20.4 20.7 %all-gather = f32[1984,128]{1,0:T(8,128)S(1)} all-gather(f32[248,128]{1,0:T(8,128)S(1)} %get-tuple-element.45), channel_id=2, replica_groups={{0,8,16,24,32,40,48,56},{64,72,80,88,96,104,112,120},{128,136,144,152,1..., dimensions={0}, use_global_device_ids=true | all-gather | bytes 1142784 | tf_op jit(solution)/shard_map/all_gather | solution.py:538
  41.1 1.6 %shard_map.86 = (f32[328,128]{1,0:T(8,128)S(1)}, f32[2,328,128]{2,1,0:T(8,128)S(1)}, f32[4,2,80,128]{3,2,1,0:T(8,128)S(1)}) custom-call(f32[8,248,128]{2,1,0:T(8,128)S(1)} %bitcast.5), custom_call_target="tpu_custom_call" | custom-call | bytes 1048576 | tf_op jit(solution)/shard_map/pallas_call | solution.py:482
  42.7 3.2 %collective-permute-start.4 = (f32[328,128]{1,0:T(8,128)S(1)}, f32[328,128]{1,0:T(8,128)S(1)}, u32[]{:S(2)}, u32[]{:S(2)}) collective-permute-start(f32[328,128]{1,0:T(8,128)S(1)} %get-tuple-element.47.own), channel_id=1, source_target_pairs={{0,64},{8,72},{16,80},{24,88},{32,96},{40,104},{48,112},{56,120},{... | collective-permute-start | bytes 503816 | tf_op jit(solution)/shard_map/ppermute | solution.py:531
  45.9 1.2 %shard_map.88 = (f32[2,320,128]{2,1,0:T(8,128)S(1)}, f32[2,320,128]{2,1,0:T(8,128)S(1)}, f32[2,320,128]{2,1,0:T(8,128)S(1)}) custom-call(f32[1,1,2,320,320]{4,3,2,1,0:T(8,128)S(1)} %get-tuple-element.35.inv, f32[1,1,2,80,80]{4,3,2,1,0:T(8,128)S(1)} %get-tuple-element.36.low, f32[1,1,8,2,320]{4,3,2,1,0:T(2,128)S(1)} %get-tuple-element.38.rhs, ...), custom_call_target="tpu_custom_call" | custom-call | bytes 1048576 | tf_op jit(solution)/shard_map/pallas_call | solution.py:482
  47.1 1.9 %shard_map.87 = (f32[2,3,80,128]{3,2,1,0:T(8,128)S(1)}, f32[8,128]{1,0:T(8,128)S(1)}) custom-call(s32[1]{0:T(128)} %bitcast.place.at, f32[7,8,128]{2,1,0:T(8,128)S(1)} %get-tuple-element.34.upper, f32[488,128]{1,0:T(8,128)S(1)} %get-tuple-element.44.own.one, f32[488,128]{1,0:T(8,128)S(1)} %collective-permute-done.3.got.one_got, ...), custom_call_target="tpu_custom_call" | custom-call | bytes 1048576 | tf_op jit(solution)/shard_map/pallas_call | solution.py:482
  49.0 0.6 shard_map.89
  49.6 0.7 collective-permute-done.4.got.got8
  50.3 0.6 shard_map.90
  50.9 19.4 %all-gather.1 = f32[1344,128]{1,0:T(8,128)S(1)} all-gather(f32[168,128]{1,0:T(8,128)S(1)} %shard_map.90), channel_id=3, replica_groups={{0,8,128,136,256,264,384,392},{16,24,144,152,272,280,400,408},{32,40,16..., dimensions={0}, use_global_device_ids=true | all-gather | bytes 774144 | tf_op jit(solution)/shard_map/all_gather | solution.py:557
  70.3 2.4 %shard_map.91 = f32[8,2,320]{2,1,0:T(2,128)} custom-call(f32[7,8,128]{2,1,0:T(8,128)S(1)} %get-tuple-element.34.upper, f32[8,168,128]{2,1,0:T(8,128)S(1)} %bitcast.7, f32[328,128]{1,0:T(8,128)S(1)} %get-tuple-element.47.own, f32[328,128]{1,0:T(8,128)S(1)} %collective-permute-done.4.got.got8, f32[8,128]{1,0:T(8,128)S(1)} %get-tuple-element.60.turn, ...), custom_call_target="tpu_custom_call" | custom-call | bytes 1048576 | tf_op jit(solution)/shard_map/pallas_call | solution.py:482
Async XLA Ops:
  1.3 11.5 %collective-permute-start = (f32[2,8,80]{2,1,0:T(8,128)S(1)}, f32[2,8,80]{2,1,0:T(8,128)S(1)}, u32[]{:S(2)}, u32[]{:S(2)}) collective-permute-start(f32[2,8,80]{2,1,0:T(8,128)S(1)} %get-tuple-element.41), channel_id=1, source_target_pairs={{0,7},{1,2},{2,1},{3,4},{4,3},{5,6},{6,5},{7,0},{8,15},{9,10},{10,... | collective-permute-start | bytes 15368 | tf_op jit(solution)/shard_map/ppermute | solution.py:521
  8.4 4.5 %collective-permute-start.1 = (f32[2,8,80]{2,1,0:T(8,128)S(1)}, f32[2,8,80]{2,1,0:T(8,128)S(1)}, u32[]{:S(2)}, u32[]{:S(2)}) collective-permute-start(f32[2,8,80]{2,1,0:T(8,128)S(1)} %get-tuple-element.42), channel_id=1, source_target_pairs={{0,1},{1,0},{2,3},{3,2},{4,5},{5,4},{6,7},{7,6},{8,9},{9,8},{10,11... | collective-permute-start | bytes 15368 | tf_op jit(solution)/shard_map/ppermute | solution.py:522
  10.3 5.2 %collective-permute-start.2 = (f32[2,8,80]{2,1,0:T(8,128)S(1)}, f32[2,8,80]{2,1,0:T(8,128)S(1)}, u32[]{:S(2)}, u32[]{:S(2)}) collective-permute-start(f32[2,8,80]{2,1,0:T(8,128)S(1)} %get-tuple-element.39.ahead), channel_id=1, source_target_pairs={{64,8},{128,72},{192,136},{256,200},{320,264},{384,328},{448,392},... | collective-permute-start | bytes 15368 | tf_op jit(solution)/shard_map/ppermute | solution.py:523
  11.6 3.9 %copy-start = (f32[1,1,2,80,80]{4,3,2,1,0:T(8,128)S(1)}, f32[1,1,2,80,80]{4,3,2,1,0:T(8,128)}, u32[]{:S(2)}) copy-start(f32[1,1,2,80,80]{4,3,2,1,0:T(8,128)} %west.1) | copy-start | bytes 153604
  11.6 3.9 %copy-start.1 = (f32[1,1,2,80,80]{4,3,2,1,0:T(8,128)S(1)}, f32[1,1,2,80,80]{4,3,2,1,0:T(8,128)}, u32[]{:S(2)}) copy-start(f32[1,1,2,80,80]{4,3,2,1,0:T(8,128)} %east.1) | copy-start | bytes 153604
  16.2 3.5 %collective-permute-start.3 = (f32[488,128]{1,0:T(8,128)S(1)}, f32[488,128]{1,0:T(8,128)S(1)}, u32[]{:S(2)}, u32[]{:S(2)}) collective-permute-start(f32[488,128]{1,0:T(8,128)S(1)} %get-tuple-element.44.own.one), channel_id=1, source_target_pairs={{0,8},{8,0},{16,24},{24,16},{32,40},{40,32},{48,56},{56,48},{64,72... | collective-permute-start | bytes 749576 | tf_op jit(solution)/shard_map/ppermute | solution.py:531
  42.7 7.6 %collective-permute-start.4 = (f32[328,128]{1,0:T(8,128)S(1)}, f32[328,128]{1,0:T(8,128)S(1)}, u32[]{:S(2)}, u32[]{:S(2)}) collective-permute-start(f32[328,128]{1,0:T(8,128)S(1)} %get-tuple-element.47.own), channel_id=1, source_target_pairs={{0,64},{8,72},{16,80},{24,88},{32,96},{40,104},{48,112},{56,120},{... | collective-permute-start | bytes 503816 | tf_op jit(solution)/shard_map/ppermute | solution.py:531

commit v6 on v5

--- a/solution.py
+++ b/solution.py
@@ -185,7 +185,7 @@
     return jnp.concatenate([before, rows, after], axis=0).T
 
 
-def make_maps(inv, low, up, rhs, coupled, flag, own):
+def make_maps(inv, low, up, rhs, west, east, coupled, flag, own):
     tables = jnp.concatenate([span_pick(0, LANES), span_pick(3, LANES), stream_pick(3, LANES)], axis=1)
     lane = lane_of((FACE, LANES))
     made, corners = [], []
@@ -196,7 +196,8 @@
         cut = pick(both, tables)
         for i in range(2):
             at = LONG + (2 * n + i) * 2 * FACE
-            own[at : at + 2 * FACE] = cut[:, i * LANES : (i + 1) * LANES]
+            block = (west, east)[i][0, 0, n]
+            own[at : at + 2 * FACE] = dot(cut[:, i * LANES : (i + 1) * LANES], tall(widen(block)))
         corners.append(cut[:FACE, 2 * LANES :])
         ahead, down = z[:FACE], z[FACE:]
         made.append(
@@ -218,11 +219,12 @@
     return jnp.full((8, LANES), which[0, 0, 0].astype(F32), F32)
 
 
-def faces_kernel(
-    guess_hbm, up_hbm, map_hbm, inv_hbm, low_hbm, rhs_hbm, place, along,
-    near, far, lag, swap, upper, inv, low, up, rhs, guess, which, sems,
+def first_kernel(
+    guess_hbm, up_hbm, map_hbm, inv_hbm, low_hbm, rhs_hbm, west_hbm, east_hbm, place, along,
+    lag, swap, upper, inv, low, up, rhs, west, east, guess, which, sems,
 ):
     pairs = [(guess_hbm, guess), (up_hbm, up), (map_hbm, which), (inv_hbm, inv), (low_hbm, low), (rhs_hbm, rhs)]
+    pairs += [(west_hbm, west), (east_hbm, east)]
     copies = [pltpu.make_async_copy(a, b, sems.at[i]) for i, (a, b) in enumerate(pairs)]
     for copy in copies:
         copy.start()
@@ -230,41 +232,37 @@
         bit = (place[0] >> level) & 1
         upper[level] = jnp.full((8, LANES), bit.astype(F32), F32)
     upper[LEVELS] = jnp.full((8, LANES), (along[0] & 1).astype(F32), F32)
-    odd = upper[LEVELS][:, :FACE] > 0.5
-    tables = jnp.concatenate([stream_pick(0, LANES), span_pick(0, LANES), span_pick(3, LANES)], axis=1)
+    pin = stream_pick(0)
     for copy in copies[:3]:
         copy.wait()
-    both = pick(jnp.concatenate([guess[0, 0, :, n, :] for n in range(2)], axis=0), tables)
+    both = pick(jnp.concatenate([guess[0, 0, :, n, :] for n in range(2)], axis=0), pin)
     flag = flag_of(which)
     swap[...] = flag
     swapped = flag[:, :FACE] > 0.5
     made = []
     for n in range(2):
-        mine = both[8 * n : 8 * n + 8]
-        west = mine[:, LANES : LANES + FACE]
-        east = mine[:, 2 * LANES : 2 * LANES + FACE]
-        near[n] = jnp.where(odd, west, east)
-        far[n] = jnp.where(odd, east, west)
-        made.append(dot(mine[:, :FACE], up[0, 0, n], NT))
+        made.append(dot(both[8 * n : 8 * n + 8], up[0, 0, n], NT))
     for p in range(2):
         lag[p] = jnp.where(swapped, made[1 - p], made[p])
     for copy in copies[3:]:
         copy.wait()
 
 
-def maps_kernel(inv, low, up, rhs, ahead, swap, own):
-    make_maps(inv, low, up, rhs, ahead, swap[...], own)
-
-
-def vectors_kernel(maps, west, east, upper, from_far, from_near, relayed, own, terms):
-    odd = upper[LEVELS][:, :FACE] > 0.5
+def maps_kernel(inv, low, up, rhs, west, east, ahead, swap, own):
+    make_maps(inv, low, up, rhs, west, east, ahead, swap[...], own)
+
+
+def vectors_kernel(maps, upper, from_far, from_near, relayed, own, terms):
+    odd = upper[LEVELS][:1, :1] > 0.5
+    near = jnp.concatenate([from_near[0, 0, :, n, :] for n in range(2)], axis=0)
+    far = jnp.concatenate([from_far[0, 0, :, n, :] for n in range(2)], axis=0)
+    from_west = pick(jnp.where(odd, near, far), span_pick(3))
+    from_east = pick(jnp.where(odd, far, near), span_pick(0))
+    terms[0], terms[1] = from_west, from_east
     b, e = [], []
     for n in range(2):
-        from_w = dot(jnp.where(odd, from_near[n], from_far[n]), west[0, 0, n], NT)
-        from_e = dot(jnp.where(odd, from_far[n], from_near[n]), east[0, 0, n], NT)
-        terms[0, 8 * n : 8 * n + 8] = from_w
-        terms[1, 8 * n : 8 * n + 8] = from_e
-        sides = jnp.concatenate([side(from_w), side(from_e)], axis=1)
+        rows = slice(8 * n, 8 * n + 8)
+        sides = jnp.concatenate([side(from_west[rows]), side(from_east[rows])], axis=1)
         at = LONG + 2 * n * 2 * FACE
         cuts = jnp.concatenate([maps[at + i * 2 * FACE : at + (i + 1) * 2 * FACE] for i in range(2)], axis=1)
         both = dot(cuts, sides, NT)
@@ -279,10 +277,14 @@
     write_tails(own, tails_of(maps))
 
 
-def rest_kernel(inv, low, rhs, terms, zin, zout, base):
+def rest_kernel(inv, low, rhs, west, east, terms, zin, zout, base):
     pout = stream_pick(3, LANES)
     lane = lane_of((DOF, LANES))
-    halo = pick(terms[0], span_pick(0), NT) + pick(terms[1], span_pick(3), NT)
+    made = [
+        jnp.concatenate([dot(terms[i, 8 * n : 8 * n + 8], block[0, 0, n], NT) for n in range(2)], axis=0)
+        for i, block in enumerate((west, east))
+    ]
+    halo = pick(made[0], span_pick(0), NT) + pick(made[1], span_pick(3), NT)
     for n in range(2):
         m = inv[0, 0, n]
         h = rhs[0, 0, :, n, :] - halo[8 * n : 8 * n + 8]
@@ -415,57 +417,68 @@
     def chain(i, p, tile):
         return got[2 * i + p, tile * FACE : (tile + 1) * FACE]
 
+    def stack(*parts):
+        return jnp.concatenate(parts, axis=0)
+
+    def beside(*parts):
+        return jnp.concatenate(parts, axis=1)
+
     segs = [
         Segment([chain(i, p, 0) for p in range(2)], [chain(i, p, 1) for p in range(2)], got[2 * i, 2 * FACE :])
         for i in range(4)
     ]
-    zero = jnp.zeros((FACE, LANES), F32)
-    t, ahead = [[zero, zero]], [None]
-    first = [vec_only(segs[0].left[p]) for p in range(2)]
-    t.append([behind(segs[0].swap, first, p) for p in range(2)])
-    for i in (1, 2, 3):
-        through, down = [], []
-        for p in range(2):
-            left, right = segs[i].left[p], segs[i].right[p]
-            both = dot(jnp.concatenate([unpack_d(left, right), left], axis=0), tall(t[i][p]))
-            down.append(both[:FACE] + vec_only(right))
-            through.append(vec_only(both[FACE:] + left))
-        ahead.append(down)
-        if i < 3:
-            t.append([behind(segs[i].swap, through, p) for p in range(2)])
-    c = [None, None, None, [zero, zero]]
-    for i in (2, 1, 0):
-        arriving = [
-            vec_only(ahead[i + 1][p] + (dot(segs[i + 1].right[p], tall(c[i + 1][p])) if i < 2 else 0.0))
-            for p in range(2)
-        ]
-        c[i] = [behind(segs[i].swap, arriving, p) for p in range(2)]
-
-    def here(pairs):
-        low, high = upper[4][:1] > 0.5, upper[5][:1] > 0.5
-        return [
-            jnp.where(high, jnp.where(low, pairs[3][p], pairs[2][p]), jnp.where(low, pairs[1][p], pairs[0][p]))
-            for p in range(2)
-        ]
-
-    t_in, c_out = here(t), here(c)
+    d = [None] + [[unpack_d(segs[i].left[p], segs[i].right[p]) for p in range(2)] for i in (1, 2, 3)]
+    w0, w1, w2 = [seg.swap for seg in segs[:3]]
     mine, other = Segment.of(own), Segment.of(got8)
     up = upper[3][:1] > 0.5
-    lower = [jnp.where(up, other.left[p], mine.left[p]) for p in range(2)]
-    swap = jnp.where(up, other.swap, mine.swap)
-    middle = [vec_only(dot(lower[p], tall(t_in[p])) + lower[p]) for p in range(2)]
+    zero = jnp.zeros((FACE, LANES), F32)
+
+    t1 = [behind(w0, [vec_only(segs[0].left[q]) for q in range(2)], p) for p in range(2)]
+    steps = [dot(stack(d[1][p], segs[1].left[p]), tall(t1[p])) for p in range(2)]
+    down1 = [steps[p][:FACE] + vec_only(segs[1].right[p]) for p in range(2)]
+    t2 = [vec_only(steps[p][FACE:] + segs[1].left[p]) for p in range(2)]
+    t2 = [behind(w1, t2, p) for p in range(2)]
+    turned = [
+        dot(behind(w2, d[3], p), tall(segs[2].left[p])) + vec_only(behind(w2, segs[3].right, p)) for p in range(2)
+    ]
+    both_back = [dot(segs[1].right[p], tall(behind(w1, segs[2].right, p))) for p in range(2)]
+    near_right = [behind(mine.swap, other.right, p) for p in range(2)]
+    near_d = [unpack_d(other.left[p], other.right[p]) for p in range(2)]
+    near_back = [
+        dot(behind(mine.swap, near_d, p), tall(mine.left[p])) + vec_only(near_right[p]) for p in range(2)
+    ]
+
+    steps = [dot(stack(d[2][p], turned[p], segs[2].left[p]), tall(t2[p])) for p in range(2)]
+    down2 = [vec_only(steps[p][:FACE]) for p in range(2)]
+    c2 = [vec_only(steps[p][FACE : 2 * FACE] + turned[p]) for p in range(2)]
+    t3 = [vec_only(steps[p][2 * FACE :] + segs[2].left[p]) for p in range(2)]
+    t3 = [behind(w2, t3, p) for p in range(2)]
+
+    c1 = [vec_only(dot(segs[2].right[p], tall(c2[p])) + down2[p] + segs[2].right[p]) for p in range(2)]
+    c1 = [behind(w1, c1, p) for p in range(2)]
+    c0 = []
+    for p in range(2):
+        made = dot(
+            beside(both_back[p], segs[1].right[p]), stack(tall(behind(w1, c2, p)), tall(behind(w1, down2, p)))
+        )
+        c0.append(vec_only(made + both_back[p] + down1[p]))
+    c0 = [behind(w0, c0, p) for p in range(2)]
+
+    def here(a, b, c, e):
+        low, high = upper[4][:1] > 0.5, upper[5][:1] > 0.5
+        return [jnp.where(high, jnp.where(low, e[p], c[p]), jnp.where(low, b[p], a[p])) for p in range(2)]
+
+    t_in = here([zero, zero], t1, t2, t3)
+    c_out = here(c0, c1, c2, [zero, zero])
+    through = [vec_only(dot(other.left[p], tall(t_in[p])) + other.left[p]) for p in range(2)]
     t_at, c_at = [], []
     for p in range(2):
-        left, right = behind(mine.swap, other.left, p), behind(mine.swap, other.right, p)
-        back = dot(
-            jnp.concatenate([unpack_d(left, right), right], axis=1),
-            jnp.concatenate([tall(middle[p]), tall(c_out[p])], axis=0),
-        )
-        t_at.append(jnp.where(up, behind(swap, middle, p), t_in[p]))
-        c_at.append(jnp.where(up, behind(swap, c_out, p), vec_only(back + right)))
+        back = dot(beside(near_back[p], near_right[p]), stack(tall(t_in[p]), tall(c_out[p])))
+        t_at.append(jnp.where(up, behind(other.swap, through, p), t_in[p]))
+        c_at.append(jnp.where(up, behind(other.swap, c_out, p), vec_only(back + near_back[p])))
     for n in range(2):
         rows = [widen(behind(turn[...], pair, n).T[VEC:REST]) for pair in (t_at, c_at)]
-        out[:, n, :] = fixed[n] - dot(jnp.concatenate(rows, axis=1), free[n], NT)
+        out[:, n, :] = fixed[n] - dot(beside(*rows), free[n], NT)
 
 
 HBM = pl.BlockSpec(memory_space=pltpu.HBM)
@@ -506,25 +519,25 @@
     layers = lax.axis_size("stream")
     place = lax.axis_index("stream").astype(jnp.int32).reshape(1)
     along = lax.axis_index("span").astype(jnp.int32).reshape(1)
-    face = f32(2, 8, FACE)
-    args = (guess, upper_block, inflow_map, inverse_diag, lower_block, rhs_field)
-    near_face, far_face, ahead, swap, upper, inv, low, up, rhs = call(
-        faces_kernel,
+    from_far = lax.ppermute(guess, "span", [(i, (i - 1 + 2 * (i & 1)) % wide) for i in range(wide)])
+    from_near = lax.ppermute(guess, "span", [(i, i ^ 1) for i in range(wide)])
+    args = (guess, upper_block, inflow_map, inverse_diag, lower_block, rhs_field, west_block, east_block)
+    ahead, swap, upper, inv, low, up, rhs, west, east = call(
+        first_kernel,
         (
-            face, face, face, f32(8, LANES), f32(LEVELS + 1, 8, LANES),
-            *(f32(*a.shape) for a in (inverse_diag, lower_block, upper_block, rhs_field)),
+            f32(2, 8, FACE), f32(8, LANES), f32(LEVELS + 1, 8, LANES),
+            *(f32(*a.shape) for a in (inverse_diag, lower_block, upper_block, rhs_field, west_block, east_block)),
         ),
         *args, place, along,
-        hbm=range(6), smem=(6, 7),
-        scratch=(pltpu.VMEM(guess.shape, F32), pltpu.SMEM(inflow_map.shape, jnp.int32), pltpu.SemaphoreType.DMA((6,))),
-    )
-    from_far = lax.ppermute(far_face, "span", [(i, (i - 1 + 2 * (i & 1)) % wide) for i in range(wide)])
-    from_near = lax.ppermute(near_face, "span", [(i, i ^ 1) for i in range(wide)])
+        hbm=range(8), smem=(8, 9),
+        scratch=(pltpu.VMEM(guess.shape, F32), pltpu.SMEM(inflow_map.shape, jnp.int32), pltpu.SemaphoreType.DMA((8,))),
+    )
+    maps = call(maps_kernel, f32(LONG + 8 * FACE, LANES), inv, low, up, rhs, west, east, ahead, swap)
+    ahead, maps = lax.optimization_barrier((ahead, maps))
     relayed = lax.ppermute(ahead, "stream", [(i + 8, i + 1) for i in range(0, layers - 8, 8)])
-    maps = call(maps_kernel, f32(LONG + 8 * FACE, LANES), inv, low, up, rhs, ahead, swap)
     own, terms = call(
         vectors_kernel, (f32(LONG, LANES), f32(2, 16, FACE)),
-        maps, west_block, east_block, upper, from_far, from_near, relayed,
+        maps, upper, from_far, from_near, relayed,
     )
 
     def across(x, distance):
@@ -543,7 +556,7 @@
     got8 = across(eight, 8)
     spot, turn = call(four_place_kernel, here, place, upper, own, got, lefts, chains, pair_lefts, halves, smem=(0,))
     terms, eight = lax.optimization_barrier((terms, eight))
-    zin, zout, base = call(rest_kernel, tuple(f32(2, DOF, LANES) for _ in range(3)), inv, low, rhs, terms)
+    zin, zout, base = call(rest_kernel, tuple(f32(2, DOF, LANES) for _ in range(3)), inv, low, rhs, west, east, terms)
     fixed, free = call(
         answer_kernel, (f32(2, 8, DOF), f32(2, DOF, 2 * LANES)), spot, turn, zin, zout, base
     )

time: 72.9 us -> 71.6 us (0.982)
  blocking collectives: 40.1 us -> 37.9 us
  waiting for transfers between devices: 4.48 us -> 5.71 us
    all_gather x1, blocking collectives: 20.7 us -> 18.5 us  [per_device(): chains = lax.all_gather(chain, 'stream', axis_index_groups=groups)]
    ppermute x1, waiting for transfers between devices: 2.65 us -> 3.67 us  [per_device(): lax.ppermute(ahead, 'stream', [(i + 8, i + 1) for i in range(0, layers -...]
  transfers between devices with their start and end apart: 5 -> 5, of which waited for: 3 -> 3; matrix products, arithmetic and copies ran while one was open for 0% -> 0% of each run, Pallas kernels for 7% -> 9%
where the time goes in v6:
time: 71.6 us; the launch traced here: 71.4 us
  blocking collectives  37.9 us (53%)
  starting transfers between devices  15.4 us (22%)
  Pallas kernels  12.3 us (17%)
  waiting for transfers between devices  5.71 us (8%)
    all_gather x1, blocking collectives, per_device(): sixteens = lax.all_gather(chain, 'stream', axis_index_groups=groups)  19.4 us
    all_gather x1, blocking collectives, per_device(): chains = lax.all_gather(chain, 'stream', axis_index_groups=groups)  18.5 us
    pallas_call x10, Pallas kernels, call(): pl.pallas_call(kernel, out_shape=out_shape, in_specs=specs, out_specs=tup...  12.3 us
    ppermute x2, starting transfers between devices, across(): return lax.ppermute(x, 'stream', [(i, i ^ distance) for i in range(layers)])  5.13 us
    ppermute x1, starting transfers between devices, per_device(): from_near = lax.ppermute(guess, 'span', [(i, i ^ 1) for i in range(wide)])  4.82 us
    ppermute x1, starting transfers between devices, per_device(): lax.ppermute(guess, 'span', [(i, (i - 1 + 2 * (i & 1)) % wide) for i in r...  4.11 us
    ppermute x1, waiting for transfers between devices, per_device(): lax.ppermute(ahead, 'stream', [(i + 8, i + 1) for i in range(0, layers -...  3.67 us
    ppermute x2, waiting for transfers between devices, across(): return lax.ppermute(x, 'stream', [(i, i ^ distance) for i in range(layers)])  2.03 us
  transfers between devices with their start and end apart: 5, of which 3 were waited for; matrix products, arithmetic and copies ran while one was open for 0% of the time, Pallas kernels for 9%

profile of v6, /device:TPU:1, one launch (start us, length us, event | category | flops | bytes accessed | tf_op | source)
XLA Modules:
  0.0 71.4 jit_solution(16493851676839954479)
XLA Ops:
  0.0 4.8 %collective-permute-start.1 = (f32[1,1,8,2,320]{4,3,2,1,0:T(2,128)}, f32[1,1,8,2,320]{4,3,2,1,0:T(2,128)S(1)}, u32[]{:S(2)}, u32[]{:S(2)}) collective-permute-start(f32[1,1,8,2,320]{4,3,2,1,0:T(2,128)} %guess_hbm.1), channel_id=1, source_target_pairs={{0,1},{1,0},{2,3},{3,2},{4,5},{5,4},{6,7},{7,6},{8,9},{9,8},{10,11... | collective-permute-start | bytes 61448 | tf_op jit(solution)/shard_map/ppermute | solution.py:523
  4.8 4.1 %collective-permute-start = (f32[1,1,8,2,320]{4,3,2,1,0:T(2,128)}, f32[1,1,8,2,320]{4,3,2,1,0:T(2,128)S(1)}, u32[]{:S(2)}, u32[]{:S(2)}) collective-permute-start(f32[1,1,8,2,320]{4,3,2,1,0:T(2,128)} %guess_hbm.1), channel_id=1, source_target_pairs={{0,7},{1,2},{2,1},{3,4},{4,3},{5,6},{6,5},{7,0},{8,15},{9,10},{10,... | collective-permute-start | bytes 61448 | tf_op jit(solution)/shard_map/ppermute | solution.py:522
  9.0 1.4 %shard_map.82 = (f32[2,8,80]{2,1,0:T(8,128)S(1)}, f32[8,128]{1,0:T(8,128)S(1)}, f32[7,8,128]{2,1,0:T(8,128)S(1)}, f32[1,1,2,320,320]{4,3,2,1,0:T(8,128)S(1)}, f3...) custom-call(f32[1,1,8,2,320]{4,3,2,1,0:T(2,128)} %guess_hbm.1, ...), custom_call_target="tpu_custom_call" | custom-call | bytes 1048576 | tf_op jit(solution)/shard_map/pallas_call | solution.py:495
  10.3 1.5 %shard_map.83.maps = f32[1128,128]{1,0:T(8,128)S(1)} custom-call(f32[1,1,2,320,320]{4,3,2,1,0:T(8,128)S(1)} %get-tuple-element.38.inv, f32[1,1,2,80,80]{4,3,2,1,0:T(8,128)S(1)} %get-tuple-element.39.low, f32[1,1,2,80,80]{4,3,2,1,0:T(8,128)S(1)} %get-tuple-element.40.up, f32[1,1,8,2,320]{4,3,2,1,0:T(2,128)S(1)} %get-tuple-element.41.rhs, ...), custom_call_target="tpu_custom_call" | custom-call | bytes 1048576 | tf_op jit(solution)/shard_map/pallas_call | solution.py:495
  11.9 1.3 %collective-permute-start.2 = (f32[2,8,80]{2,1,0:T(8,128)S(1)}, f32[2,8,80]{2,1,0:T(8,128)S(1)}, u32[]{:S(2)}, u32[]{:S(2)}) collective-permute-start(f32[2,8,80]{2,1,0:T(8,128)S(1)} %get-tuple-element.46.ahead), channel_id=1, source_target_pairs={{64,8},{128,72},{192,136},{256,200},{320,264},{384,328},{448,392},... | collective-permute-start | bytes 15368 | tf_op jit(solution)/shard_map/ppermute | solution.py:537
  13.2 3.7 %collective-permute-done.2.relayed = f32[2,8,80]{2,1,0:T(8,128)S(1)} collective-permute-done((f32[2,8,80]{2,1,0:T(8,128)S(1)}, f32[2,8,80]{2,1,0:T(8,128)S(1)}, u32[]{:S(2)}, u32[]{:S(2)}) %collective-permute-start.2) | collective-permute-done | bytes 5152 | tf_op jit(solution)/shard_map/ppermute | solution.py:537
  16.8 0.0 collective-permute-done.1.from_near
  16.8 0.0 collective-permute-done.from_far
  16.8 0.5 shard_map.84
  17.3 1.9 %collective-permute-start.3 = (f32[488,128]{1,0:T(8,128)S(1)}, f32[488,128]{1,0:T(8,128)S(1)}, u32[]{:S(2)}, u32[]{:S(2)}) collective-permute-start(f32[488,128]{1,0:T(8,128)S(1)} %get-tuple-element.48.own.one), channel_id=1, source_target_pairs={{0,8},{8,0},{16,24},{24,16},{32,40},{40,32},{48,56},{56,48},{64,72... | collective-permute-start | bytes 749576 | tf_op jit(solution)/shard_map/ppermute | solution.py:544
  19.2 1.5 %collective-permute-done.3.got.one_got = f32[488,128]{1,0:T(8,128)S(1)} collective-permute-done((f32[488,128]{1,0:T(8,128)S(1)}, f32[488,128]{1,0:T(8,128)S(1)}, u32[]{:S(2)}, u32[]{:S(2)}) %collective-permute-start.3) | collective-permute-done | bytes 249888 | tf_op jit(solution)/shard_map/ppermute | solution.py:544
  20.7 0.7 %shard_map.85 = (f32[248,128]{1,0:T(8,128)S(1)}, f32[2,80,128]{2,1,0:T(8,128)S(1)}) custom-call(f32[7,8,128]{2,1,0:T(8,128)S(1)} %get-tuple-element.36.upper, f32[488,128]{1,0:T(8,128)S(1)} %get-tuple-element.48.own.one, f32[488,128]{1,0:T(8,128)S(1)} %collective-permute-done.3.got.one_got, f32[2,8,80]{2,1,0:T(8,128)S(1)} %collective-permute-done.2.relayed), custom_call_target="tpu_custom_call" | custom-call | bytes 1048576 | tf_op jit(solution)/shard_map/pallas_call | solution.py:495
  21.4 18.5 %all-gather = f32[1984,128]{1,0:T(8,128)S(1)} all-gather(f32[248,128]{1,0:T(8,128)S(1)} %get-tuple-element.49), channel_id=2, replica_groups={{0,8,16,24,32,40,48,56},{64,72,80,88,96,104,112,120},{128,136,144,152,1..., dimensions={0}, use_global_device_ids=true | all-gather | bytes 1142784 | tf_op jit(solution)/shard_map/all_gather | solution.py:551
  40.0 1.6 %shard_map.86 = (f32[328,128]{1,0:T(8,128)S(1)}, f32[2,328,128]{2,1,0:T(8,128)S(1)}, f32[4,2,80,128]{3,2,1,0:T(8,128)S(1)}) custom-call(f32[8,248,128]{2,1,0:T(8,128)S(1)} %bitcast.5), custom_call_target="tpu_custom_call" | custom-call | bytes 1048576 | tf_op jit(solution)/shard_map/pallas_call | solution.py:495
  41.5 3.2 %collective-permute-start.4 = (f32[328,128]{1,0:T(8,128)S(1)}, f32[328,128]{1,0:T(8,128)S(1)}, u32[]{:S(2)}, u32[]{:S(2)}) collective-permute-start(f32[328,128]{1,0:T(8,128)S(1)} %get-tuple-element.51.own), channel_id=1, source_target_pairs={{0,64},{8,72},{16,80},{24,88},{32,96},{40,104},{48,112},{56,120},{... | collective-permute-start | bytes 503816 | tf_op jit(solution)/shard_map/ppermute | solution.py:544
  44.8 1.4 %shard_map.88 = (f32[2,320,128]{2,1,0:T(8,128)S(1)}, f32[2,320,128]{2,1,0:T(8,128)S(1)}, f32[2,320,128]{2,1,0:T(8,128)S(1)}) custom-call(f32[1,1,2,320,320]{4,3,2,1,0:T(8,128)S(1)} %get-tuple-element.38.inv, f32[1,1,2,80,80]{4,3,2,1,0:T(8,128)S(1)} %get-tuple-element.39.low, f32[1,1,8,2,320]{4,3,2,1,0:T(2,128)S(1)} %get-tuple-element.41.rhs, ...), custom_call_target="tpu_custom_call" | custom-call | bytes 1048576 | tf_op jit(solution)/shard_map/pallas_call | solution.py:495
  46.2 1.9 %shard_map.87 = (f32[2,3,80,128]{3,2,1,0:T(8,128)S(1)}, f32[8,128]{1,0:T(8,128)S(1)}) custom-call(s32[1]{0:T(128)} %bitcast.place.at, f32[7,8,128]{2,1,0:T(8,128)S(1)} %get-tuple-element.36.upper, f32[488,128]{1,0:T(8,128)S(1)} %get-tuple-element.48.own.one, f32[488,128]{1,0:T(8,128)S(1)} %collective-permute-done.3.got.one_got, ...), custom_call_target="tpu_custom_call" | custom-call | bytes 1048576 | tf_op jit(solution)/shard_map/pallas_call | solution.py:495
  48.1 0.6 shard_map.89
  48.6 0.5 collective-permute-done.4.got.got8
  49.2 0.6 shard_map.90
  49.8 19.4 %all-gather.1 = f32[1344,128]{1,0:T(8,128)S(1)} all-gather(f32[168,128]{1,0:T(8,128)S(1)} %shard_map.90), channel_id=3, replica_groups={{0,8,128,136,256,264,384,392},{16,24,144,152,272,280,400,408},{32,40,16..., dimensions={0}, use_global_device_ids=true | all-gather | bytes 774144 | tf_op jit(solution)/shard_map/all_gather | solution.py:570
  69.1 2.3 %shard_map.91 = f32[8,2,320]{2,1,0:T(2,128)} custom-call(f32[7,8,128]{2,1,0:T(8,128)S(1)} %get-tuple-element.36.upper, f32[8,168,128]{2,1,0:T(8,128)S(1)} %bitcast.7, f32[328,128]{1,0:T(8,128)S(1)} %get-tuple-element.51.own, f32[328,128]{1,0:T(8,128)S(1)} %collective-permute-done.4.got.got8, f32[8,128]{1,0:T(8,128)S(1)} %get-tuple-element.64.turn, ...), custom_call_target="tpu_custom_call" | custom-call | bytes 1048576 | tf_op jit(solution)/shard_map/pallas_call | solution.py:495
Async XLA Ops:
  0.0 16.8 %collective-permute-start.1 = (f32[1,1,8,2,320]{4,3,2,1,0:T(2,128)}, f32[1,1,8,2,320]{4,3,2,1,0:T(2,128)S(1)}, u32[]{:S(2)}, u32[]{:S(2)}) collective-permute-start(f32[1,1,8,2,320]{4,3,2,1,0:T(2,128)} %guess_hbm.1), channel_id=1, source_target_pairs={{0,1},{1,0},{2,3},{3,2},{4,5},{5,4},{6,7},{7,6},{8,9},{9,8},{10,11... | collective-permute-start | bytes 61448 | tf_op jit(solution)/shard_map/ppermute | solution.py:523
  4.8 12.0 %collective-permute-start = (f32[1,1,8,2,320]{4,3,2,1,0:T(2,128)}, f32[1,1,8,2,320]{4,3,2,1,0:T(2,128)S(1)}, u32[]{:S(2)}, u32[]{:S(2)}) collective-permute-start(f32[1,1,8,2,320]{4,3,2,1,0:T(2,128)} %guess_hbm.1), channel_id=1, source_target_pairs={{0,7},{1,2},{2,1},{3,4},{4,3},{5,6},{6,5},{7,0},{8,15},{9,10},{10,... | collective-permute-start | bytes 61448 | tf_op jit(solution)/shard_map/ppermute | solution.py:522
  11.9 5.0 %collective-permute-start.2 = (f32[2,8,80]{2,1,0:T(8,128)S(1)}, f32[2,8,80]{2,1,0:T(8,128)S(1)}, u32[]{:S(2)}, u32[]{:S(2)}) collective-permute-start(f32[2,8,80]{2,1,0:T(8,128)S(1)} %get-tuple-element.46.ahead), channel_id=1, source_target_pairs={{64,8},{128,72},{192,136},{256,200},{320,264},{384,328},{448,392},... | collective-permute-start | bytes 15368 | tf_op jit(solution)/shard_map/ppermute | solution.py:537
  17.3 3.4 %collective-permute-start.3 = (f32[488,128]{1,0:T(8,128)S(1)}, f32[488,128]{1,0:T(8,128)S(1)}, u32[]{:S(2)}, u32[]{:S(2)}) collective-permute-start(f32[488,128]{1,0:T(8,128)S(1)} %get-tuple-element.48.own.one), channel_id=1, source_target_pairs={{0,8},{8,0},{16,24},{24,16},{32,40},{40,32},{48,56},{56,48},{64,72... | collective-permute-start | bytes 749576 | tf_op jit(solution)/shard_map/ppermute | solution.py:544
  41.5 7.6 %collective-permute-start.4 = (f32[328,128]{1,0:T(8,128)S(1)}, f32[328,128]{1,0:T(8,128)S(1)}, u32[]{:S(2)}, u32[]{:S(2)}) collective-permute-start(f32[328,128]{1,0:T(8,128)S(1)} %get-tuple-element.51.own), channel_id=1, source_target_pairs={{0,64},{8,72},{16,80},{24,88},{32,96},{40,104},{48,112},{56,120},{... | collective-permute-start | bytes 503816 | tf_op jit(solution)/shard_map/ppermute | solution.py:544

commit v7 on v6

--- a/solution.py
+++ b/solution.py
@@ -252,7 +252,7 @@
     make_maps(inv, low, up, rhs, west, east, ahead, swap[...], own)
 
 
-def vectors_kernel(maps, upper, from_far, from_near, relayed, own, terms):
+def vectors_kernel(maps, upper, from_near, from_far, relayed, own, terms):
     odd = upper[LEVELS][:1, :1] > 0.5
     near = jnp.concatenate([from_near[0, 0, :, n, :] for n in range(2)], axis=0)
     far = jnp.concatenate([from_far[0, 0, :, n, :] for n in range(2)], axis=0)
@@ -533,11 +533,10 @@
         scratch=(pltpu.VMEM(guess.shape, F32), pltpu.SMEM(inflow_map.shape, jnp.int32), pltpu.SemaphoreType.DMA((8,))),
     )
     maps = call(maps_kernel, f32(LONG + 8 * FACE, LANES), inv, low, up, rhs, west, east, ahead, swap)
-    ahead, maps = lax.optimization_barrier((ahead, maps))
     relayed = lax.ppermute(ahead, "stream", [(i + 8, i + 1) for i in range(0, layers - 8, 8)])
     own, terms = call(
         vectors_kernel, (f32(LONG, LANES), f32(2, 16, FACE)),
-        maps, upper, from_far, from_near, relayed,
+        maps, upper, from_near, from_far, relayed,
     )
 
     def across(x, distance):

time: 71.6 us -> 71.1 us (level)
  waiting for transfers between devices: 5.71 us -> 4.19 us
  blocking collectives: 37.9 us -> 38.9 us
    ppermute x1, starting transfers between devices: 4.11 us -> 7.01 us  [per_device(): lax.ppermute(guess, 'span', [(i, (i - 1 + 2 * (i & 1)) % wide) for i in r...]
    ppermute x1, starting transfers between devices: 4.82 us -> 1.92 us  [per_device(): from_near = lax.ppermute(guess, 'span', [(i, i ^ 1) for i in range(wide)])]
    ppermute x1, waiting for transfers between devices: 3.67 us -> 2.16 us  [per_device(): lax.ppermute(ahead, 'stream', [(i + 8, i + 1) for i in range(0, layers -...]
    all_gather x1, blocking collectives: 18.5 us -> 19.5 us  [per_device(): chains = lax.all_gather(chain, 'stream', axis_index_groups=groups)]
  transfers between devices with their start and end apart: 5 -> 5, of which waited for: 3 -> 3; matrix products, arithmetic and copies ran while one was open for 0% -> 0% of each run, Pallas kernels for 9% -> 10%
where the time goes in v7:
time: 71.1 us; the launch traced here: 70.8 us
  blocking collectives  38.9 us (55%)
  starting transfers between devices  15.4 us (22%)
  Pallas kernels  12.3 us (17%)
  waiting for transfers between devices  4.19 us (6%)
    all_gather x1, blocking collectives, per_device(): chains = lax.all_gather(chain, 'stream', axis_index_groups=groups)  19.5 us
    all_gather x1, blocking collectives, per_device(): sixteens = lax.all_gather(chain, 'stream', axis_index_groups=groups)  19.3 us
    pallas_call x10, Pallas kernels, call(): pl.pallas_call(kernel, out_shape=out_shape, in_specs=specs, out_specs=tup...  12.3 us
    ppermute x1, starting transfers between devices, per_device(): lax.ppermute(guess, 'span', [(i, (i - 1 + 2 * (i & 1)) % wide) for i in r...  7.01 us
    ppermute x2, starting transfers between devices, across(): return lax.ppermute(x, 'stream', [(i, i ^ distance) for i in range(layers)])  5.13 us
    ppermute x1, waiting for transfers between devices, per_device(): lax.ppermute(ahead, 'stream', [(i + 8, i + 1) for i in range(0, layers -...  2.16 us
    ppermute x2, waiting for transfers between devices, across(): return lax.ppermute(x, 'stream', [(i, i ^ distance) for i in range(layers)])  2.02 us
    ppermute x1, starting transfers between devices, per_device(): from_near = lax.ppermute(guess, 'span', [(i, i ^ 1) for i in range(wide)])  1.92 us
  transfers between devices with their start and end apart: 5, of which 3 were waited for; matrix products, arithmetic and copies ran while one was open for 0% of the time, Pallas kernels for 10%

profile of v7, /device:TPU:1, one launch (start us, length us, event | category | flops | bytes accessed | tf_op | source)
XLA Modules:
  0.0 70.8 jit_solution(5009777912138562821)
XLA Ops:
  0.0 7.0 %collective-permute-start.1 = (f32[1,1,8,2,320]{4,3,2,1,0:T(2,128)}, f32[1,1,8,2,320]{4,3,2,1,0:T(2,128)S(1)}, u32[]{:S(2)}, u32[]{:S(2)}) collective-permute-start(f32[1,1,8,2,320]{4,3,2,1,0:T(2,128)} %guess_hbm.1), channel_id=1, source_target_pairs={{0,7},{1,2},{2,1},{3,4},{4,3},{5,6},{6,5},{7,0},{8,15},{9,10},{10,... | collective-permute-start | bytes 61448 | tf_op jit(solution)/shard_map/ppermute | solution.py:522
  7.0 1.9 %collective-permute-start = (f32[1,1,8,2,320]{4,3,2,1,0:T(2,128)}, f32[1,1,8,2,320]{4,3,2,1,0:T(2,128)S(1)}, u32[]{:S(2)}, u32[]{:S(2)}) collective-permute-start(f32[1,1,8,2,320]{4,3,2,1,0:T(2,128)} %guess_hbm.1), channel_id=1, source_target_pairs={{0,1},{1,0},{2,3},{3,2},{4,5},{5,4},{6,7},{7,6},{8,9},{9,8},{10,11... | collective-permute-start | bytes 61448 | tf_op jit(solution)/shard_map/ppermute | solution.py:523
  9.0 1.4 %shard_map.82 = (f32[2,8,80]{2,1,0:T(8,128)S(1)}, f32[8,128]{1,0:T(8,128)S(1)}, f32[7,8,128]{2,1,0:T(8,128)S(1)}, f32[1,1,2,320,320]{4,3,2,1,0:T(8,128)S(1)}, f3...) custom-call(f32[1,1,8,2,320]{4,3,2,1,0:T(2,128)} %guess_hbm.1, ...), custom_call_target="tpu_custom_call" | custom-call | bytes 1048576 | tf_op jit(solution)/shard_map/pallas_call | solution.py:495
  10.3 1.3 %collective-permute-start.2 = (f32[2,8,80]{2,1,0:T(8,128)S(1)}, f32[2,8,80]{2,1,0:T(8,128)S(1)}, u32[]{:S(2)}, u32[]{:S(2)}) collective-permute-start(f32[2,8,80]{2,1,0:T(8,128)S(1)} %get-tuple-element.41.ahead), channel_id=1, source_target_pairs={{64,8},{128,72},{192,136},{256,200},{320,264},{384,328},{448,392},... | collective-permute-start | bytes 15368 | tf_op jit(solution)/shard_map/ppermute | solution.py:536
  11.6 1.5 %shard_map.83.maps = f32[1128,128]{1,0:T(8,128)S(1)} custom-call(f32[1,1,2,320,320]{4,3,2,1,0:T(8,128)S(1)} %get-tuple-element.35.inv, f32[1,1,2,80,80]{4,3,2,1,0:T(8,128)S(1)} %get-tuple-element.36.low, f32[1,1,2,80,80]{4,3,2,1,0:T(8,128)S(1)} %get-tuple-element.37.up, f32[1,1,8,2,320]{4,3,2,1,0:T(2,128)S(1)} %get-tuple-element.38.rhs, ...), custom_call_target="tpu_custom_call" | custom-call | bytes 1048576 | tf_op jit(solution)/shard_map/pallas_call | solution.py:495
  13.2 2.2 %collective-permute-done.2.relayed = f32[2,8,80]{2,1,0:T(8,128)S(1)} collective-permute-done((f32[2,8,80]{2,1,0:T(8,128)S(1)}, f32[2,8,80]{2,1,0:T(8,128)S(1)}, u32[]{:S(2)}, u32[]{:S(2)}) %collective-permute-start.2) | collective-permute-done | bytes 5152 | tf_op jit(solution)/shard_map/ppermute | solution.py:536
  15.3 0.0 collective-permute-done.1.from_far
  15.3 0.0 collective-permute-done.from_near
  15.3 0.5 shard_map.84
  15.8 1.9 %collective-permute-start.3 = (f32[488,128]{1,0:T(8,128)S(1)}, f32[488,128]{1,0:T(8,128)S(1)}, u32[]{:S(2)}, u32[]{:S(2)}) collective-permute-start(f32[488,128]{1,0:T(8,128)S(1)} %get-tuple-element.44.own.one), channel_id=1, source_target_pairs={{0,8},{8,0},{16,24},{24,16},{32,40},{40,32},{48,56},{56,48},{64,72... | collective-permute-start | bytes 749576 | tf_op jit(solution)/shard_map/ppermute | solution.py:543
  17.7 1.5 %collective-permute-done.3.got.one_got = f32[488,128]{1,0:T(8,128)S(1)} collective-permute-done((f32[488,128]{1,0:T(8,128)S(1)}, f32[488,128]{1,0:T(8,128)S(1)}, u32[]{:S(2)}, u32[]{:S(2)}) %collective-permute-start.3) | collective-permute-done | bytes 249888 | tf_op jit(solution)/shard_map/ppermute | solution.py:543
  19.2 0.7 %shard_map.85 = (f32[248,128]{1,0:T(8,128)S(1)}, f32[2,80,128]{2,1,0:T(8,128)S(1)}) custom-call(f32[7,8,128]{2,1,0:T(8,128)S(1)} %get-tuple-element.34.upper, f32[488,128]{1,0:T(8,128)S(1)} %get-tuple-element.44.own.one, f32[488,128]{1,0:T(8,128)S(1)} %collective-permute-done.3.got.one_got, f32[2,8,80]{2,1,0:T(8,128)S(1)} %collective-permute-done.2.relayed), custom_call_target="tpu_custom_call" | custom-call | bytes 1048576 | tf_op jit(solution)/shard_map/pallas_call | solution.py:495
  19.9 19.5 %all-gather = f32[1984,128]{1,0:T(8,128)S(1)} all-gather(f32[248,128]{1,0:T(8,128)S(1)} %get-tuple-element.45), channel_id=2, replica_groups={{0,8,16,24,32,40,48,56},{64,72,80,88,96,104,112,120},{128,136,144,152,1..., dimensions={0}, use_global_device_ids=true | all-gather | bytes 1142784 | tf_op jit(solution)/shard_map/all_gather | solution.py:550
  39.5 1.6 %shard_map.86 = (f32[328,128]{1,0:T(8,128)S(1)}, f32[2,328,128]{2,1,0:T(8,128)S(1)}, f32[4,2,80,128]{3,2,1,0:T(8,128)S(1)}) custom-call(f32[8,248,128]{2,1,0:T(8,128)S(1)} %bitcast.5), custom_call_target="tpu_custom_call" | custom-call | bytes 1048576 | tf_op jit(solution)/shard_map/pallas_call | solution.py:495
  41.0 3.2 %collective-permute-start.4 = (f32[328,128]{1,0:T(8,128)S(1)}, f32[328,128]{1,0:T(8,128)S(1)}, u32[]{:S(2)}, u32[]{:S(2)}) collective-permute-start(f32[328,128]{1,0:T(8,128)S(1)} %get-tuple-element.47.own), channel_id=1, source_target_pairs={{0,64},{8,72},{16,80},{24,88},{32,96},{40,104},{48,112},{56,120},{... | collective-permute-start | bytes 503816 | tf_op jit(solution)/shard_map/ppermute | solution.py:543
  44.2 1.4 %shard_map.88 = (f32[2,320,128]{2,1,0:T(8,128)S(1)}, f32[2,320,128]{2,1,0:T(8,128)S(1)}, f32[2,320,128]{2,1,0:T(8,128)S(1)}) custom-call(f32[1,1,2,320,320]{4,3,2,1,0:T(8,128)S(1)} %get-tuple-element.35.inv, f32[1,1,2,80,80]{4,3,2,1,0:T(8,128)S(1)} %get-tuple-element.36.low, f32[1,1,8,2,320]{4,3,2,1,0:T(2,128)S(1)} %get-tuple-element.38.rhs, ...), custom_call_target="tpu_custom_call" | custom-call | bytes 1048576 | tf_op jit(solution)/shard_map/pallas_call | solution.py:495
  45.7 1.9 %shard_map.87 = (f32[2,3,80,128]{3,2,1,0:T(8,128)S(1)}, f32[8,128]{1,0:T(8,128)S(1)}) custom-call(s32[1]{0:T(128)} %bitcast.place.at, f32[7,8,128]{2,1,0:T(8,128)S(1)} %get-tuple-element.34.upper, f32[488,128]{1,0:T(8,128)S(1)} %get-tuple-element.44.own.one, f32[488,128]{1,0:T(8,128)S(1)} %collective-permute-done.3.got.one_got, ...), custom_call_target="tpu_custom_call" | custom-call | bytes 1048576 | tf_op jit(solution)/shard_map/pallas_call | solution.py:495
  47.5 0.6 shard_map.89
  48.1 0.5 collective-permute-done.4.got.got8
  48.7 0.6 shard_map.90
  49.2 19.3 %all-gather.1 = f32[1344,128]{1,0:T(8,128)S(1)} all-gather(f32[168,128]{1,0:T(8,128)S(1)} %shard_map.90), channel_id=3, replica_groups={{0,8,128,136,256,264,384,392},{16,24,144,152,272,280,400,408},{32,40,16..., dimensions={0}, use_global_device_ids=true | all-gather | bytes 774144 | tf_op jit(solution)/shard_map/all_gather | solution.py:569
  68.6 2.3 %shard_map.91 = f32[8,2,320]{2,1,0:T(2,128)} custom-call(f32[7,8,128]{2,1,0:T(8,128)S(1)} %get-tuple-element.34.upper, f32[8,168,128]{2,1,0:T(8,128)S(1)} %bitcast.7, f32[328,128]{1,0:T(8,128)S(1)} %get-tuple-element.47.own, f32[328,128]{1,0:T(8,128)S(1)} %collective-permute-done.4.got.got8, f32[8,128]{1,0:T(8,128)S(1)} %get-tuple-element.60.turn, ...), custom_call_target="tpu_custom_call" | custom-call | bytes 1048576 | tf_op jit(solution)/shard_map/pallas_call | solution.py:495
Async XLA Ops:
  0.0 15.3 %collective-permute-start.1 = (f32[1,1,8,2,320]{4,3,2,1,0:T(2,128)}, f32[1,1,8,2,320]{4,3,2,1,0:T(2,128)S(1)}, u32[]{:S(2)}, u32[]{:S(2)}) collective-permute-start(f32[1,1,8,2,320]{4,3,2,1,0:T(2,128)} %guess_hbm.1), channel_id=1, source_target_pairs={{0,7},{1,2},{2,1},{3,4},{4,3},{5,6},{6,5},{7,0},{8,15},{9,10},{10,... | collective-permute-start | bytes 61448 | tf_op jit(solution)/shard_map/ppermute | solution.py:522
  7.0 8.3 %collective-permute-start = (f32[1,1,8,2,320]{4,3,2,1,0:T(2,128)}, f32[1,1,8,2,320]{4,3,2,1,0:T(2,128)S(1)}, u32[]{:S(2)}, u32[]{:S(2)}) collective-permute-start(f32[1,1,8,2,320]{4,3,2,1,0:T(2,128)} %guess_hbm.1), channel_id=1, source_target_pairs={{0,1},{1,0},{2,3},{3,2},{4,5},{5,4},{6,7},{7,6},{8,9},{9,8},{10,11... | collective-permute-start | bytes 61448 | tf_op jit(solution)/shard_map/ppermute | solution.py:523
  10.3 5.0 %collective-permute-start.2 = (f32[2,8,80]{2,1,0:T(8,128)S(1)}, f32[2,8,80]{2,1,0:T(8,128)S(1)}, u32[]{:S(2)}, u32[]{:S(2)}) collective-permute-start(f32[2,8,80]{2,1,0:T(8,128)S(1)} %get-tuple-element.41.ahead), channel_id=1, source_target_pairs={{64,8},{128,72},{192,136},{256,200},{320,264},{384,328},{448,392},... | collective-permute-start | bytes 15368 | tf_op jit(solution)/shard_map/ppermute | solution.py:536
  15.8 3.4 %collective-permute-start.3 = (f32[488,128]{1,0:T(8,128)S(1)}, f32[488,128]{1,0:T(8,128)S(1)}, u32[]{:S(2)}, u32[]{:S(2)}) collective-permute-start(f32[488,128]{1,0:T(8,128)S(1)} %get-tuple-element.44.own.one), channel_id=1, source_target_pairs={{0,8},{8,0},{16,24},{24,16},{32,40},{40,32},{48,56},{56,48},{64,72... | collective-permute-start | bytes 749576 | tf_op jit(solution)/shard_map/ppermute | solution.py:543
  41.0 7.6 %collective-permute-start.4 = (f32[328,128]{1,0:T(8,128)S(1)}, f32[328,128]{1,0:T(8,128)S(1)}, u32[]{:S(2)}, u32[]{:S(2)}) collective-permute-start(f32[328,128]{1,0:T(8,128)S(1)} %get-tuple-element.47.own), channel_id=1, source_target_pairs={{0,64},{8,72},{16,80},{24,88},{32,96},{40,104},{48,112},{56,120},{... | collective-permute-start | bytes 503816 | tf_op jit(solution)/shard_map/ppermute | solution.py:543

commit v8 on v7

--- a/solution.py
+++ b/solution.py
@@ -221,7 +221,7 @@
 
 def first_kernel(
     guess_hbm, up_hbm, map_hbm, inv_hbm, low_hbm, rhs_hbm, west_hbm, east_hbm, place, along,
-    lag, swap, upper, inv, low, up, rhs, west, east, guess, which, sems,
+    lag, swap, upper, inv, low, rhs, west, east, own, guess, up, which, sems,
 ):
     pairs = [(guess_hbm, guess), (up_hbm, up), (map_hbm, which), (inv_hbm, inv), (low_hbm, low), (rhs_hbm, rhs)]
     pairs += [(west_hbm, west), (east_hbm, east)]
@@ -246,10 +246,7 @@
         lag[p] = jnp.where(swapped, made[1 - p], made[p])
     for copy in copies[3:]:
         copy.wait()
-
-
-def maps_kernel(inv, low, up, rhs, west, east, ahead, swap, own):
-    make_maps(inv, low, up, rhs, west, east, ahead, swap[...], own)
+    make_maps(inv, low, up, rhs, west, east, lag, flag, own)
 
 
 def vectors_kernel(maps, upper, from_near, from_far, relayed, own, terms):
@@ -522,17 +519,17 @@
     from_far = lax.ppermute(guess, "span", [(i, (i - 1 + 2 * (i & 1)) % wide) for i in range(wide)])
     from_near = lax.ppermute(guess, "span", [(i, i ^ 1) for i in range(wide)])
     args = (guess, upper_block, inflow_map, inverse_diag, lower_block, rhs_field, west_block, east_block)
-    ahead, swap, upper, inv, low, up, rhs, west, east = call(
+    ahead, swap, upper, inv, low, rhs, west, east, maps = call(
         first_kernel,
         (
             f32(2, 8, FACE), f32(8, LANES), f32(LEVELS + 1, 8, LANES),
-            *(f32(*a.shape) for a in (inverse_diag, lower_block, upper_block, rhs_field, west_block, east_block)),
+            *(f32(*a.shape) for a in (inverse_diag, lower_block, rhs_field, west_block, east_block)),
+            f32(LONG + 8 * FACE, LANES),
         ),
         *args, place, along,
         hbm=range(8), smem=(8, 9),
-        scratch=(pltpu.VMEM(guess.shape, F32), pltpu.SMEM(inflow_map.shape, jnp.int32), pltpu.SemaphoreType.DMA((8,))),
-    )
-    maps = call(maps_kernel, f32(LONG + 8 * FACE, LANES), inv, low, up, rhs, west, east, ahead, swap)
+        scratch=(pltpu.VMEM(guess.shape, F32), pltpu.VMEM(upper_block.shape, F32), pltpu.SMEM(inflow_map.shape, jnp.int32), pltpu.SemaphoreType.DMA((8,))),
+    )
     relayed = lax.ppermute(ahead, "stream", [(i + 8, i + 1) for i in range(0, layers - 8, 8)])
     own, terms = call(
         vectors_kernel, (f32(LONG, LANES), f32(2, 16, FACE)),

time: 71.1 us -> 70.9 us (level)
  blocking collectives: 38.9 us -> 36.9 us
  waiting for transfers between devices: 4.19 us -> 5.71 us
    all_gather x1, blocking collectives: 19.5 us -> 17.5 us  [per_device(): chains = lax.all_gather(chain, 'stream', axis_index_groups=groups)]
    ppermute x1, waiting for transfers between devices: 2.16 us -> 3.67 us  [per_device(): lax.ppermute(ahead, 'stream', [(i + 8, i + 1) for i in range(0, layers -...]
    pallas_call x10 -> x9, Pallas kernels: 12.3 us -> 12.6 us  [call(): pl.pallas_call(kernel, out_shape=out_shape, in_specs=specs, out_specs=tup...]
where the time goes in v8:
time: 70.9 us; the launch traced here: 70.7 us
  blocking collectives  36.9 us (52%)
  starting transfers between devices  15.3 us (22%)
  Pallas kernels  12.6 us (18%)
  waiting for transfers between devices  5.71 us (8%)
    all_gather x1, blocking collectives, per_device(): sixteens = lax.all_gather(chain, 'stream', axis_index_groups=groups)  19.4 us
    all_gather x1, blocking collectives, per_device(): chains = lax.all_gather(chain, 'stream', axis_index_groups=groups)  17.5 us
    pallas_call x9, Pallas kernels, call(): pl.pallas_call(kernel, out_shape=out_shape, in_specs=specs, out_specs=tup...  12.6 us
    ppermute x1, starting transfers between devices, per_device(): lax.ppermute(guess, 'span', [(i, (i - 1 + 2 * (i & 1)) % wide) for i in r...  7.01 us
    ppermute x2, starting transfers between devices, across(): return lax.ppermute(x, 'stream', [(i, i ^ distance) for i in range(layers)])  5.12 us
    ppermute x1, waiting for transfers between devices, per_device(): lax.ppermute(ahead, 'stream', [(i + 8, i + 1) for i in range(0, layers -...  3.67 us
    ppermute x2, waiting for transfers between devices, across(): return lax.ppermute(x, 'stream', [(i, i ^ distance) for i in range(layers)])  2.04 us
    ppermute x1, starting transfers between devices, per_device(): from_near = lax.ppermute(guess, 'span', [(i, i ^ 1) for i in range(wide)])  1.92 us
  transfers between devices with their start and end apart: 5, of which 3 were waited for; matrix products, arithmetic and copies ran while one was open for 0% of the time, Pallas kernels for 10%

profile of v8, /device:TPU:1, one launch (start us, length us, event | category | flops | bytes accessed | tf_op | source)
XLA Modules:
  0.0 70.7 jit_solution(16682423243970166217)
XLA Ops:
  0.0 7.0 %collective-permute-start.1 = (f32[1,1,8,2,320]{4,3,2,1,0:T(2,128)}, f32[1,1,8,2,320]{4,3,2,1,0:T(2,128)S(1)}, u32[]{:S(2)}, u32[]{:S(2)}) collective-permute-start(f32[1,1,8,2,320]{4,3,2,1,0:T(2,128)} %guess_hbm.1), channel_id=1, source_target_pairs={{0,7},{1,2},{2,1},{3,4},{4,3},{5,6},{6,5},{7,0},{8,15},{9,10},{10,... | collective-permute-start | bytes 61448 | tf_op jit(solution)/shard_map/ppermute | solution.py:519
  7.0 1.9 %collective-permute-start = (f32[1,1,8,2,320]{4,3,2,1,0:T(2,128)}, f32[1,1,8,2,320]{4,3,2,1,0:T(2,128)S(1)}, u32[]{:S(2)}, u32[]{:S(2)}) collective-permute-start(f32[1,1,8,2,320]{4,3,2,1,0:T(2,128)} %guess_hbm.1), channel_id=1, source_target_pairs={{0,1},{1,0},{2,3},{3,2},{4,5},{5,4},{6,7},{7,6},{8,9},{9,8},{10,11... | collective-permute-start | bytes 61448 | tf_op jit(solution)/shard_map/ppermute | solution.py:520
  9.0 3.2 %shard_map.82 = (f32[2,8,80]{2,1,0:T(8,128)S(1)}, f32[8,128]{1,0:T(8,128)}, f32[7,8,128]{2,1,0:T(8,128)S(1)}, f32[1,1,2,320,320]{4,3,2,1,0:T(8,128)S(1)}, f32[1,...) custom-call(f32[1,1,8,2,320]{4,3,2,1,0:T(2,128)} %guess_hbm.1, ...), custom_call_target="tpu_custom_call" | custom-call | bytes 1048576 | tf_op jit(solution)/shard_map/pallas_call | solution.py:492
  12.2 1.3 %collective-permute-start.2 = (f32[2,8,80]{2,1,0:T(8,128)S(1)}, f32[2,8,80]{2,1,0:T(8,128)S(1)}, u32[]{:S(2)}, u32[]{:S(2)}) collective-permute-start(f32[2,8,80]{2,1,0:T(8,128)S(1)} %get-tuple-element.35), channel_id=1, source_target_pairs={{64,8},{128,72},{192,136},{256,200},{320,264},{384,328},{448,392},... | collective-permute-start | bytes 15368 | tf_op jit(solution)/shard_map/ppermute | solution.py:533
  13.5 3.7 %collective-permute-done.2.relayed = f32[2,8,80]{2,1,0:T(8,128)S(1)} collective-permute-done((f32[2,8,80]{2,1,0:T(8,128)S(1)}, f32[2,8,80]{2,1,0:T(8,128)S(1)}, u32[]{:S(2)}, u32[]{:S(2)}) %collective-permute-start.2) | collective-permute-done | bytes 5152 | tf_op jit(solution)/shard_map/ppermute | solution.py:533
  17.1 0.0 collective-permute-done.1.from_far
  17.1 0.0 collective-permute-done.from_near
  17.1 0.5 shard_map.83
  17.6 1.9 %collective-permute-start.3 = (f32[488,128]{1,0:T(8,128)S(1)}, f32[488,128]{1,0:T(8,128)S(1)}, u32[]{:S(2)}, u32[]{:S(2)}) collective-permute-start(f32[488,128]{1,0:T(8,128)S(1)} %get-tuple-element.37.own.one), channel_id=1, source_target_pairs={{0,8},{8,0},{16,24},{24,16},{32,40},{40,32},{48,56},{56,48},{64,72... | collective-permute-start | bytes 749576 | tf_op jit(solution)/shard_map/ppermute | solution.py:540
  19.5 1.5 %collective-permute-done.3.got.one_got = f32[488,128]{1,0:T(8,128)S(1)} collective-permute-done((f32[488,128]{1,0:T(8,128)S(1)}, f32[488,128]{1,0:T(8,128)S(1)}, u32[]{:S(2)}, u32[]{:S(2)}) %collective-permute-start.3) | collective-permute-done | bytes 249888 | tf_op jit(solution)/shard_map/ppermute | solution.py:540
  21.0 0.7 %shard_map.84 = (f32[248,128]{1,0:T(8,128)S(1)}, f32[2,80,128]{2,1,0:T(8,128)S(1)}) custom-call(f32[7,8,128]{2,1,0:T(8,128)S(1)} %get-tuple-element.33.upper, f32[488,128]{1,0:T(8,128)S(1)} %get-tuple-element.37.own.one, f32[488,128]{1,0:T(8,128)S(1)} %collective-permute-done.3.got.one_got, f32[2,8,80]{2,1,0:T(8,128)S(1)} %collective-permute-done.2.relayed), custom_call_target="tpu_custom_call" | custom-call | bytes 1048576 | tf_op jit(solution)/shard_map/pallas_call | solution.py:492
  21.7 17.5 %all-gather = f32[1984,128]{1,0:T(8,128)S(1)} all-gather(f32[248,128]{1,0:T(8,128)S(1)} %get-tuple-element.38), channel_id=2, replica_groups={{0,8,16,24,32,40,48,56},{64,72,80,88,96,104,112,120},{128,136,144,152,1..., dimensions={0}, use_global_device_ids=true | all-gather | bytes 1142784 | tf_op jit(solution)/shard_map/all_gather | solution.py:547
  39.3 1.6 %shard_map.85 = (f32[328,128]{1,0:T(8,128)S(1)}, f32[2,328,128]{2,1,0:T(8,128)S(1)}, f32[4,2,80,128]{3,2,1,0:T(8,128)S(1)}) custom-call(f32[8,248,128]{2,1,0:T(8,128)S(1)} %bitcast.5), custom_call_target="tpu_custom_call" | custom-call | bytes 1048576 | tf_op jit(solution)/shard_map/pallas_call | solution.py:492
  40.8 3.2 %collective-permute-start.4 = (f32[328,128]{1,0:T(8,128)S(1)}, f32[328,128]{1,0:T(8,128)S(1)}, u32[]{:S(2)}, u32[]{:S(2)}) collective-permute-start(f32[328,128]{1,0:T(8,128)S(1)} %get-tuple-element.40.own), channel_id=1, source_target_pairs={{0,64},{8,72},{16,80},{24,88},{32,96},{40,104},{48,112},{56,120},{... | collective-permute-start | bytes 503816 | tf_op jit(solution)/shard_map/ppermute | solution.py:540
  44.1 1.4 %shard_map.87 = (f32[2,320,128]{2,1,0:T(8,128)S(1)}, f32[2,320,128]{2,1,0:T(8,128)S(1)}, f32[2,320,128]{2,1,0:T(8,128)S(1)}) custom-call(f32[1,1,2,320,320]{4,3,2,1,0:T(8,128)S(1)} %get-tuple-element.46.inv, f32[1,1,2,80,80]{4,3,2,1,0:T(8,128)S(1)} %get-tuple-element.47.low, f32[1,1,8,2,320]{4,3,2,1,0:T(2,128)S(1)} %get-tuple-element.48.rhs, ...), custom_call_target="tpu_custom_call" | custom-call | bytes 1048576 | tf_op jit(solution)/shard_map/pallas_call | solution.py:492
  45.5 1.9 %shard_map.86 = (f32[2,3,80,128]{3,2,1,0:T(8,128)S(1)}, f32[8,128]{1,0:T(8,128)S(1)}) custom-call(s32[1]{0:T(128)} %bitcast.place.at, f32[7,8,128]{2,1,0:T(8,128)S(1)} %get-tuple-element.33.upper, f32[488,128]{1,0:T(8,128)S(1)} %get-tuple-element.37.own.one, f32[488,128]{1,0:T(8,128)S(1)} %collective-permute-done.3.got.one_got, ...), custom_call_target="tpu_custom_call" | custom-call | bytes 1048576 | tf_op jit(solution)/shard_map/pallas_call | solution.py:492
  47.3 0.6 shard_map.88
  47.9 0.6 collective-permute-done.4.got.got8
  48.5 0.6 shard_map.89
  49.1 19.4 %all-gather.1 = f32[1344,128]{1,0:T(8,128)S(1)} all-gather(f32[168,128]{1,0:T(8,128)S(1)} %shard_map.89), channel_id=3, replica_groups={{0,8,128,136,256,264,384,392},{16,24,144,152,272,280,400,408},{32,40,16..., dimensions={0}, use_global_device_ids=true | all-gather | bytes 774144 | tf_op jit(solution)/shard_map/all_gather | solution.py:566
  68.4 2.3 %shard_map.90 = f32[8,2,320]{2,1,0:T(2,128)} custom-call(f32[7,8,128]{2,1,0:T(8,128)S(1)} %get-tuple-element.33.upper, f32[8,168,128]{2,1,0:T(8,128)S(1)} %bitcast.7, f32[328,128]{1,0:T(8,128)S(1)} %get-tuple-element.40.own, f32[328,128]{1,0:T(8,128)S(1)} %collective-permute-done.4.got.got8, f32[8,128]{1,0:T(8,128)S(1)} %get-tuple-element.58.turn, ...), custom_call_target="tpu_custom_call" | custom-call | bytes 1048576 | tf_op jit(solution)/shard_map/pallas_call | solution.py:492
Async XLA Ops:
  0.0 17.1 %collective-permute-start.1 = (f32[1,1,8,2,320]{4,3,2,1,0:T(2,128)}, f32[1,1,8,2,320]{4,3,2,1,0:T(2,128)S(1)}, u32[]{:S(2)}, u32[]{:S(2)}) collective-permute-start(f32[1,1,8,2,320]{4,3,2,1,0:T(2,128)} %guess_hbm.1), channel_id=1, source_target_pairs={{0,7},{1,2},{2,1},{3,4},{4,3},{5,6},{6,5},{7,0},{8,15},{9,10},{10,... | collective-permute-start | bytes 61448 | tf_op jit(solution)/shard_map/ppermute | solution.py:519
  7.0 10.1 %collective-permute-start = (f32[1,1,8,2,320]{4,3,2,1,0:T(2,128)}, f32[1,1,8,2,320]{4,3,2,1,0:T(2,128)S(1)}, u32[]{:S(2)}, u32[]{:S(2)}) collective-permute-start(f32[1,1,8,2,320]{4,3,2,1,0:T(2,128)} %guess_hbm.1), channel_id=1, source_target_pairs={{0,1},{1,0},{2,3},{3,2},{4,5},{5,4},{6,7},{7,6},{8,9},{9,8},{10,11... | collective-permute-start | bytes 61448 | tf_op jit(solution)/shard_map/ppermute | solution.py:520
  12.2 5.0 %collective-permute-start.2 = (f32[2,8,80]{2,1,0:T(8,128)S(1)}, f32[2,8,80]{2,1,0:T(8,128)S(1)}, u32[]{:S(2)}, u32[]{:S(2)}) collective-permute-start(f32[2,8,80]{2,1,0:T(8,128)S(1)} %get-tuple-element.35), channel_id=1, source_target_pairs={{64,8},{128,72},{192,136},{256,200},{320,264},{384,328},{448,392},... | collective-permute-start | bytes 15368 | tf_op jit(solution)/shard_map/ppermute | solution.py:533
  17.6 3.4 %collective-permute-start.3 = (f32[488,128]{1,0:T(8,128)S(1)}, f32[488,128]{1,0:T(8,128)S(1)}, u32[]{:S(2)}, u32[]{:S(2)}) collective-permute-start(f32[488,128]{1,0:T(8,128)S(1)} %get-tuple-element.37.own.one), channel_id=1, source_target_pairs={{0,8},{8,0},{16,24},{24,16},{32,40},{40,32},{48,56},{56,48},{64,72... | collective-permute-start | bytes 749576 | tf_op jit(solution)/shard_map/ppermute | solution.py:540
  40.8 7.6 %collective-permute-start.4 = (f32[328,128]{1,0:T(8,128)S(1)}, f32[328,128]{1,0:T(8,128)S(1)}, u32[]{:S(2)}, u32[]{:S(2)}) collective-permute-start(f32[328,128]{1,0:T(8,128)S(1)} %get-tuple-element.40.own), channel_id=1, source_target_pairs={{0,64},{8,72},{16,80},{24,88},{32,96},{40,104},{48,112},{56,120},{... | collective-permute-start | bytes 503816 | tf_op jit(solution)/shard_map/ppermute | solution.py:540

commit v9 on v8

--- a/solution.py
+++ b/solution.py
@@ -317,7 +317,7 @@
     out[3 * FACE :] = both.swap
 
 
-def four_kernel(got, out, halves, lefts):
+def four_kernel(got, out, lefts):
     def chain(i, p, tile):
         return got[2 * i + p, tile * FACE : (tile + 1) * FACE]
 
@@ -332,8 +332,6 @@
         segs.append(seg)
     both = [join(segs[2 * i], segs[2 * i + 1]) for i in range(2)]
     join(*both).write(out)
-    for i in range(2):
-        both[i].write(halves.at[i])
 
 
 def start_place():
@@ -378,7 +376,7 @@
             ref[p, i] = place[p][i]
 
 
-def four_place_kernel(at, upper, one, one_got, lefts, got, pair_lefts, halves, out, swap_out):
+def four_place_kernel(at, upper, one, one_got, lefts, got, pair_lefts, out, swap_out):
     mine, other = Segment.of(one), Segment.of(one_got)
     up = upper[0][:1] > 0.5
     mine.left = [jnp.where(up, mine.left[p], lefts[p]) for p in range(2)]
@@ -395,7 +393,8 @@
     mine, other = pair_of(j), pair_of(j ^ 1)
     made = widen_place(made, upper[1], mine, other)
     x = jnp.abs(x - jnp.where(upper[1] > 0.5, other.swap, 0.0))
-    mine, other = Segment.of(halves.at[half]), Segment.of(halves.at[1 - half])
+    mine = join(pair_of(2 * half), pair_of(2 * half + 1))
+    other = join(pair_of(2 - 2 * half), pair_of(3 - 2 * half))
     write_place(out, widen_place(made, upper[2], mine, other))
     swap_out[...] = jnp.abs(x - jnp.where(upper[2] > 0.5, other.swap, 0.0))
 
@@ -545,12 +544,12 @@
     )
     groups = [[8 * g + j for j in range(8)] for g in range(layers // 8)]
     chains = lax.all_gather(chain, "stream", axis_index_groups=groups)
-    eight, halves, pair_lefts = call(
-        four_kernel, (f32(ROWS, LANES), f32(2, ROWS, LANES), f32(4, 2, FACE, LANES)), chains
+    eight, pair_lefts = call(
+        four_kernel, (f32(ROWS, LANES), f32(4, 2, FACE, LANES)), chains
     )
     here = (f32(2, 3, FACE, LANES), f32(8, LANES))
     got8 = across(eight, 8)
-    spot, turn = call(four_place_kernel, here, place, upper, own, got, lefts, chains, pair_lefts, halves, smem=(0,))
+    spot, turn = call(four_place_kernel, here, place, upper, own, got, lefts, chains, pair_lefts, smem=(0,))
     terms, eight = lax.optimization_barrier((terms, eight))
     zin, zout, base = call(rest_kernel, tuple(f32(2, DOF, LANES) for _ in range(3)), inv, low, rhs, west, east, terms)
     fixed, free = call(

time: 70.9 us -> 70.9 us (level)
  transfers between devices with their start and end apart: 5 -> 5, of which waited for: 3 -> 2; matrix products, arithmetic and copies ran while one was open for 0% -> 0% of each run, Pallas kernels for 10% -> 11%
where the time goes in v9:
time: 70.9 us; the launch traced here: 70.7 us
  blocking collectives  36.9 us (52%)
  starting transfers between devices  15.3 us (22%)
  Pallas kernels  13.2 us (19%)
  waiting for transfers between devices  5.16 us (7%)
    all_gather x1, blocking collectives, per_device(): sixteens = lax.all_gather(chain, 'stream', axis_index_groups=groups)  19.3 us
    all_gather x1, blocking collectives, per_device(): chains = lax.all_gather(chain, 'stream', axis_index_groups=groups)  17.5 us
    pallas_call x9, Pallas kernels, call(): pl.pallas_call(kernel, out_shape=out_shape, in_specs=specs, out_specs=tup...  13.2 us
    ppermute x1, starting transfers between devices, per_device(): lax.ppermute(guess, 'span', [(i, (i - 1 + 2 * (i & 1)) % wide) for i in r...  7.01 us
    ppermute x2, starting transfers between devices, across(): return lax.ppermute(x, 'stream', [(i, i ^ distance) for i in range(layers)])  5.12 us
    ppermute x1, waiting for transfers between devices, per_device(): lax.ppermute(ahead, 'stream', [(i + 8, i + 1) for i in range(0, layers -...  3.67 us
    ppermute x1, starting transfers between devices, per_device(): from_near = lax.ppermute(guess, 'span', [(i, i ^ 1) for i in range(wide)])  1.92 us
    ppermute x2, waiting for transfers between devices, across(): return lax.ppermute(x, 'stream', [(i, i ^ distance) for i in range(layers)])  1.49 us
  transfers between devices with their start and end apart: 5, of which 2 were waited for; matrix products, arithmetic and copies ran while one was open for 0% of the time, Pallas kernels for 11%

profile of v9, /device:TPU:1, one launch (start us, length us, event | category | flops | bytes accessed | tf_op | source)
XLA Modules:
  0.0 70.7 jit_solution(10846103219281142762)
XLA Ops:
  0.0 7.0 %collective-permute-start.1 = (f32[1,1,8,2,320]{4,3,2,1,0:T(2,128)}, f32[1,1,8,2,320]{4,3,2,1,0:T(2,128)S(1)}, u32[]{:S(2)}, u32[]{:S(2)}) collective-permute-start(f32[1,1,8,2,320]{4,3,2,1,0:T(2,128)} %guess_hbm.1), channel_id=1, source_target_pairs={{0,7},{1,2},{2,1},{3,4},{4,3},{5,6},{6,5},{7,0},{8,15},{9,10},{10,... | collective-permute-start | bytes 61448 | tf_op jit(solution)/shard_map/ppermute | solution.py:518
  7.0 1.9 %collective-permute-start = (f32[1,1,8,2,320]{4,3,2,1,0:T(2,128)}, f32[1,1,8,2,320]{4,3,2,1,0:T(2,128)S(1)}, u32[]{:S(2)}, u32[]{:S(2)}) collective-permute-start(f32[1,1,8,2,320]{4,3,2,1,0:T(2,128)} %guess_hbm.1), channel_id=1, source_target_pairs={{0,1},{1,0},{2,3},{3,2},{4,5},{5,4},{6,7},{7,6},{8,9},{9,8},{10,11... | collective-permute-start | bytes 61448 | tf_op jit(solution)/shard_map/ppermute | solution.py:519
  9.0 3.2 %shard_map.82 = (f32[2,8,80]{2,1,0:T(8,128)S(1)}, f32[8,128]{1,0:T(8,128)}, f32[7,8,128]{2,1,0:T(8,128)S(1)}, f32[1,1,2,320,320]{4,3,2,1,0:T(8,128)S(1)}, f32[1,...) custom-call(f32[1,1,8,2,320]{4,3,2,1,0:T(2,128)} %guess_hbm.1, ...), custom_call_target="tpu_custom_call" | custom-call | bytes 1048576 | tf_op jit(solution)/shard_map/pallas_call | solution.py:491
  12.2 1.3 %collective-permute-start.2 = (f32[2,8,80]{2,1,0:T(8,128)S(1)}, f32[2,8,80]{2,1,0:T(8,128)S(1)}, u32[]{:S(2)}, u32[]{:S(2)}) collective-permute-start(f32[2,8,80]{2,1,0:T(8,128)S(1)} %get-tuple-element.34), channel_id=1, source_target_pairs={{64,8},{128,72},{192,136},{256,200},{320,264},{384,328},{448,392},... | collective-permute-start | bytes 15368 | tf_op jit(solution)/shard_map/ppermute | solution.py:532
  13.5 3.7 %collective-permute-done.2.relayed = f32[2,8,80]{2,1,0:T(8,128)S(1)} collective-permute-done((f32[2,8,80]{2,1,0:T(8,128)S(1)}, f32[2,8,80]{2,1,0:T(8,128)S(1)}, u32[]{:S(2)}, u32[]{:S(2)}) %collective-permute-start.2) | collective-permute-done | bytes 5152 | tf_op jit(solution)/shard_map/ppermute | solution.py:532
  17.1 0.0 collective-permute-done.1.from_far
  17.1 0.0 collective-permute-done.from_near
  17.1 0.5 shard_map.83
  17.6 1.9 %collective-permute-start.3 = (f32[488,128]{1,0:T(8,128)S(1)}, f32[488,128]{1,0:T(8,128)S(1)}, u32[]{:S(2)}, u32[]{:S(2)}) collective-permute-start(f32[488,128]{1,0:T(8,128)S(1)} %get-tuple-element.36.own.one), channel_id=1, source_target_pairs={{0,8},{8,0},{16,24},{24,16},{32,40},{40,32},{48,56},{56,48},{64,72... | collective-permute-start | bytes 749576 | tf_op jit(solution)/shard_map/ppermute | solution.py:539
  19.5 1.5 %collective-permute-done.3.got.one_got = f32[488,128]{1,0:T(8,128)S(1)} collective-permute-done((f32[488,128]{1,0:T(8,128)S(1)}, f32[488,128]{1,0:T(8,128)S(1)}, u32[]{:S(2)}, u32[]{:S(2)}) %collective-permute-start.3) | collective-permute-done | bytes 249888 | tf_op jit(solution)/shard_map/ppermute | solution.py:539
  21.0 0.7 %shard_map.84 = (f32[248,128]{1,0:T(8,128)S(1)}, f32[2,80,128]{2,1,0:T(8,128)S(1)}) custom-call(f32[7,8,128]{2,1,0:T(8,128)S(1)} %get-tuple-element.32.upper, f32[488,128]{1,0:T(8,128)S(1)} %get-tuple-element.36.own.one, f32[488,128]{1,0:T(8,128)S(1)} %collective-permute-done.3.got.one_got, f32[2,8,80]{2,1,0:T(8,128)S(1)} %collective-permute-done.2.relayed), custom_call_target="tpu_custom_call" | custom-call | bytes 1048576 | tf_op jit(solution)/shard_map/pallas_call | solution.py:491
  21.8 17.5 %all-gather = f32[1984,128]{1,0:T(8,128)S(1)} all-gather(f32[248,128]{1,0:T(8,128)S(1)} %get-tuple-element.37), channel_id=2, replica_groups={{0,8,16,24,32,40,48,56},{64,72,80,88,96,104,112,120},{128,136,144,152,1..., dimensions={0}, use_global_device_ids=true | all-gather | bytes 1142784 | tf_op jit(solution)/shard_map/all_gather | solution.py:546
  39.3 1.6 %shard_map.85 = (f32[328,128]{1,0:T(8,128)S(1)}, f32[4,2,80,128]{3,2,1,0:T(8,128)S(1)}) custom-call(f32[8,248,128]{2,1,0:T(8,128)S(1)} %bitcast.5), custom_call_target="tpu_custom_call" | custom-call | bytes 1048576 | tf_op jit(solution)/shard_map/pallas_call | solution.py:491
  40.9 3.2 %collective-permute-start.4 = (f32[328,128]{1,0:T(8,128)S(1)}, f32[328,128]{1,0:T(8,128)S(1)}, u32[]{:S(2)}, u32[]{:S(2)}) collective-permute-start(f32[328,128]{1,0:T(8,128)S(1)} %get-tuple-element.39.own), channel_id=1, source_target_pairs={{0,64},{8,72},{16,80},{24,88},{32,96},{40,104},{48,112},{56,120},{... | collective-permute-start | bytes 503816 | tf_op jit(solution)/shard_map/ppermute | solution.py:539
  44.1 1.4 %shard_map.87 = (f32[2,320,128]{2,1,0:T(8,128)S(1)}, f32[2,320,128]{2,1,0:T(8,128)S(1)}, f32[2,320,128]{2,1,0:T(8,128)S(1)}) custom-call(f32[1,1,2,320,320]{4,3,2,1,0:T(8,128)S(1)} %get-tuple-element.44.inv, f32[1,1,2,80,80]{4,3,2,1,0:T(8,128)S(1)} %get-tuple-element.45.low, f32[1,1,8,2,320]{4,3,2,1,0:T(2,128)S(1)} %get-tuple-element.46.rhs, ...), custom_call_target="tpu_custom_call" | custom-call | bytes 1048576 | tf_op jit(solution)/shard_map/pallas_call | solution.py:491
  45.5 2.4 %shard_map.86 = (f32[2,3,80,128]{3,2,1,0:T(8,128)S(1)}, f32[8,128]{1,0:T(8,128)S(1)}) custom-call(s32[1]{0:T(128)} %bitcast.place.at, f32[7,8,128]{2,1,0:T(8,128)S(1)} %get-tuple-element.32.upper, f32[488,128]{1,0:T(8,128)S(1)} %get-tuple-element.36.own.one, f32[488,128]{1,0:T(8,128)S(1)} %collective-permute-done.3.got.one_got, ...), custom_call_target="tpu_custom_call" | custom-call | bytes 1048576 | tf_op jit(solution)/shard_map/pallas_call | solution.py:491
  47.9 0.6 shard_map.88
  48.5 0.0 collective-permute-done.4.got.got8
  48.5 0.6 shard_map.89
  49.1 19.3 %all-gather.1 = f32[1344,128]{1,0:T(8,128)S(1)} all-gather(f32[168,128]{1,0:T(8,128)S(1)} %shard_map.89), channel_id=3, replica_groups={{0,8,128,136,256,264,384,392},{16,24,144,152,272,280,400,408},{32,40,16..., dimensions={0}, use_global_device_ids=true | all-gather | bytes 774144 | tf_op jit(solution)/shard_map/all_gather | solution.py:565
  68.4 2.3 %shard_map.90 = f32[8,2,320]{2,1,0:T(2,128)} custom-call(f32[7,8,128]{2,1,0:T(8,128)S(1)} %get-tuple-element.32.upper, f32[8,168,128]{2,1,0:T(8,128)S(1)} %bitcast.7, f32[328,128]{1,0:T(8,128)S(1)} %get-tuple-element.39.own, f32[328,128]{1,0:T(8,128)S(1)} %collective-permute-done.4.got.got8, f32[8,128]{1,0:T(8,128)S(1)} %get-tuple-element.56.turn, ...), custom_call_target="tpu_custom_call" | custom-call | bytes 1048576 | tf_op jit(solution)/shard_map/pallas_call | solution.py:491
Async XLA Ops:
  0.0 17.1 %collective-permute-start.1 = (f32[1,1,8,2,320]{4,3,2,1,0:T(2,128)}, f32[1,1,8,2,320]{4,3,2,1,0:T(2,128)S(1)}, u32[]{:S(2)}, u32[]{:S(2)}) collective-permute-start(f32[1,1,8,2,320]{4,3,2,1,0:T(2,128)} %guess_hbm.1), channel_id=1, source_target_pairs={{0,7},{1,2},{2,1},{3,4},{4,3},{5,6},{6,5},{7,0},{8,15},{9,10},{10,... | collective-permute-start | bytes 61448 | tf_op jit(solution)/shard_map/ppermute | solution.py:518
  7.0 10.1 %collective-permute-start = (f32[1,1,8,2,320]{4,3,2,1,0:T(2,128)}, f32[1,1,8,2,320]{4,3,2,1,0:T(2,128)S(1)}, u32[]{:S(2)}, u32[]{:S(2)}) collective-permute-start(f32[1,1,8,2,320]{4,3,2,1,0:T(2,128)} %guess_hbm.1), channel_id=1, source_target_pairs={{0,1},{1,0},{2,3},{3,2},{4,5},{5,4},{6,7},{7,6},{8,9},{9,8},{10,11... | collective-permute-start | bytes 61448 | tf_op jit(solution)/shard_map/ppermute | solution.py:519
  12.2 5.0 %collective-permute-start.2 = (f32[2,8,80]{2,1,0:T(8,128)S(1)}, f32[2,8,80]{2,1,0:T(8,128)S(1)}, u32[]{:S(2)}, u32[]{:S(2)}) collective-permute-start(f32[2,8,80]{2,1,0:T(8,128)S(1)} %get-tuple-element.34), channel_id=1, source_target_pairs={{64,8},{128,72},{192,136},{256,200},{320,264},{384,328},{448,392},... | collective-permute-start | bytes 15368 | tf_op jit(solution)/shard_map/ppermute | solution.py:532
  17.6 3.4 %collective-permute-start.3 = (f32[488,128]{1,0:T(8,128)S(1)}, f32[488,128]{1,0:T(8,128)S(1)}, u32[]{:S(2)}, u32[]{:S(2)}) collective-permute-start(f32[488,128]{1,0:T(8,128)S(1)} %get-tuple-element.36.own.one), channel_id=1, source_target_pairs={{0,8},{8,0},{16,24},{24,16},{32,40},{40,32},{48,56},{56,48},{64,72... | collective-permute-start | bytes 749576 | tf_op jit(solution)/shard_map/ppermute | solution.py:539
  40.9 7.6 %collective-permute-start.4 = (f32[328,128]{1,0:T(8,128)S(1)}, f32[328,128]{1,0:T(8,128)S(1)}, u32[]{:S(2)}, u32[]{:S(2)}) collective-permute-start(f32[328,128]{1,0:T(8,128)S(1)} %get-tuple-element.39.own), channel_id=1, source_target_pairs={{0,64},{8,72},{16,80},{24,88},{32,96},{40,104},{48,112},{56,120},{... | collective-permute-start | bytes 503816 | tf_op jit(solution)/shard_map/ppermute | solution.py:539

commit v10 on v8

--- a/solution.py
+++ b/solution.py
@@ -314,7 +314,11 @@
         lefts[p] = first.left[p]
     for i, pair in enumerate((both.left, both.right, tails)):
         out[i * FACE : (i + 1) * FACE] = jnp.where(up, pair[1], pair[0]) + (behind_eight if i == 2 else 0.0)
-    out[3 * FACE :] = both.swap
+    out[2 * FACE : 2 * FACE + 8, LANES - 8 :] = both.swap[:, LANES - 8 :]
+
+
+def swap_in(rows):
+    return jnp.broadcast_to(rows[:, LANES - 1 :], rows.shape)
 
 
 def four_kernel(got, out, halves, lefts):
@@ -325,7 +329,7 @@
     last = [pltpu.roll(tails[0][1], LANES - 8 * (p + 1), 1) for p in range(2)]
     segs = []
     for i in range(4):
-        seg = Segment([chain(i, p, 0) for p in range(2)], [chain(i, p, 1) for p in range(2)], got[2 * i, 3 * FACE :])
+        seg = Segment([chain(i, p, 0) for p in range(2)], [chain(i, p, 1) for p in range(2)], swap_in(got[2 * i, 2 * FACE : 2 * FACE + 8]))
         seg = Segment(lagged_left(seg, tails[i], tails[i + 1] if i < 3 else last), seg.right, seg.swap)
         for p in range(2):
             lefts[i, p] = seg.left[p]
@@ -390,7 +394,7 @@
 
     def pair_of(i):
         right = [got[2 * i + p, FACE : 2 * FACE] for p in range(2)]
-        return Segment([pair_lefts[i, p] for p in range(2)], right, got[2 * i, 3 * FACE :])
+        return Segment([pair_lefts[i, p] for p in range(2)], right, swap_in(got[2 * i, 2 * FACE : 2 * FACE + 8]))
 
     mine, other = pair_of(j), pair_of(j ^ 1)
     made = widen_place(made, upper[1], mine, other)
@@ -541,7 +545,7 @@
 
     got = across(own, 1)
     chain, lefts = call(
-        first_pair_kernel, (f32(3 * FACE + 8, LANES), f32(2, FACE, LANES)), upper, own, got, relayed
+        first_pair_kernel, (f32(3 * FACE, LANES), f32(2, FACE, LANES)), upper, own, got, relayed
     )
     groups = [[8 * g + j for j in range(8)] for g in range(layers // 8)]
     chains = lax.all_gather(chain, "stream", axis_index_groups=groups)

time: 70.9 us -> 70.8 us (level)
  no operation moved by 1% of the time
where the time goes in v10:
time: 70.8 us; the launch traced here: 70.5 us
  blocking collectives  36.6 us (52%)
  starting transfers between devices  15.4 us (22%)
  Pallas kernels  12.7 us (18%)
  waiting for transfers between devices  5.72 us (8%)
    all_gather x1, blocking collectives, per_device(): sixteens = lax.all_gather(chain, 'stream', axis_index_groups=groups)  19.4 us
    all_gather x1, blocking collectives, per_device(): chains = lax.all_gather(chain, 'stream', axis_index_groups=groups)  17.2 us
    pallas_call x9, Pallas kernels, call(): pl.pallas_call(kernel, out_shape=out_shape, in_specs=specs, out_specs=tup...  12.7 us
    ppermute x1, starting transfers between devices, per_device(): lax.ppermute(guess, 'span', [(i, (i - 1 + 2 * (i & 1)) % wide) for i in r...  7.01 us
    ppermute x2, starting transfers between devices, across(): return lax.ppermute(x, 'stream', [(i, i ^ distance) for i in range(layers)])  5.13 us
    ppermute x1, waiting for transfers between devices, per_device(): lax.ppermute(ahead, 'stream', [(i + 8, i + 1) for i in range(0, layers -...  3.67 us
    ppermute x2, waiting for transfers between devices, across(): return lax.ppermute(x, 'stream', [(i, i ^ distance) for i in range(layers)])  2.04 us
    ppermute x1, starting transfers between devices, per_device(): from_near = lax.ppermute(guess, 'span', [(i, i ^ 1) for i in range(wide)])  1.92 us
  transfers between devices with their start and end apart: 5, of which 3 were waited for; matrix products, arithmetic and copies ran while one was open for 0% of the time, Pallas kernels for 10%

profile of v10, /device:TPU:1, one launch (start us, length us, event | category | flops | bytes accessed | tf_op | source)
XLA Modules:
  0.0 70.5 jit_solution(14477325066076962738)
XLA Ops:
  0.0 7.0 %collective-permute-start.1 = (f32[1,1,8,2,320]{4,3,2,1,0:T(2,128)}, f32[1,1,8,2,320]{4,3,2,1,0:T(2,128)S(1)}, u32[]{:S(2)}, u32[]{:S(2)}) collective-permute-start(f32[1,1,8,2,320]{4,3,2,1,0:T(2,128)} %guess_hbm.1), channel_id=1, source_target_pairs={{0,7},{1,2},{2,1},{3,4},{4,3},{5,6},{6,5},{7,0},{8,15},{9,10},{10,... | collective-permute-start | bytes 61448 | tf_op jit(solution)/shard_map/ppermute | solution.py:523
  7.0 1.9 %collective-permute-start = (f32[1,1,8,2,320]{4,3,2,1,0:T(2,128)}, f32[1,1,8,2,320]{4,3,2,1,0:T(2,128)S(1)}, u32[]{:S(2)}, u32[]{:S(2)}) collective-permute-start(f32[1,1,8,2,320]{4,3,2,1,0:T(2,128)} %guess_hbm.1), channel_id=1, source_target_pairs={{0,1},{1,0},{2,3},{3,2},{4,5},{5,4},{6,7},{7,6},{8,9},{9,8},{10,11... | collective-permute-start | bytes 61448 | tf_op jit(solution)/shard_map/ppermute | solution.py:524
  9.0 3.2 %shard_map.82 = (f32[2,8,80]{2,1,0:T(8,128)S(1)}, f32[8,128]{1,0:T(8,128)}, f32[7,8,128]{2,1,0:T(8,128)S(1)}, f32[1,1,2,320,320]{4,3,2,1,0:T(8,128)S(1)}, f32[1,...) custom-call(f32[1,1,8,2,320]{4,3,2,1,0:T(2,128)} %guess_hbm.1, ...), custom_call_target="tpu_custom_call" | custom-call | bytes 1048576 | tf_op jit(solution)/shard_map/pallas_call | solution.py:496
  12.2 1.3 %collective-permute-start.2 = (f32[2,8,80]{2,1,0:T(8,128)S(1)}, f32[2,8,80]{2,1,0:T(8,128)S(1)}, u32[]{:S(2)}, u32[]{:S(2)}) collective-permute-start(f32[2,8,80]{2,1,0:T(8,128)S(1)} %get-tuple-element.35), channel_id=1, source_target_pairs={{64,8},{128,72},{192,136},{256,200},{320,264},{384,328},{448,392},... | collective-permute-start | bytes 15368 | tf_op jit(solution)/shard_map/ppermute | solution.py:537
  13.5 3.7 %collective-permute-done.2.relayed = f32[2,8,80]{2,1,0:T(8,128)S(1)} collective-permute-done((f32[2,8,80]{2,1,0:T(8,128)S(1)}, f32[2,8,80]{2,1,0:T(8,128)S(1)}, u32[]{:S(2)}, u32[]{:S(2)}) %collective-permute-start.2) | collective-permute-done | bytes 5152 | tf_op jit(solution)/shard_map/ppermute | solution.py:537
  17.1 0.0 collective-permute-done.1.from_far
  17.1 0.0 collective-permute-done.from_near
  17.1 0.5 shard_map.83
  17.6 1.9 %collective-permute-start.3 = (f32[488,128]{1,0:T(8,128)S(1)}, f32[488,128]{1,0:T(8,128)S(1)}, u32[]{:S(2)}, u32[]{:S(2)}) collective-permute-start(f32[488,128]{1,0:T(8,128)S(1)} %get-tuple-element.37.own.one), channel_id=1, source_target_pairs={{0,8},{8,0},{16,24},{24,16},{32,40},{40,32},{48,56},{56,48},{64,72... | collective-permute-start | bytes 749576 | tf_op jit(solution)/shard_map/ppermute | solution.py:544
  19.5 1.5 %collective-permute-done.3.got.one_got = f32[488,128]{1,0:T(8,128)S(1)} collective-permute-done((f32[488,128]{1,0:T(8,128)S(1)}, f32[488,128]{1,0:T(8,128)S(1)}, u32[]{:S(2)}, u32[]{:S(2)}) %collective-permute-start.3) | collective-permute-done | bytes 249888 | tf_op jit(solution)/shard_map/ppermute | solution.py:544
  21.0 0.7 %shard_map.84 = (f32[240,128]{1,0:T(8,128)S(1)}, f32[2,80,128]{2,1,0:T(8,128)S(1)}) custom-call(f32[7,8,128]{2,1,0:T(8,128)S(1)} %get-tuple-element.33.upper, f32[488,128]{1,0:T(8,128)S(1)} %get-tuple-element.37.own.one, f32[488,128]{1,0:T(8,128)S(1)} %collective-permute-done.3.got.one_got, f32[2,8,80]{2,1,0:T(8,128)S(1)} %collective-permute-done.2.relayed), custom_call_target="tpu_custom_call" | custom-call | bytes 1048576 | tf_op jit(solution)/shard_map/pallas_call | solution.py:496
  21.8 17.2 %all-gather = f32[1920,128]{1,0:T(8,128)S(1)} all-gather(f32[240,128]{1,0:T(8,128)S(1)} %get-tuple-element.38), channel_id=2, replica_groups={{0,8,16,24,32,40,48,56},{64,72,80,88,96,104,112,120},{128,136,144,152,1..., dimensions={0}, use_global_device_ids=true | all-gather | bytes 1105920 | tf_op jit(solution)/shard_map/all_gather | solution.py:551
  39.0 1.6 %shard_map.85 = (f32[328,128]{1,0:T(8,128)S(1)}, f32[2,328,128]{2,1,0:T(8,128)S(1)}, f32[4,2,80,128]{3,2,1,0:T(8,128)S(1)}) custom-call(f32[8,240,128]{2,1,0:T(8,128)S(1)} %bitcast.5), custom_call_target="tpu_custom_call" | custom-call | bytes 1048576 | tf_op jit(solution)/shard_map/pallas_call | solution.py:496
  40.6 3.2 %collective-permute-start.4 = (f32[328,128]{1,0:T(8,128)S(1)}, f32[328,128]{1,0:T(8,128)S(1)}, u32[]{:S(2)}, u32[]{:S(2)}) collective-permute-start(f32[328,128]{1,0:T(8,128)S(1)} %get-tuple-element.40.own), channel_id=1, source_target_pairs={{0,64},{8,72},{16,80},{24,88},{32,96},{40,104},{48,112},{56,120},{... | collective-permute-start | bytes 503816 | tf_op jit(solution)/shard_map/ppermute | solution.py:544
  43.8 1.4 %shard_map.87 = (f32[2,320,128]{2,1,0:T(8,128)S(1)}, f32[2,320,128]{2,1,0:T(8,128)S(1)}, f32[2,320,128]{2,1,0:T(8,128)S(1)}) custom-call(f32[1,1,2,320,320]{4,3,2,1,0:T(8,128)S(1)} %get-tuple-element.46.inv, f32[1,1,2,80,80]{4,3,2,1,0:T(8,128)S(1)} %get-tuple-element.47.low, f32[1,1,8,2,320]{4,3,2,1,0:T(2,128)S(1)} %get-tuple-element.48.rhs, ...), custom_call_target="tpu_custom_call" | custom-call | bytes 1048576 | tf_op jit(solution)/shard_map/pallas_call | solution.py:496
  45.2 1.9 %shard_map.86 = (f32[2,3,80,128]{3,2,1,0:T(8,128)S(1)}, f32[8,128]{1,0:T(8,128)S(1)}) custom-call(s32[1]{0:T(128)} %bitcast.place.at, f32[7,8,128]{2,1,0:T(8,128)S(1)} %get-tuple-element.33.upper, f32[488,128]{1,0:T(8,128)S(1)} %get-tuple-element.37.own.one, f32[488,128]{1,0:T(8,128)S(1)} %collective-permute-done.3.got.one_got, ...), custom_call_target="tpu_custom_call" | custom-call | bytes 1048576 | tf_op jit(solution)/shard_map/pallas_call | solution.py:496
  47.1 0.6 shard_map.88
  47.7 0.6 collective-permute-done.4.got.got8
  48.2 0.6 shard_map.89
  48.8 19.4 %all-gather.1 = f32[1344,128]{1,0:T(8,128)S(1)} all-gather(f32[168,128]{1,0:T(8,128)S(1)} %shard_map.89), channel_id=3, replica_groups={{0,8,128,136,256,264,384,392},{16,24,144,152,272,280,400,408},{32,40,16..., dimensions={0}, use_global_device_ids=true | all-gather | bytes 774144 | tf_op jit(solution)/shard_map/all_gather | solution.py:570
  68.3 2.3 %shard_map.90 = f32[8,2,320]{2,1,0:T(2,128)} custom-call(f32[7,8,128]{2,1,0:T(8,128)S(1)} %get-tuple-element.33.upper, f32[8,168,128]{2,1,0:T(8,128)S(1)} %bitcast.7, f32[328,128]{1,0:T(8,128)S(1)} %get-tuple-element.40.own, f32[328,128]{1,0:T(8,128)S(1)} %collective-permute-done.4.got.got8, f32[8,128]{1,0:T(8,128)S(1)} %get-tuple-element.58.turn, ...), custom_call_target="tpu_custom_call" | custom-call | bytes 1048576 | tf_op jit(solution)/shard_map/pallas_call | solution.py:496
Async XLA Ops:
  0.0 17.1 %collective-permute-start.1 = (f32[1,1,8,2,320]{4,3,2,1,0:T(2,128)}, f32[1,1,8,2,320]{4,3,2,1,0:T(2,128)S(1)}, u32[]{:S(2)}, u32[]{:S(2)}) collective-permute-start(f32[1,1,8,2,320]{4,3,2,1,0:T(2,128)} %guess_hbm.1), channel_id=1, source_target_pairs={{0,7},{1,2},{2,1},{3,4},{4,3},{5,6},{6,5},{7,0},{8,15},{9,10},{10,... | collective-permute-start | bytes 61448 | tf_op jit(solution)/shard_map/ppermute | solution.py:523
  7.0 10.1 %collective-permute-start = (f32[1,1,8,2,320]{4,3,2,1,0:T(2,128)}, f32[1,1,8,2,320]{4,3,2,1,0:T(2,128)S(1)}, u32[]{:S(2)}, u32[]{:S(2)}) collective-permute-start(f32[1,1,8,2,320]{4,3,2,1,0:T(2,128)} %guess_hbm.1), channel_id=1, source_target_pairs={{0,1},{1,0},{2,3},{3,2},{4,5},{5,4},{6,7},{7,6},{8,9},{9,8},{10,11... | collective-permute-start | bytes 61448 | tf_op jit(solution)/shard_map/ppermute | solution.py:524
  12.2 5.0 %collective-permute-start.2 = (f32[2,8,80]{2,1,0:T(8,128)S(1)}, f32[2,8,80]{2,1,0:T(8,128)S(1)}, u32[]{:S(2)}, u32[]{:S(2)}) collective-permute-start(f32[2,8,80]{2,1,0:T(8,128)S(1)} %get-tuple-element.35), channel_id=1, source_target_pairs={{64,8},{128,72},{192,136},{256,200},{320,264},{384,328},{448,392},... | collective-permute-start | bytes 15368 | tf_op jit(solution)/shard_map/ppermute | solution.py:537
  17.6 3.4 %collective-permute-start.3 = (f32[488,128]{1,0:T(8,128)S(1)}, f32[488,128]{1,0:T(8,128)S(1)}, u32[]{:S(2)}, u32[]{:S(2)}) collective-permute-start(f32[488,128]{1,0:T(8,128)S(1)} %get-tuple-element.37.own.one), channel_id=1, source_target_pairs={{0,8},{8,0},{16,24},{24,16},{32,40},{40,32},{48,56},{56,48},{64,72... | collective-permute-start | bytes 749576 | tf_op jit(solution)/shard_map/ppermute | solution.py:544
  40.6 7.6 %collective-permute-start.4 = (f32[328,128]{1,0:T(8,128)S(1)}, f32[328,128]{1,0:T(8,128)S(1)}, u32[]{:S(2)}, u32[]{:S(2)}) collective-permute-start(f32[328,128]{1,0:T(8,128)S(1)} %get-tuple-element.40.own), channel_id=1, source_target_pairs={{0,64},{8,72},{16,80},{24,88},{32,96},{40,104},{48,112},{56,120},{... | collective-permute-start | bytes 503816 | tf_op jit(solution)/shard_map/ppermute | solution.py:544
